TPU v7x, 32 devices: a whole 2x2x4 slice. The times are simulated.
32 devices in a mesh: sub: 8 (over z, x), blk: 4 (over y, core).
Axes of the slice: x: 2, y: 2, z: 4, core: 2. Of those that a mesh axis runs over, the one named last changes fastest.
Arguments:
- right_side: float32 [32, 1024, 512], P('sub', 'blk'), may hold values from -8 to 8
- trans_x: float32 [32, 1024, 512], P('sub', 'blk'), may hold values from 0.01 to 10
- trans_y: float32 [32, 1024, 512], P('sub', 'blk'), may hold values from 0.01 to 10
- trans_z: float32 [32, 1024, 512], P('sub', 'blk'), may hold values from 0.01 to 10
- storage: float32 [32, 1024, 512], P('sub', 'blk'), may hold values from 0.05 to 1
- pair_perm: int32 [8, 4, 1024], P('sub', 'blk'), may hold values from 0 to 1023, each once within a row
- pair_type: int32 [8, 4, 1024], P('sub', 'blk'), may hold values from 0 to 3
- pair_count: int32 [8, 4], P('sub', 'blk'), may hold values from 256 to 1024
- proj: float32 [4, 128, 128], replicated, may hold values from -1 to 2, as said below
Outputs:
- solution_field: float32 [32, 1024, 512], P('sub', 'blk')
- residual: float32 [32, 1024, 512], P('sub', 'blk')
Inputs may be any that keep to these rules, and one draw needn't show every extreme that they name: `pair_perm`: each subdomain's list is a permutation of its face blocks. `proj`: projection matrices of order one.
All inputs are finite; a program needn't handle non-finite values.
Results may differ from a plain program's by a relative error of at most 0.00013.
Values sent between devices are 32-bit elements; how exact they have to be, the bound alone decides.
No kernel may reach another device: no remote copies, remote signals or barrier semaphores. Data moves between devices by JAX's collectives and lax.ppermute only.
A program may use at most 128 MiB of HBM per device.

v0:
```python
import jax
import jax.numpy as jnp
from jax import lax
from jax.sharding import PartitionSpec as P

ITERS = 2


penalty = 4.0


def shifted(array, axis, by):
    size = lax.axis_size(axis)
    pairs = [(i, i + by) for i in range(size) if 0 <= i + by < size]
    return lax.ppermute(array, axis, pairs)


def with_halo(block, sides, width):
    for axis, dim in sides:
        count = lax.axis_size(axis)
        forward = [(i, i + 1) for i in range(count - 1)]
        backward = [(target, source) for source, target in forward]
        low = lax.ppermute(
            lax.slice_in_dim(block, block.shape[dim] - width, None, axis=dim), axis, forward
        )
        high = lax.ppermute(lax.slice_in_dim(block, 0, width, axis=dim), axis, backward)
        block = jnp.concatenate([low, block, high], axis=dim)
    return block


def mortar_jump(last_face, gathered, selects, live, proj):
    projected = jnp.zeros_like(last_face)
    for kind in range(len(selects)):
        projected = projected + selects[kind] * jnp.einsum(
            "kc,ac->ka", gathered, proj[kind], precision=lax.Precision.HIGHEST
        )
    return live * (last_face - projected)


def mortar_back(jump, selects, proj):
    back = jnp.zeros_like(jump)
    for kind in range(len(selects)):
        back = back + selects[kind] * jnp.einsum(
            "ka,ac->kc", jump, proj[kind], precision=lax.Precision.HIGHEST
        )
    return -penalty * back


def body(right_side, trans_x, trans_y, trans_z, storage, pair_perm, pair_type, pair_count, proj):
    cells_x, cells_y, cells_z = right_side.shape
    blocks = pair_perm.shape[2]
    width = proj.shape[1]
    kinds_total = proj.shape[0]
    total_y = cells_y * lax.axis_size("blk")
    x_index = jnp.arange(cells_x, dtype=jnp.int32)[:, None, None]
    y_index = lax.axis_index("blk") * cells_y + jnp.arange(cells_y, dtype=jnp.int32)[None, :, None]
    z_index = jnp.arange(cells_z, dtype=jnp.int32)[None, None, :]
    coeff_x = trans_x * (x_index != cells_x - 1).astype(jnp.float32)
    coeff_y = trans_y * (y_index != total_y - 1).astype(jnp.float32)
    coeff_z = trans_z * (z_index != cells_z - 1).astype(jnp.float32)
    below = shifted(coeff_y[:, cells_y - 1 :, :], "blk", 1)
    prev_y = jnp.concatenate([below, coeff_y[:, : cells_y - 1]], 1)
    prev_x = jnp.concatenate([jnp.zeros_like(coeff_x[:1]), coeff_x[: cells_x - 1]], 0)
    prev_z = jnp.concatenate([jnp.zeros_like(coeff_z[:, :, :1]), coeff_z[:, :, : cells_z - 1]], 2)
    partner = pair_perm[0, 0]
    kinds = pair_type[0, 0]
    block_ids = jnp.arange(blocks, dtype=jnp.int32)
    live = (block_ids < pair_count[0, 0]).astype(jnp.float32)[:, None]
    selects = [(kinds == kind).astype(jnp.float32)[:, None] for kind in range(kinds_total)]

    def squares(values):
        return lax.psum(jnp.sum(values * values), ("sub", "blk"))

    solution_field = jnp.zeros_like(right_side)
    residual = right_side
    direction = right_side
    norm_now = squares(residual)
    for step in range(ITERS):
        padded = with_halo(direction, (("blk", 1),), 1)
        next_y = padded[:, 2:]
        before_y = padded[:, :-2]
        next_x = jnp.concatenate([direction[1:], jnp.zeros_like(direction[:1])], 0)
        before_x = jnp.concatenate([jnp.zeros_like(direction[:1]), direction[:-1]], 0)
        next_z = jnp.concatenate([direction[:, :, 1:], jnp.zeros_like(direction[:, :, :1])], 2)
        before_z = jnp.concatenate([jnp.zeros_like(direction[:, :, :1]), direction[:, :, :-1]], 2)
        result = storage * direction
        result = result + coeff_x * (direction - next_x) + prev_x * (direction - before_x)
        result = result + coeff_y * (direction - next_y) + prev_y * (direction - before_y)
        result = result + coeff_z * (direction - next_z) + prev_z * (direction - before_z)
        last_face = direction[cells_x - 1].reshape(blocks, width)
        first_face = direction[0].reshape(blocks, width)
        right_face = shifted(first_face, "sub", -1)
        jump = mortar_jump(last_face, jnp.take(right_face, partner, axis=0), selects, live, proj)
        back = mortar_back(jump, selects, proj)
        ordered = jnp.zeros_like(back).at[partner].set(back)
        received = shifted(ordered, "sub", 1)
        result = result.at[cells_x - 1].add((penalty * jump).reshape(cells_y, cells_z))
        result = result.at[0].add(received.reshape(cells_y, cells_z))
        alpha = norm_now / lax.psum(jnp.sum(direction * result), ("sub", "blk"))
        solution_field = solution_field + alpha * direction
        residual = residual - alpha * result
        norm_next = squares(residual)
        direction = residual + norm_next / norm_now * direction
        norm_now = norm_next
    return (solution_field, residual)


def solution(mesh):
    in_specs = (
        P("sub", "blk", None),
        P("sub", "blk", None),
        P("sub", "blk", None),
        P("sub", "blk", None),
        P("sub", "blk", None),
        P("sub", "blk", None),
        P("sub", "blk", None),
        P("sub", "blk"),
        P(),
    )
    out_specs = (P("sub", "blk", None), P("sub", "blk", None))
    return jax.shard_map(body, mesh=mesh, in_specs=in_specs, out_specs=out_specs, check_vma=False)
```

profile of v0, /device:TPU:0, one launch (start us, length us, event | category | flops | bytes accessed | tf_op | source)
XLA Modules:
  0.0 259.2 jit_solution(1644019896084067171)
XLA Ops:
  0.6 0.9 fusion.118
  1.5 2.4 collective-permute-start.2
  3.9 1.3 collective-permute-start
  5.2 1.9 broadcast_multiply_fusion.1
  7.2 1.3 copy-done.3
  8.5 5.2 %collective-permute-start.1 = (f32[4,1,512]{2,1,0:T(1,128)S(1)}, f32[4,1,512]{2,1,0:T(1,128)S(1)}, u32[]{:S(2)}, u32[]{:S(2)}) collective-permute-start(f32[4,1,512]{2,1,0:T(1,128)S(1)} %slice.225), channel_id=1, source_target_pairs={{0,1},{1,2},{2,3},{4,5},{5,6},{6,7},{8,9},{9,10},{10,11},{12,13},{... | collective-permute-start | bytes 24584 | tf_op jit(solution)/shard_map/ppermute | solution.py:15
  13.8 0.9 reshape_squeeze.13
  14.6 1.3 collective-permute-start.3
  16.0 2.2 fusion.116
  18.2 1.1 copy-done.6
  19.3 2.0 broadcast_multiply_fusion
  21.3 1.3 copy-done.2
  22.6 1.3 slice.224
  23.9 0.9 reshape_squeeze.12
  25.5 2.8 %fusion.117 = (f32[4,256,511]{2,1,0:T(8,128)}, f32[4,256,511]{2,1,0:T(8,128)}) fusion(f32[4,256,512]{2,1,0:T(8,128)S(1)} %copy-done), kind=kLoop, calls=%fused_computation.172 | loop fusion | bytes 8372224 | tf_op jit(solution)/shard_map/slice | solution.py:84
  28.3 2.5 collective-permute-done.3
  30.8 2.8 %gather_fusion = f32[1024,128]{1,0:T(8,128)S(1)} fusion(f32[1024,128]{1,0:T(8,128)S(1)} %collective-permute-done.3, s32[1024]{0:T(1024)S(1)} %fusion.101), kind=kCustom, calls=%fused_computation.clone | custom fusion | bytes 1052672 | tf_op jit(solution)/shard_map/jit(_take)/gather | solution.py:93
  33.6 0.6 convolution_multiply_fusion.12
  34.2 0.6 convolution_multiply_fusion.13
  34.9 0.6 convolution_multiply_fusion.14
  35.5 2.1 broadcast_multiply_fusion.4
  37.6 0.6 convolution_multiply_fusion.11
  38.2 0.6 fusion.28
  38.8 0.6 fusion.27
  39.3 0.6 fusion.26
  39.9 3.9 %scatter_custom_fusion = f32[1024,128]{1,0:T(8,128)} fusion(s32[1024]{0:T(1024)S(1)} %bitcast.82, f32[1024,128]{1,0:T(8,128)S(1)} %fusion.26, f32[]{:T(128)} %constant.121.clone.1), kind=kCustom, calls=%fused_computation.100 | custom fusion | bytes 524292 | tf_op jit(solution)/shard_map/scatter | solution.py:95
  43.8 5.1 %collective-permute-start.4 = (f32[1024,128]{1,0:T(8,128)}, f32[1024,128]{1,0:T(8,128)}, u32[]{:S(2)}, u32[]{:S(2)}) collective-permute-start(f32[1024,128]{1,0:T(8,128)} %scatter_custom_fusion), channel_id=1, source_target_pairs={{0,4},{4,8},{8,12},{12,16},{16,20},{20,24},{24,28},{1,5},{5,9},{9,... | collective-permute-start | bytes 1572872 | tf_op jit(solution)/shard_map/ppermute | solution.py:15
  48.9 10.3 %fusion.4 = f32[4,256,512]{2,1,0:T(8,128)} fusion(f32[3,256,512]{2,1,0:T(8,128)} %slice.224, f32[4,256,512]{2,1,0:T(8,128)S(1)} %copy-done, f32[4,1,512]{2,1,0:T(1,128)S(1)} %collective-permute-done.2, f32[4,1,512]{2,1,0:T(1,128)S(1)} %collective-permute-done, f32[4,256,511]{2,1,0:T(8,128)} %get-tuple-element.70, f32[4,256,512]{2,1,0:T(8,128)} %get-tuple-element.81, ...), kind=kLoop, calls=%fused_computation.10 | loop fusion | flops 12058624 | bytes 25695232 | tf_op jit(solution)/shard_map/add | solution.py:89
  59.2 0.1 reshape.229
  59.3 1.9 fusion.39
  61.2 1.1 reshape.230
  62.3 2.0 fusion.38
  64.3 2.7 %multiply_reduce_fusion.2 = (f32[]{:T(128)}, f32[]{:T(128)}) fusion(f32[4,256,512]{2,1,0:T(8,128)S(1)} %copy-done, f32[4,256,512]{2,1,0:T(8,128)} %fusion.38), kind=kLoop, calls=%fused_computation.35 | loop fusion | flops 2097150 | bytes 4194312 | tf_op jit(solution)/shard_map/reduce_sum | solution.py:99
  67.0 40.4 %all-reduce.10 = (f32[]{:T(128)}, f32[]{:T(128)}) all-reduce(f32[]{:T(128)} %get-tuple-element.52, f32[]{:T(128)} %get-tuple-element.51), channel_id=1, replica_groups=mesh['sub'=8,'blk'=4] {'sub','blk'}, use_global_device_ids=true, to_apply=%region_1.0 | all-reduce | flops 2 | bytes 16 | tf_op jit(solution)/shard_map/psum | solution.py:72
  108.8 2.7 %multiply_reduce_fusion.1 = f32[]{:T(128)} fusion(f32[4,256,512]{2,1,0:T(8,128)S(1)} %copy-done, f32[4,256,512]{2,1,0:T(8,128)} %fusion.38, f32[]{:T(128)S(6)} %div.9), kind=kLoop, calls=%fused_computation.33 | loop fusion | flops 2097151 | bytes 4194312 | tf_op jit(solution)/shard_map/reduce_sum | solution.py:72
  111.6 40.1 %psum.30 = f32[]{:T(128)} all-reduce(f32[]{:T(128)} %multiply_reduce_fusion.1), channel_id=1, replica_groups=mesh['sub'=8,'blk'=4] {'sub','blk'}, use_global_device_ids=true, to_apply=%region_6.8 | all-reduce | flops 1 | bytes 8 | tf_op jit(solution)/shard_map/psum | solution.py:72
  153.1 2.1 multiply_add_fusion.1
  155.2 2.3 fusion.112
  157.6 0.9 reshape_squeeze.15
  158.5 1.3 collective-permute-start.7
  159.7 0.9 fusion.114
  160.6 1.3 collective-permute-start.6
  161.9 1.3 collective-permute-start.5
  163.2 0.8 reshape_squeeze.14
  164.1 4.9 %fusion.113 = (f32[4,256,511]{2,1,0:T(8,128)}, f32[4,256,511]{2,1,0:T(8,128)}) fusion(f32[4,256,512]{2,1,0:T(8,128)} %copy-done.1), kind=kLoop, calls=%fused_computation.168 | loop fusion | bytes 8372224 | tf_op jit(solution)/shard_map/slice | solution.py:84
  169.0 5.6 %collective-permute-done.7 = f32[1024,128]{1,0:T(8,128)S(1)} collective-permute-done((f32[1024,128]{1,0:T(8,128)}, f32[1024,128]{1,0:T(8,128)S(1)}, u32[]{:S(2)}, u32[]{:S(2)}) %collective-permute-start.7) | collective-permute-done | bytes 524320 | tf_op jit(solution)/shard_map/ppermute | solution.py:15
  174.5 2.8 %gather_fusion.1 = f32[1024,128]{1,0:T(8,128)S(1)} fusion(f32[1024,128]{1,0:T(8,128)S(1)} %collective-permute-done.7, s32[1024]{0:T(1024)S(1)} %fusion.101), kind=kCustom, calls=%fused_computation.1.clone | custom fusion | bytes 1052672 | tf_op jit(solution)/shard_map/jit(_take)/gather | solution.py:93
  177.4 0.6 convolution_multiply_fusion.4
  178.0 0.6 convolution_multiply_fusion.5
  178.6 0.6 convolution_multiply_fusion.6
  179.3 2.1 broadcast_multiply_fusion.3
  181.3 0.6 convolution_multiply_fusion.3
  181.9 0.6 fusion.21
  182.5 0.6 fusion.20
  183.1 0.6 fusion.19
  183.7 3.9 %scatter_custom_fusion.1 = f32[1024,128]{1,0:T(8,128)} fusion(s32[1024]{0:T(1024)S(1)} %bitcast.83, f32[1024,128]{1,0:T(8,128)S(1)} %fusion.19, f32[]{:T(128)} %constant.121.clone.1), kind=kCustom, calls=%fused_computation.98 | custom fusion | bytes 524292 | tf_op jit(solution)/shard_map/scatter | solution.py:95
  187.6 5.3 %collective-permute-start.8 = (f32[1024,128]{1,0:T(8,128)}, f32[1024,128]{1,0:T(8,128)}, u32[]{:S(2)}, u32[]{:S(2)}) collective-permute-start(f32[1024,128]{1,0:T(8,128)} %scatter_custom_fusion.1), channel_id=1, source_target_pairs={{0,4},{4,8},{8,12},{12,16},{16,20},{20,24},{24,28},{1,5},{5,9},{9,... | collective-permute-start | bytes 1572872 | tf_op jit(solution)/shard_map/ppermute | solution.py:15
  192.9 12.2 %fusion.9 = f32[4,256,512]{2,1,0:T(8,128)} fusion(f32[3,256,512]{2,1,0:T(8,128)} %slice.224, f32[4,256,512]{2,1,0:T(8,128)} %copy-done.1, f32[4,1,512]{2,1,0:T(1,128)S(1)} %collective-permute-done.6, f32[4,1,512]{2,1,0:T(1,128)S(1)} %collective-permute-done.5, f32[4,256,511]{2,1,0:T(8,128)} %get-tuple-element.62, f32[4,256,512]{2,1,0:T(8,128)} %get-tuple-element.81, ...), kind=kLoop, calls=%fused_computation.15 | loop fusion | flops 12058624 | bytes 25695232 | tf_op jit(solution)/shard_map/add | solution.py:89
  205.2 1.9 fusion.37
  207.1 1.1 reshape.232
  208.3 1.9 fusion.36
  210.2 3.4 %multiply_reduce_fusion = f32[]{:T(128)} fusion(f32[4,256,512]{2,1,0:T(8,128)} %copy-done.1, f32[4,256,512]{2,1,0:T(8,128)} %fusion.36), kind=kLoop, calls=%fused_computation.31 | loop fusion | flops 1048575 | bytes 4194308 | tf_op jit(solution)/shard_map/reduce_sum | solution.py:99
  213.6 38.5 %psum.31 = f32[]{:T(128)} all-reduce(f32[]{:T(128)} %multiply_reduce_fusion), channel_id=1, replica_groups=mesh['sub'=8,'blk'=4] {'sub','blk'}, use_global_device_ids=true, to_apply=%region_9.11 | all-reduce | flops 1 | bytes 8 | tf_op jit(solution)/shard_map/psum | solution.py:99
  253.2 6.0 %multiply_subtract_fusion = (f32[4,256,512]{2,1,0:T(8,128)}, f32[4,256,512]{2,1,0:T(8,128)}) fusion(f32[4,256,512]{2,1,0:T(8,128)} %fusion.36, f32[]{:T(128)S(6)} %div.11, f32[4,256,512]{2,1,0:T(8,128)S(1)} %copy-done, f32[4,256,512]{2,1,0:T(8,128)} %fusion.38, f32[]{:T(128)S(6)} %div.9, f32[4,256,512]{2,1,0:T(8,128)} %copy-done.1), kind=kLoop, calls=%fused_computation.29 | loop fusion | flops 3670016 | bytes 12582920 | tf_op jit(solution)/shard_map/sub | solution.py:101
  (41 shorter events, 0.4 us)
Async XLA Ops:
  1.5 47.4 %collective-permute-start.2 = (f32[4,1,512]{2,1,0:T(1,128)S(1)}, f32[4,1,512]{2,1,0:T(1,128)S(1)}, u32[]{:S(2)}, u32[]{:S(2)}) collective-permute-start(f32[4,1,512]{2,1,0:T(1,128)S(1)} %get-tuple-element.72), channel_id=1, source_target_pairs={{0,1},{1,2},{2,3},{4,5},{5,6},{6,7},{8,9},{9,10},{10,11},{12,13},{... | collective-permute-start | bytes 24584 | tf_op jit(solution)/shard_map/ppermute | solution.py:23
  3.9 45.0 %collective-permute-start = (f32[4,1,512]{2,1,0:T(1,128)S(1)}, f32[4,1,512]{2,1,0:T(1,128)S(1)}, u32[]{:S(2)}, u32[]{:S(2)}) collective-permute-start(f32[4,1,512]{2,1,0:T(1,128)S(1)} %get-tuple-element.71), channel_id=1, source_target_pairs={{1,0},{2,1},{3,2},{5,4},{6,5},{7,6},{9,8},{10,9},{11,10},{13,12},{... | collective-permute-start | bytes 24584 | tf_op jit(solution)/shard_map/ppermute | solution.py:26
  5.2 8.5 %copy-start = (f32[4,256,512]{2,1,0:T(8,128)S(1)}, f32[4,256,512]{2,1,0:T(8,128)}, u32[]{:S(2)}) copy-start(f32[4,256,512]{2,1,0:T(8,128)} %param.19) | copy-start | bytes 6291460
  7.2 1.3 copy-start.3
  8.5 40.4 %collective-permute-start.1 = (f32[4,1,512]{2,1,0:T(1,128)S(1)}, f32[4,1,512]{2,1,0:T(1,128)S(1)}, u32[]{:S(2)}, u32[]{:S(2)}) collective-permute-start(f32[4,1,512]{2,1,0:T(1,128)S(1)} %slice.225), channel_id=1, source_target_pairs={{0,1},{1,2},{2,3},{4,5},{5,6},{6,7},{8,9},{9,10},{10,11},{12,13},{... | collective-permute-start | bytes 24584 | tf_op jit(solution)/shard_map/ppermute | solution.py:15
  14.6 16.2 %collective-permute-start.3 = (f32[1024,128]{1,0:T(8,128)}, f32[1024,128]{1,0:T(8,128)S(1)}, u32[]{:S(2)}, u32[]{:S(2)}) collective-permute-start(f32[1024,128]{1,0:T(8,128)} %reshape_squeeze.13), channel_id=1, source_target_pairs={{4,0},{8,4},{12,8},{16,12},{20,16},{24,20},{28,24},{5,1},{9,5},{13... | collective-permute-start | bytes 1572872 | tf_op jit(solution)/shard_map/ppermute | solution.py:15
  15.9 2.3 copy-start.5
  16.0 3.4 %copy-start.6 = (f32[4,256,512]{2,1,0:T(8,128)S(1)}, f32[4,256,512]{2,1,0:T(8,128)}, u32[]{:S(2)}) copy-start(f32[4,256,512]{2,1,0:T(8,128)} %param.20) | copy-start | bytes 6291460
  21.3 1.3 copy-start.2
  22.6 2.1 copy-start.11
  22.6 2.2 copy-start.12
  28.3 5.3 %copy-start.4 = (f32[4,128,128]{2,1,0:T(8,128)S(1)}, f32[4,128,128]{2,1,0:T(8,128)}, u32[]{:S(2)}) copy-start(f32[4,128,128]{2,1,0:T(8,128)} %param.27) | copy-start | bytes 786436
  33.6 1.9 copy-start.9
  43.8 17.4 %collective-permute-start.4 = (f32[1024,128]{1,0:T(8,128)}, f32[1024,128]{1,0:T(8,128)}, u32[]{:S(2)}, u32[]{:S(2)}) collective-permute-start(f32[1024,128]{1,0:T(8,128)} %scatter_custom_fusion), channel_id=1, source_target_pairs={{0,4},{4,8},{8,12},{12,16},{16,20},{20,24},{24,28},{1,5},{5,9},{9,... | collective-permute-start | bytes 1572872 | tf_op jit(solution)/shard_map/ppermute | solution.py:15
  48.9 10.3 %copy-start.8 = (f32[1024,128]{1,0:T(8,128)S(1)}, f32[1024,128]{1,0:T(8,128)}, u32[]{:S(2)}) copy-start(f32[1024,128]{1,0:T(8,128)} %get-tuple-element.77) | copy-start | bytes 1572868
  155.2 2.3 copy-start.1
  158.5 16.1 %collective-permute-start.7 = (f32[1024,128]{1,0:T(8,128)}, f32[1024,128]{1,0:T(8,128)S(1)}, u32[]{:S(2)}, u32[]{:S(2)}) collective-permute-start(f32[1024,128]{1,0:T(8,128)} %reshape_squeeze.15), channel_id=1, source_target_pairs={{4,0},{8,4},{12,8},{16,12},{20,16},{24,20},{28,24},{5,1},{9,5},{13... | collective-permute-start | bytes 1572872 | tf_op jit(solution)/shard_map/ppermute | solution.py:15
  160.6 32.3 %collective-permute-start.6 = (f32[4,1,512]{2,1,0:T(1,128)S(1)}, f32[4,1,512]{2,1,0:T(1,128)S(1)}, u32[]{:S(2)}, u32[]{:S(2)}) collective-permute-start(f32[4,1,512]{2,1,0:T(1,128)S(1)} %get-tuple-element.64), channel_id=1, source_target_pairs={{0,1},{1,2},{2,3},{4,5},{5,6},{6,7},{8,9},{9,10},{10,11},{12,13},{... | collective-permute-start | bytes 24584 | tf_op jit(solution)/shard_map/ppermute | solution.py:23
  161.9 31.0 %collective-permute-start.5 = (f32[4,1,512]{2,1,0:T(1,128)S(1)}, f32[4,1,512]{2,1,0:T(1,128)S(1)}, u32[]{:S(2)}, u32[]{:S(2)}) collective-permute-start(f32[4,1,512]{2,1,0:T(1,128)S(1)} %get-tuple-element.63), channel_id=1, source_target_pairs={{1,0},{2,1},{3,2},{5,4},{6,5},{7,6},{9,8},{10,9},{11,10},{13,12},{... | collective-permute-start | bytes 24584 | tf_op jit(solution)/shard_map/ppermute | solution.py:26
  177.3 1.9 copy-start.10
  187.6 19.6 %collective-permute-start.8 = (f32[1024,128]{1,0:T(8,128)}, f32[1024,128]{1,0:T(8,128)}, u32[]{:S(2)}, u32[]{:S(2)}) collective-permute-start(f32[1024,128]{1,0:T(8,128)} %scatter_custom_fusion.1), channel_id=1, source_target_pairs={{0,4},{4,8},{8,12},{12,16},{16,20},{20,24},{24,28},{1,5},{5,9},{9,... | collective-permute-start | bytes 1572872 | tf_op jit(solution)/shard_map/ppermute | solution.py:15
  192.9 12.2 %copy-start.7 = (f32[1024,128]{1,0:T(8,128)S(1)}, f32[1024,128]{1,0:T(8,128)}, u32[]{:S(2)}) copy-start(f32[1024,128]{1,0:T(8,128)} %get-tuple-element.79) | copy-start | bytes 1572868
where the time goes:
time: 260 us; the launch traced here: 259 us
  blocking collectives  119 us (46%)
  other arithmetic  51.1 us (20%)
  local copies, waits for them, and re-layouts  38.5 us (15%)
  starting transfers between devices  24.4 us (9%)
  matrix products  12.5 us (5%)
  waiting for transfers between devices  8.1 us (3%)
  between operations  5.64 us (2%)
    psum x2, blocking collectives, squares(): return lax.psum(jnp.sum(values * values), ('sub', 'blk'))  80.6 us
    psum x1, blocking collectives, body(): alpha = norm_now / lax.psum(jnp.sum(direction * result), ('sub', 'blk'))  38.5 us
    add x2, other arithmetic, body(): result + coeff_z * (direction - next_z) + prev_z * (direction - before_z)  22.5 us
    ppermute x5, starting transfers between devices, shifted(): return lax.ppermute(array, axis, pairs)  18.2 us
    ppermute x5, waiting for transfers between devices, shifted(): return lax.ppermute(array, axis, pairs)  8.09 us
    dot_general x8, matrix products, mortar_jump(): jnp.einsum('kc,ac->ka', gathered, proj[kind], precision=lax.Precision.HIG...  7.91 us
    scatter x2, local copies, waits for them, and re-layouts, body(): ordered = jnp.zeros_like(back).at[partner].set(back)  7.8 us
    slice x2, local copies, waits for them, and re-layouts, body(): direction[:, :, 1:]  7.67 us
  transfers between devices with their start and end apart: 9, of which 2 were waited for; matrix products, arithmetic and copies ran while one was open for 27% of the time, Pallas kernels for 0%

commit v1 on v0

v1 whole, which is shorter than its diff:
```python
import jax
import jax.numpy as jnp
from jax import lax
from jax.experimental import pallas as pl
from jax.experimental.pallas import tpu as pltpu
from jax.sharding import PartitionSpec as P

ROWS = 32
FIELDS = 16
SUB = 8
LANES = 128
F32 = jnp.float32
BF16 = jnp.bfloat16
penalty = 4.0


def tile_ids(dim, shape):
    return lax.broadcasted_iota(jnp.int32, shape, dim)


def as_tile(scalars):
    lane = tile_ids(1, (SUB, LANES))
    tile = jnp.zeros((SUB, LANES), F32)
    for place, value in enumerate(scalars):
        tile = jnp.where(lane == place, value, tile)
    return tile


def from_tile(tile, place):
    pick = (tile_ids(1, tile.shape) == place) & (tile_ids(0, tile.shape) == 0)
    return jnp.sum(jnp.where(pick, tile, 0.0))


def at(array, layers, start):
    return [array[layer, pl.ds(start, SUB), :] for layer in range(layers)]


def stencil(values, after, tx, ty, tz, st, carry, below=None, above=None):
    shape = values[0].shape
    row = tile_ids(0, shape)
    last_z = tile_ids(1, shape) == shape[1] - 1
    results, carries = [], []
    flux_x = None if below is None else below[1] * (below[0] - values[0])
    for layer, value in enumerate(values):
        follow = value if after is None else pltpu.roll(after[layer], SUB - 1, 0)
        follow = jnp.where(row == SUB - 1, follow, pltpu.roll(value, SUB - 1, 0))
        flux_y = ty[layer] * (value - follow)
        rolled = pltpu.roll(flux_y, 1, 0)
        carries.append(rolled)
        flux_z = jnp.where(last_z, 0.0, tz[layer] * (value - pltpu.roll(value, shape[1] - 1, 1)))
        result = st[layer] * value + (flux_y - jnp.where(row == 0, carry[layer], rolled))
        result = result + (flux_z - pltpu.roll(flux_z, 1, 1))
        if flux_x is not None:
            result = result - flux_x
        next_x = values[layer + 1] if layer < len(values) - 1 else above
        flux_x = None
        if next_x is not None:
            flux_x = tx[layer] * (value - next_x)
            result = result + flux_x
        results.append(result)
    return results, carries


def at_last_block():
    return lax.axis_index("blk") == lax.axis_size("blk") - 1


def edge_terms(before, first, last, beyond, ty_before, ty_last):
    low = ty_before * (first - before)
    high = jnp.where(at_last_block(), 0.0, ty_last * (last - beyond))
    return low, high


def pack_kernel(b_hbm, ty_hbm, face, sems):
    rows = b_hbm.shape[1]
    copies = [
        pltpu.make_async_copy(b_hbm.at[0], face.at[pl.ds(0, rows), :], sems.at[0]),
        pltpu.make_async_copy(ty_hbm.at[0, pl.ds(rows - SUB, SUB), :], face.at[pl.ds(rows, SUB), :], sems.at[1]),
    ]
    for copy in copies:
        copy.start()
    for copy in copies:
        copy.wait()


def two_parts(array):
    high = array.astype(BF16)
    return high, (array - high.astype(F32)).astype(BF16)


def prepare_pairs(perm, kind, count, proj, rows, groups, picks, puts, codes, proj_t, proj_n):
    kinds, width, _ = proj.shape
    blocks = rows * groups
    lane = tile_ids(1, (1, blocks))
    target = lax.rem(perm, groups) * rows + lax.div(perm, groups)
    shift = kinds.bit_length()
    keys = (target * (1 << shift) + jnp.where(lane < count, kind, kinds)).astype(F32)
    span = LANES // groups
    spread = tile_ids(1, (span, LANES)) - groups * tile_ids(0, (span, LANES))
    lanes = tile_ids(1, (rows, LANES))
    across = []
    for group in range(groups):
        column = jnp.concatenate(
            [
                jnp.sum(jnp.where(spread == group, keys[:, place * LANES : (place + 1) * LANES], 0.0), 1, keepdims=True)
                for place in range(blocks // LANES)
            ],
            axis=0,
        ).astype(jnp.int32)
        column = jnp.broadcast_to(column, (rows, LANES))
        here = pl.ds(group * rows, rows)
        codes[here, :] = column & ((1 << shift) - 1)
        column = column >> shift
        for place in range(blocks // LANES):
            picks[here, pl.ds(place * LANES, LANES)] = jnp.where(column == lanes + place * LANES, 1.0, 0.0).astype(BF16)
        for place in range(rows // LANES):
            turned = jnp.transpose(column[place * LANES : (place + 1) * LANES].astype(F32))
            across.append(turned[0:1, :].astype(jnp.int32))
    across = jnp.concatenate(across, axis=1)
    down = tile_ids(0, (rows, blocks))
    for group in range(groups):
        puts[pl.ds(group * rows, rows), :] = jnp.where(across == down + group * rows, 1.0, 0.0).astype(BF16)
    for kind in range(kinds):
        here = pl.ds(kind * width, width)
        proj_t[here, :] = jnp.concatenate(two_parts(jnp.transpose(proj[kind])), axis=1)
        proj_n[here, :] = jnp.concatenate(two_parts(proj[kind]), axis=1)


def first_kernel(
    count, perm, kind, proj, b_hbm, tx_hbm, ty_hbm, tz_hbm, st_hbm,
    b, tx, ty, tz, st, face_next, s_first, s_mid, s_last, sums, picks, puts, codes, proj_t, proj_n, total, sems,
):
    layers, rows, depth = b.shape
    steps = rows // ROWS
    sources, targets = (b_hbm, tx_hbm, ty_hbm, tz_hbm, st_hbm), (b, tx, ty, tz, st)

    def copy(which, step):
        part = pl.ds(step * ROWS, ROWS)
        return pltpu.make_async_copy(
            sources[which].at[:, part, :], targets[which].at[:, part, :], sems.at[which, step]
        )

    for step in range(steps):
        for which in range(len(sources)):
            copy(which, step).start()
    width = proj.shape[1]
    prepare_pairs(
        perm[0], kind[0], count[0, 0], proj, rows, depth // width, picks, puts, codes, proj_t, proj_n
    )
    total[...] = jnp.zeros_like(total)
    copy(0, 0).wait()

    def chunk(start, after, carry):
        values = at(b, layers, start)
        results, carry = stencil(values, after, *[at(array, layers, start) for array in (tx, ty, tz, st)], carry)
        here = pl.ds(start, SUB)
        squares, products = values[0] * values[0], values[0] * results[0]
        for layer in range(1, layers):
            squares = squares + values[layer] * values[layer]
            products = products + values[layer] * results[layer]
        total[0] += squares
        total[1] += products
        face_next[here, :] = results[0]
        s_first[here, :] = results[0]
        for layer in range(1, layers - 1):
            s_mid[layer - 1, here, :] = results[layer]
        s_last[here, :] = results[layers - 1]
        return carry

    carry = [jnp.zeros((SUB, depth), F32)] * layers
    for step in range(steps):
        for which in range(1, len(sources)):
            copy(which, step).wait()
        if step < steps - 1:
            copy(0, step + 1).wait()
        for start in range(step * ROWS, (step + 1) * ROWS, SUB):
            carry = chunk(start, None if start == rows - SUB else at(b, layers, start + SUB), carry)
    sums[...] = as_tile([jnp.sum(total[0]), jnp.sum(total[1])])


def up_places(layers):
    return 0, layers, 2 * layers, 3 * layers, 3 * layers + 1, 3 * layers + 2


def edge_kernel(
    sums_in, b, ty, right, up, down, s_first_in, s_mid_in, s_last_in, w_last_in, back_in,
    s_first, s_mid, s_last, w_last, back, sums, right_edges, w_up, w_down,
):
    layers, rows, _ = b.shape
    at_b, at_ty, at_w, at_back, at_right, at_right_ty = up_places(layers)
    product = 0.0
    for layer in range(layers):
        first, last = b[layer, 0:1, :], b[layer, rows - 1 :, :]
        low, high = edge_terms(
            up[at_b + layer : at_b + layer + 1, :], first, last, down[layer : layer + 1, :],
            up[at_ty + layer : at_ty + layer + 1, :], ty[layer, rows - 1 :, :],
        )
        pairs = [(s_first_in, s_first)] if layer == 0 else [(s_last_in, s_last), (w_last_in, w_last)]
        if 0 < layer < layers - 1:
            pairs = [(s_mid_in.at[layer - 1], s_mid.at[layer - 1])]
        for source, target in pairs:
            target[0:1, :] = source[0:1, :] + low
            target[rows - 1 :, :] = source[rows - 1 :, :] + high
        product = product + first * low + last * high
        w_up[layer : layer + 1, :] = up[at_w + layer : at_w + layer + 1, :] - low
        w_down[layer : layer + 1, :] = down[layers + layer : layers + layer + 1, :] - high
    sums[...] = sums_in[...] + as_tile([0.0, jnp.sum(product)])
    back[rows : rows + 1, :] = up[at_back : at_back + 1, :]
    back[rows + 1 : rows + 2, :] = down[2 * layers : 2 * layers + 1, :]
    low, high = edge_terms(
        up[at_right : at_right + 1, :], right[0:1, :], right[rows - 1 : rows, :], down[2 * layers + 1 :, :],
        up[at_right_ty : at_right_ty + 1, :], right[rows + SUB - 1 :, :],
    )
    right_edges[0:1, :] = low
    right_edges[1:2, :] = high


def mm(left, right):
    return lax.dot_general(left, right, (((1,), (0,)), ((), ())), preferred_element_type=F32)


def by_kind(codes, array, kinds):
    zero = jnp.zeros_like(array)
    return jnp.concatenate([jnp.where(codes == kind, array, zero) for kind in range(kinds)], axis=1)


def apply_proj(codes, high, low, proj, kinds, width):
    both = mm(by_kind(codes, high, kinds), proj[...])
    return both[:, :width] + both[:, width:] + mm(by_kind(codes, low, kinds), proj[:, :width])


def take_jump(group, faces, last, picks, codes_col, proj_t):
    width = proj_t.shape[1] // 2
    kinds = proj_t.shape[0] // width
    here = pl.ds(group * last.shape[0], last.shape[0])
    codes = codes_col[here, :]
    taken = mm(picks[here, :], faces)
    projected = apply_proj(codes, taken[:, :width].astype(BF16), taken[:, width:].astype(BF16), proj_t, kinds, width)
    return jnp.where(codes < kinds, last - projected, 0.0)


def turn_back(group, jump, codes_col, proj_n):
    width = proj_n.shape[1] // 2
    kinds = proj_n.shape[0] // width
    scale = jnp.where(lax.axis_index("sub") < lax.axis_size("sub") - 1, -penalty, 0.0)
    codes = codes_col[pl.ds(group * jump.shape[0], jump.shape[0]), :]
    return jnp.concatenate(two_parts(scale * apply_proj(codes, *two_parts(jump), proj_n, kinds, width)), axis=1)


def put_back(group, backs, puts, rows):
    width = backs.shape[1] // 2
    placed = mm(puts[pl.ds(group * rows, rows), :], backs)
    return placed[:, :width] + placed[:, width:]


def stack_parts(parts):
    return jnp.concatenate(two_parts(jnp.concatenate(parts, axis=0)), axis=1)


def jump_first_kernel(b, right, s_last, picks, codes, proj_t, w_last, jump_face, sums):
    width = proj_t.shape[1] // 2
    layers, rows, depth = b.shape
    parts = [pl.ds(group * width, width) for group in range(depth // width)]
    faces = stack_parts([right[:rows, part] for part in parts])
    square = jnp.zeros((rows, width), F32)
    for group, part in enumerate(parts):
        jump = take_jump(group, faces, b[layers - 1, :, part], picks, codes, proj_t)
        square = square + jump * jump
        jump_face[:, part] = jump
        w_last[:, part] = s_last[:, part] + penalty * jump
    sums[...] = as_tile([jnp.sum(square)])


def back_first_kernel(jump, right, b, ty, s_first, s_mid, w_last, puts, codes, proj_n, back, up, down):
    back_kernel(jump, puts, codes, proj_n, back)
    layers, rows, _ = b.shape
    at_b, at_ty, at_w, at_back, at_right, at_right_ty = up_places(layers)
    end = pl.ds(rows - 1, 1)
    back[rows:, :] = jnp.zeros((SUB, back.shape[1]), F32)
    for layer in range(layers):
        image = s_first if layer == 0 else w_last if layer == layers - 1 else s_mid.at[layer - 1]
        up[at_b + layer : at_b + layer + 1, :] = b[layer, end, :]
        up[at_ty + layer : at_ty + layer + 1, :] = ty[layer, end, :]
        up[at_w + layer : at_w + layer + 1, :] = image[end, :]
        down[layer : layer + 1, :] = b[layer, 0:1, :]
        down[layers + layer : layers + layer + 1, :] = image[0:1, :]
    up[at_back : at_back + 1, :] = back[end, :]
    up[at_right : at_right + 1, :] = right[end, :]
    up[at_right_ty : at_right_ty + 1, :] = right[rows + SUB - 1 :, :]
    down[2 * layers : 2 * layers + 1, :] = back[0:1, :]
    down[2 * layers + 1 : 2 * layers + 2, :] = right[0:1, :]


def jump_second_kernel(
    near_sums, w_last, jump, right, right_edges, back_before, picks, codes, proj_t, jump_next, sums, field
):
    width = proj_t.shape[1] // 2
    rows, depth = right.shape
    parts = [pl.ds(group * width, width) for group in range(depth // width)]
    near = from_tile(near_sums[...], 2)
    field[...] = right[...] + back_before[:rows, :]
    field[0:1, :] += right_edges[0:1, :]
    field[rows - 1 :, :] += right_edges[1:2, :]
    faces = stack_parts([field[:, part] for part in parts])
    totals = [jnp.zeros((rows, width), F32)] * 3
    for group, part in enumerate(parts):
        later = take_jump(group, faces, w_last[:, part], picks, codes, proj_t)
        jump_next[:, part] = later
        close = jump[:, part] - near * later
        totals = [total + new for total, new in zip(totals, (close * close, close * later, later * later))]
    found = [jnp.sum(total) for total in totals]
    sums[...] = as_tile([0.0] * 6 + [penalty * found[0], 2.0 * penalty * found[1], penalty * found[2]])


def back_kernel(jump_next, puts, codes, proj_n, back):
    width = proj_n.shape[1] // 2
    rows, depth = jump_next.shape
    parts = [pl.ds(group * width, width) for group in range(depth // width)]
    backs = [turn_back(group, jump_next[:, part], codes, proj_n) for group, part in enumerate(parts)]
    backs = jnp.concatenate(backs, axis=0)
    for group, part in enumerate(parts):
        back[:rows, part] = put_back(group, backs, puts, rows)


def stencil_sums(read, own, near, b, plain, tx, ty, tz, st, image, total):
    layers, rows, depth = b.shape
    first, last = own[0], own[-1]
    total[...] = jnp.zeros_like(total)

    def chunk(start, values, after, carry):
        here = pl.ds(start, SUB)
        below = (values[0], tx[first - 1, here, :]) if first > 0 else None
        above = values[-1] if last < layers - 1 else None
        skip = 0 if below is None else 1
        mine = values[skip : skip + len(own)]
        results, carry = stencil(
            mine, None if after is None else after[skip : skip + len(own)],
            *[[array[layer, here, :] for layer in own] for array in (tx, ty, tz, st)], carry, below, above,
        )
        terms = None
        for place, layer in enumerate(own):
            w, s = mine[place], results[place]
            image[place, here, :] = s
            u = b[layer, here, :] - near * w
            q = plain(layer, here) - near * s
            new = [u * u, u * w, w * w, u * q, u * s + w * q, w * s]
            terms = new if terms is None else [old + more for old, more in zip(terms, new)]
        return terms, carry

    def several(start, count, carry, at_end=False):
        values = [read(pl.multiple_of(start + SUB * place, SUB)) for place in range(count)]
        values.append(None if at_end else read(pl.multiple_of(start + SUB * count, SUB)))
        terms = None
        for place in range(count):
            new, carry = chunk(pl.multiple_of(start + SUB * place, SUB), values[place], values[place + 1], carry)
            terms = new if terms is None else [old + more for old, more in zip(terms, new)]
        for place, term in enumerate(terms):
            total[place] += term
        return carry

    group = 2
    carry = lax.fori_loop(
        0, rows // (group * SUB) - 1,
        lambda index, carry: tuple(several(pl.multiple_of(index * group * SUB, SUB), group, list(carry))),
        (jnp.zeros((SUB, depth), F32),) * len(own),
    )
    several(rows - group * SUB, group, list(carry), True)
    return [jnp.sum(total[place]) for place in range(total.shape[0])]


def second_high_kernel(first_sums, jump_sums, b, s_mid, s_last, w_last, tx, ty, tz, st, image, sums, total):
    layers = b.shape[0]
    split = layers // 2
    norm = from_tile(first_sums[...], 0)
    energy = from_tile(first_sums[...], 1) + penalty * from_tile(jump_sums[...], 0)
    safe = energy > 0.01 * norm
    ratio = jnp.full((SUB, LANES), norm, F32) / jnp.full((SUB, LANES), jnp.where(safe, energy, 1.0), F32)
    near = jnp.where(safe, jnp.max(ratio), 0.0)

    def read(start):
        here = pl.ds(start, SUB)
        return [s_mid[layer - 1, here, :] for layer in range(split - 1, layers - 1)] + [w_last[here, :]]

    def plain(layer, here):
        return s_last[here, :] if layer == layers - 1 else s_mid[layer - 1, here, :]

    found = stencil_sums(read, list(range(split, layers)), near, b, plain, tx, ty, tz, st, image, total)
    sums[...] = as_tile([norm, energy, near] + found)


def second_low_kernel(
    high_sums, jump_sums, b, s_first, s_mid, w_last, recv, w_up, w_down, up, tx, ty, tz, st,
    image, edge_high, table, total,
):
    layers, rows, depth = b.shape
    split = layers // 2
    near = from_tile(high_sums[...], 2)

    def read(start):
        here = pl.ds(start, SUB)
        return [s_first[here, :] + recv[here, :]] + [s_mid[layer - 1, here, :] for layer in range(1, split + 1)]

    def plain(layer, here):
        return s_first[here, :] if layer == 0 else s_mid[layer - 1, here, :]

    found = stencil_sums(read, list(range(split)), near, b, plain, tx, ty, tz, st, image, total)

    def row(layer, place):
        here = pl.ds(place, 1)
        if layer == 0:
            return s_first[here, :] + recv[here, :]
        return w_last[here, :] if layer == layers - 1 else s_mid[layer - 1, here, :]

    extra = [0.0] * 3
    for layer in range(layers):
        before, beyond = w_up[layer : layer + 1, :], w_down[layer : layer + 1, :]
        if layer == 0:
            before, beyond = before + recv[rows : rows + 1, :], beyond + recv[rows + 1 : rows + 2, :]
        ends = row(layer, 0), row(layer, rows - 1)
        added = edge_terms(
            before, *ends, beyond, up[layers + layer : layers + layer + 1, :], ty[layer, rows - 1 :, :]
        )
        for side, (place, w, s) in enumerate(zip((0, rows - 1), ends, added)):
            u = b[layer, place : place + 1, :] - near * w
            new = [-near * u * s, u * s - near * w * s, w * s]
            extra = [old + more for old, more in zip(extra, new)]
            if layer < split:
                image[layer, place : place + 1, :] += s
            else:
                spot = side * (layers - split) + layer - split
                edge_high[spot : spot + 1, :] = s
    extra = [jnp.sum(value) for value in extra]
    sums = high_sums[...] + jump_sums[...] + as_tile([0.0] * 3 + found) + as_tile([0.0] * 6 + extra)
    mine = lax.axis_index("sub") * lax.axis_size("blk") + lax.axis_index("blk")
    device = tile_ids(0, table.shape) * (LANES // FIELDS) + lax.div(tile_ids(1, table.shape), FIELDS)
    field = lax.rem(tile_ids(1, table.shape), FIELDS)
    filled = jnp.zeros(table.shape, F32)
    for place in range(9):
        filled = jnp.where((device == mine) & (field == place), jnp.sum(sums[0:1, place : place + 1]), filled)
    table[...] = filled


def final_kernel(
    tables, b, s_first, s_mid, w_last, recv, image_low, image_high, edge_high, jump_next, recv_next, solution_hbm, residual_hbm,
    solution, residual, sems,
):
    layers, rows, depth = b.shape
    split = image_low.shape[0]
    flat = tables[...]
    norm, energy, near, uu, uw, ww, uq, cross, wq = [
        flat if place == 0 else pltpu.roll(flat, LANES - place, 1) for place in range(9)
    ]
    own = lax.rem(tile_ids(1, flat.shape), FIELDS) == 0

    def whole(array):
        array = jnp.sum(jnp.where(own, array, 0.0), axis=0, keepdims=True)
        return jnp.sum(array, axis=1, keepdims=True)

    norm, energy = whole(norm), whole(energy)
    alpha = norm / energy
    away = alpha - near
    norm_next = whole(uu - away * (2.0 * uw - away * ww))
    energy_next = whole(uq - away * (cross - away * wq))
    beta = norm_next / norm
    step_size = norm_next / (energy_next - beta * norm_next / alpha)
    c0 = jnp.broadcast_to(alpha + step_size * beta + step_size, (SUB, depth))
    c1 = jnp.broadcast_to(step_size * alpha, (SUB, depth))
    c2 = jnp.broadcast_to(alpha + step_size * (1.0 + beta), (SUB, depth))

    def copy(which, step):
        part = pl.ds(step * ROWS, ROWS)
        source, target = ((solution, solution_hbm), (residual, residual_hbm))[which]
        return pltpu.make_async_copy(source.at[:, part, :], target.at[:, part, :], sems.at[which, step])

    for step in range(rows // ROWS):

        def one(index, done):
            here = pl.ds(pl.multiple_of(step * ROWS + index * SUB, SUB), SUB)
            for layer in range(layers):
                v = b[layer, here, :]
                s = image_low[layer, here, :] if layer < split else image_high[layer - split, here, :]
                if layer == 0:
                    w = s_first[here, :] + recv[here, :]
                    s = s + recv_next[here, :]
                elif layer < layers - 1:
                    w = s_mid[layer - 1, here, :]
                else:
                    w = w_last[here, :]
                    s = s + penalty * jump_next[here, :]
                solution[layer, here, :] = c0 * v - c1 * w
                residual[layer, here, :] = v - c2 * w + c1 * s
            return done

        lax.fori_loop(0, ROWS // SUB, one, 0, unroll=True)
        for side, last_step in enumerate((0, rows // ROWS - 1)):
            if step == last_step:
                place = side * (rows - 1)
                for layer in range(split, layers):
                    spot = side * (layers - split) + layer - split
                    residual[layer, place : place + 1, :] += c1[0:1, :] * edge_high[spot : spot + 1, :]
        for which in range(2):
            copy(which, step).start()
    for step in range(rows // ROWS):
        for which in range(2):
            copy(which, step).wait()


SMEM = pl.BlockSpec(memory_space=pltpu.SMEM)
VMEM = pl.BlockSpec(memory_space=pltpu.VMEM)
HBM = pl.BlockSpec(memory_space=pltpu.HBM)


def held(*dims, dtype=F32):
    return pltpu.VMEM(dims, dtype)


def near_core(*arrays):
    return [pltpu.with_memory_space_constraint(array, pltpu.VMEM) for array in arrays]


def in_hbm(*arrays):
    return [pltpu.with_memory_space_constraint(array, pltpu.HBM) for array in arrays]


def params(mib):
    return pltpu.CompilerParams(vmem_limit_bytes=mib * 1024 * 1024)


def shifted(array, axis, by):
    size = lax.axis_size(axis)
    return lax.ppermute(array, axis, [(i, i + by) for i in range(size) if 0 <= i + by < size])


def gather_rows(table):
    for axis in ("blk", "sub"):
        size = lax.axis_size(axis)
        reach = 1 if axis == "blk" else size // 2
        while 0 < reach < size:
            table = table + lax.ppermute(table, axis, [(i, i ^ reach) for i in range(size)])
            reach = reach * 2 if axis == "blk" else reach // 2
    return table


def body(right_side, trans_x, trans_y, trans_z, storage, pair_perm, pair_type, pair_count, proj):
    layers, rows, depth = right_side.shape
    blocks, width, kinds = pair_perm.shape[2], proj.shape[1], proj.shape[0]
    subs, blks = lax.axis_size("sub"), lax.axis_size("blk")
    steps = rows // ROWS
    cells = layers * rows * depth
    cost = lambda flops, size: pl.CostEstimate(flops=int(flops), bytes_accessed=int(size), transcendentals=0)

    (face,) = pl.pallas_call(
        pack_kernel,
        in_specs=[HBM, HBM],
        out_specs=[VMEM],
        out_shape=[held(rows + SUB, depth)],
        scratch_shapes=[pltpu.SemaphoreType.DMA((2,))],
        compiler_params=params(2),
        cost_estimate=cost(0, 4 * rows * depth),
        name="pack",
    )(*in_hbm(right_side, trans_y))
    face_right = shifted(face, "sub", -1)

    b, tx, ty, tz, st, face_next, s_first, s_mid, s_last, first_sums, picks, puts, codes, proj_t, proj_n = pl.pallas_call(
        first_kernel,
        in_specs=[SMEM] + [VMEM] * 3 + [HBM] * 5,
        out_specs=[VMEM] * 15,
        out_shape=[held(layers, rows, depth)] * 5
        + [
            held(rows, depth), held(rows, depth), held(layers - 2, rows, depth), held(rows, depth), held(SUB, LANES),
            held(blocks, blocks, dtype=BF16), held(blocks, blocks, dtype=BF16), held(blocks, width, dtype=jnp.int32),
            held(kinds * width, 2 * width, dtype=BF16), held(kinds * width, 2 * width, dtype=BF16),
        ],
        scratch_shapes=[pltpu.VMEM((2, SUB, depth), F32), pltpu.SemaphoreType.DMA((5, steps))],
        compiler_params=params(16),
        cost_estimate=cost(20 * cells, 24 * cells),
        name="stencil_first",
    )(
        pair_count, pair_perm, pair_type, proj,
        *in_hbm(right_side, trans_x, trans_y, trans_z, storage),
    )
    face_right_next = shifted(face_next, "sub", -1)

    mortar_cost = cost(4 * blocks * blocks * width + 6 * kinds * blocks * width * width, 14 * rows * depth)
    w_last, jump, jump_sums = pl.pallas_call(
        jump_first_kernel,
        in_specs=[VMEM] * 6,
        out_specs=[VMEM] * 3,
        out_shape=[held(rows, depth), held(rows, depth), held(SUB, LANES)],
        compiler_params=params(16),
        cost_estimate=mortar_cost,
        name="jump_first",
    )(*near_core(b, face_right, s_last, picks, codes, proj_t))
    back, up_out, down_out = pl.pallas_call(
        back_first_kernel,
        in_specs=[VMEM] * 10,
        out_specs=[VMEM] * 3,
        out_shape=[held(rows + SUB, depth), held(3 * layers + 3, depth), held(2 * layers + 2, depth)],
        compiler_params=params(16),
        cost_estimate=mortar_cost,
        name="back_first",
    )(*near_core(jump, face_right, b, ty, s_first, s_mid, w_last, puts, codes, proj_n))
    up = shifted(up_out, "blk", 1)
    down = shifted(down_out, "blk", -1)
    s_first, s_mid, s_last, w_last, back, first_sums, right_edges, w_up, w_down = pl.pallas_call(
        edge_kernel,
        in_specs=[VMEM] * 11,
        out_specs=[VMEM] * 9,
        out_shape=[held(rows, depth), held(layers - 2, rows, depth), held(rows, depth), held(rows, depth)]
        + [held(rows + SUB, depth), held(SUB, LANES), held(2, depth), held(layers, depth), held(layers, depth)],
        input_output_aliases={6: 0, 7: 1, 8: 2, 9: 3, 10: 4},
        compiler_params=params(2),
        cost_estimate=cost(32 * depth, 64 * depth),
        name="edges_first",
    )(*near_core(first_sums, b, ty, face_right, up, down, s_first, s_mid, s_last, w_last, back))
    recv = shifted(back, "sub", 1)

    split = layers // 2
    image_high, high_sums = pl.pallas_call(
        second_high_kernel,
        in_specs=[VMEM] * 10,
        out_specs=[VMEM] * 2,
        out_shape=[held(layers - split, rows, depth), held(SUB, LANES)],
        scratch_shapes=[pltpu.VMEM((6, SUB, depth), F32)],
        compiler_params=params(8),
        cost_estimate=cost(20 * cells, 15 * cells),
        name="stencil_second_high",
    )(*near_core(first_sums, jump_sums, b, s_mid, s_last, w_last, tx, ty, tz, st))

    jump_next, second_sums = pl.pallas_call(
        jump_second_kernel,
        in_specs=[VMEM] * 9,
        out_specs=[VMEM] * 2,
        out_shape=[held(rows, depth), held(SUB, LANES)],
        scratch_shapes=[pltpu.VMEM((rows, depth), F32)],
        compiler_params=params(16),
        cost_estimate=mortar_cost,
        name="jump_second",
    )(*near_core(high_sums, w_last, jump, face_right_next, right_edges, back, picks, codes, proj_t))

    count = subs * blks
    image_low, edge_high, table = pl.pallas_call(
        second_low_kernel,
        in_specs=[VMEM] * 14,
        out_specs=[VMEM] * 3,
        out_shape=[held(split, rows, depth), held(2 * (layers - split), depth), held(-(-count * FIELDS // LANES), LANES)],
        scratch_shapes=[pltpu.VMEM((6, SUB, depth), F32)],
        compiler_params=params(8),
        cost_estimate=cost(20 * cells, 15 * cells),
        name="stencil_second_low",
    )(
        *near_core(
            high_sums, second_sums, b, s_first, s_mid, w_last, recv, w_up, w_down, up, tx, ty, tz, st,
        )
    )
    tables = gather_rows(table)

    (back_next,) = pl.pallas_call(
        back_kernel,
        in_specs=[VMEM] * 4,
        out_specs=[VMEM],
        out_shape=[held(rows, depth)],
        compiler_params=params(16),
        cost_estimate=mortar_cost,
        name="back_second",
    )(*near_core(jump_next, puts, codes, proj_n))
    recv_next = shifted(back_next, "sub", 1)

    return pl.pallas_call(
        final_kernel,
        in_specs=[VMEM] * 11,
        out_specs=[HBM] * 2,
        out_shape=[jax.ShapeDtypeStruct((layers, rows, depth), F32)] * 2,
        scratch_shapes=[pltpu.VMEM((layers, rows, depth), F32)] * 2 + [pltpu.SemaphoreType.DMA((2, steps))],
        compiler_params=params(8),
        cost_estimate=cost(8 * cells, 22 * cells),
        name="final_update",
    )(*near_core(tables, b, s_first, s_mid, w_last, recv, image_low, image_high, edge_high, jump_next, recv_next))


def solution(mesh):
    cells = P("sub", "blk", None)
    in_specs = (cells,) * 7 + (P("sub", "blk"), P())
    return jax.shard_map(body, mesh=mesh, in_specs=in_specs, out_specs=(cells, cells), check_vma=False)
```

time: 260 us -> 71.1 us (0.27)
  blocking collectives: 119 us -> 0 us
  other arithmetic: 51.1 us -> 0.02 us
  local copies, waits for them, and re-layouts: 38.5 us -> 0.01 us
  Pallas kernels: 0 us -> 21.8 us
  waiting for transfers between devices: 8.1 us -> 23.9 us
  matrix products: 12.5 us -> 0 us
  between operations: 5.64 us -> 1.45 us
    psum x3 -> x0, blocking collectives: 119 us -> none  [the longest x2 80.6 us: squares(): return lax.psum(jnp.sum(values * values), ('sub', 'blk'))]
    add x3 -> x5, other arithmetic: 24.6 us -> 0.02 us  [gather_rows(): table + lax.ppermute(table, axis, [(i, i ^ reach) for i in range(size)])]
    pallas_call x0 -> x10, Pallas kernels: none -> 21.8 us  [the longest x1 5.33 us: body(): pl.pallas_call(first_kernel, in_specs=[SMEM] + [VMEM] * 3 + [HBM] * 5, ou...]
    ppermute x9 -> x11, waiting for transfers between devices: 8.1 us -> 23.9 us  [the longest x6 15.3 us: shifted(): lax.ppermute(array, axis, [(i, i + by) for i in range(size) if 0 <= i + b...]
    slice x10 -> x0, local copies, waits for them, and re-layouts: 15.4 us -> none  [the longest x2 7.67 us: body(): direction[:, :, 1:]]
    dot_general x16 -> x0, matrix products: 12.5 us -> none  [the longest x8 7.91 us: mortar_jump(): jnp.einsum('kc,ac->ka', gathered, proj[kind], precision=lax.Precision.HIG...]
    reduce_sum x3 -> x0, other arithmetic: 8.83 us -> none  [the longest x2 6.09 us: body(): alpha = norm_now / lax.psum(jnp.sum(direction * result), ('sub', 'blk'))]
    scatter x2 -> x0, local copies, waits for them, and re-layouts: 7.8 us -> none  [body(): ordered = jnp.zeros_like(back).at[partner].set(back)]
  transfers between devices with their start and end apart: 9 -> 11, of which waited for: 2 -> 8; matrix products, arithmetic and copies ran while one was open for 27% -> 0% of each run, Pallas kernels for 0% -> 26%
where the time goes in v1:
time: 71.1 us; the launch traced here: 70.8 us
  waiting for transfers between devices  23.9 us (34%)
  starting transfers between devices  23.7 us (33%)
  Pallas kernels  21.8 us (31%)
  between operations  1.45 us (2%)
    ppermute x6, waiting for transfers between devices, shifted(): lax.ppermute(array, axis, [(i, i + by) for i in range(size) if 0 <= i + b...  15.3 us
    ppermute x6, starting transfers between devices, shifted(): lax.ppermute(array, axis, [(i, i + by) for i in range(size) if 0 <= i + b...  12.1 us
    ppermute x5, starting transfers between devices, gather_rows(): lax.ppermute(table, axis, [(i, i ^ reach) for i in range(size)])  11.6 us
    ppermute x5, waiting for transfers between devices, gather_rows(): lax.ppermute(table, axis, [(i, i ^ reach) for i in range(size)])  8.54 us
    pallas_call x1, Pallas kernels, body(): pl.pallas_call(first_kernel, in_specs=[SMEM] + [VMEM] * 3 + [HBM] * 5, ou...  5.33 us
    pallas_call x1, Pallas kernels, body(): pl.pallas_call(second_high_kernel, in_specs=[VMEM] * 10, out_specs=[VMEM]...  3.31 us
    pallas_call x1, Pallas kernels, body(): pl.pallas_call(second_low_kernel, in_specs=[VMEM] * 14, out_specs=[VMEM]...  3.29 us
    pallas_call x1, Pallas kernels, body(): pl.pallas_call(final_kernel, in_specs=[VMEM] * 11, out_specs=[HBM] * 2, o...  2.47 us
  transfers between devices with their start and end apart: 11, of which 8 were waited for; matrix products, arithmetic and copies ran while one was open for 0% of the time, Pallas kernels for 26%

profile of v1, /device:TPU:0, one launch (start us, length us, event | category | flops | bytes accessed | tf_op | source)
XLA Modules:
  0.0 70.8 jit_solution(9801130505876141112)
XLA Ops:
  0.6 0.0 copy-start
  0.6 0.0 copy-start.2
  0.7 0.0 copy-start.1
  0.7 1.1 %pack.1 = f32[264,512]{1,0:T(8,128)S(1)} custom-call(f32[4,256,512]{2,1,0:T(8,128)} %b_hbm.3, f32[4,256,512]{2,1,0:T(8,128)} %ty_hbm.3), custom_call_target="tpu_custom_call" | custom-call | bytes 524288 | tf_op jit(solution)/shard_map/pack/pallas_call | solution.py:552
  1.8 1.3 %collective-permute-start = (f32[264,512]{1,0:T(8,128)S(1)}, f32[264,512]{1,0:T(8,128)S(1)}, u32[]{:S(2)}, u32[]{:S(2)}) collective-permute-start(f32[264,512]{1,0:T(8,128)S(1)} %pack.1), channel_id=1, source_target_pairs={{4,0},{8,4},{12,8},{16,12},{20,16},{24,20},{28,24},{5,1},{9,5},{13... | collective-permute-start | bytes 1622024 | tf_op jit(solution)/shard_map/ppermute | solution.py:531
  3.7 0.0 copy-done
  3.7 0.0 copy-done.2
  3.7 0.0 copy-done.1
  3.7 5.3 %stencil_first.1 = (f32[4,256,512]{2,1,0:T(8,128)S(1)}, f32[4,256,512]{2,1,0:T(8,128)S(1)}, f32[4,256,512]{2,1,0:T(8,128)S(1)}, f32[4,256,512]{2,1,0:T(8,128)S(1...) custom-call(s32[1,1]{1,0:T(1,128)S(6)} %copy.21.count, ...), custom_call_target="tpu_custom_call" | custom-call | flops 10485760 | bytes 12582912 | tf_op jit(solution)/shard_map/stencil_first/pallas_call | solution.py:564
  9.1 1.3 %collective-permute-start.3 = (f32[256,512]{1,0:T(8,128)S(1)}, f32[256,512]{1,0:T(8,128)S(1)}, u32[]{:S(2)}, u32[]{:S(2)}) collective-permute-start(f32[256,512]{1,0:T(8,128)S(1)} %get-tuple-element.64), channel_id=1, source_target_pairs={{4,0},{8,4},{12,8},{16,12},{20,16},{24,20},{28,24},{5,1},{9,5},{13... | collective-permute-start | bytes 1572872 | tf_op jit(solution)/shard_map/ppermute | solution.py:531
  10.4 9.3 %collective-permute-done.right = f32[264,512]{1,0:T(8,128)S(1)} collective-permute-done((f32[264,512]{1,0:T(8,128)S(1)}, f32[264,512]{1,0:T(8,128)S(1)}, u32[]{:S(2)}, u32[]{:S(2)}) %collective-permute-start) | collective-permute-done | bytes 540704 | tf_op jit(solution)/shard_map/ppermute | solution.py:531
  19.7 1.8 %jump_first.1 = (f32[256,512]{1,0:T(8,128)S(1)}, f32[256,512]{1,0:T(8,128)S(1)}, f32[8,128]{1,0:T(8,128)S(1)}) custom-call(f32[4,256,512]{2,1,0:T(8,128)S(1)} %get-tuple-element.40.b, f32[264,512]{1,0:T(8,128)S(1)} %collective-permute-done.right, f32[256,512]{1,0:T(8,128)S(1)} %get-tuple-element.42.s_last.s_last_in, ...), custom_call_target="tpu_custom_call" | custom-call | flops 939524096 | bytes 1835008 | tf_op jit(solution)/shard_map/jump_first/pallas_call | solution.py:585
  21.5 1.3 %back_first.1 = (f32[264,512]{1,0:T(8,128)S(1)}, f32[15,512]{1,0:T(8,128)S(1)}, f32[10,512]{1,0:T(8,128)S(1)}) custom-call(f32[256,512]{1,0:T(8,128)S(1)} %get-tuple-element.46.jump, f32[264,512]{1,0:T(8,128)S(1)} %collective-permute-done.right, f32[4,256,512]{2,1,0:T(8,128)S(1)} %get-tuple-element.40.b, f32[4,256,512]{2,1,0:T(8,128)S(1)} %get-tuple-element.41.ty, ...), custom_call_target="tpu_custom_call" | custom-call | flops 939524096 | bytes 1835008 | tf_op jit(solution)/shard_map/back_first/pallas_call | solution.py:594
  22.8 1.3 %collective-permute-start.1 = (f32[15,512]{1,0:T(8,128)S(1)}, f32[15,512]{1,0:T(8,128)S(1)}, u32[]{:S(2)}, u32[]{:S(2)}) collective-permute-start(f32[15,512]{1,0:T(8,128)S(1)} %get-tuple-element.52), channel_id=1, source_target_pairs={{0,1},{1,2},{2,3},{4,5},{5,6},{6,7},{8,9},{9,10},{10,11},{12,13},{... | collective-permute-start | bytes 92168 | tf_op jit(solution)/shard_map/ppermute | solution.py:531
  24.1 1.3 %collective-permute-start.2 = (f32[10,512]{1,0:T(8,128)S(1)}, f32[10,512]{1,0:T(8,128)S(1)}, u32[]{:S(2)}, u32[]{:S(2)}) collective-permute-start(f32[10,512]{1,0:T(8,128)S(1)} %get-tuple-element.53), channel_id=1, source_target_pairs={{1,0},{2,1},{3,2},{5,4},{6,5},{7,6},{9,8},{10,9},{11,10},{13,12},{... | collective-permute-start | bytes 61448 | tf_op jit(solution)/shard_map/ppermute | solution.py:531
  25.4 4.1 %collective-permute-done.2.down = f32[10,512]{1,0:T(8,128)S(1)} collective-permute-done((f32[10,512]{1,0:T(8,128)S(1)}, f32[10,512]{1,0:T(8,128)S(1)}, u32[]{:S(2)}, u32[]{:S(2)}) %collective-permute-start.2) | collective-permute-done | bytes 20512 | tf_op jit(solution)/shard_map/ppermute | solution.py:531
  29.5 0.0 collective-permute-done.1.up
  29.5 0.1 edges_first.1
  29.6 4.3 %collective-permute-start.4 = (f32[264,512]{1,0:T(8,128)S(1)}, f32[264,512]{1,0:T(8,128)S(1)}, u32[]{:S(2)}, u32[]{:S(2)}) collective-permute-start(f32[264,512]{1,0:T(8,128)S(1)} %get-tuple-element.66.back_before), channel_id=1, source_target_pairs={{0,4},{4,8},{8,12},{12,16},{16,20},{20,24},{24,28},{1,5},{5,9},{9,... | collective-permute-start | bytes 1622024 | tf_op jit(solution)/shard_map/ppermute | solution.py:531
  34.0 3.3 %stencil_second_high.1 = (f32[2,256,512]{2,1,0:T(8,128)S(1)}, f32[8,128]{1,0:T(8,128)S(1)}) custom-call(f32[8,128]{1,0:T(8,128)S(1)} %get-tuple-element.55.first_sums, f32[8,128]{1,0:T(8,128)S(1)} %get-tuple-element.56.jump_sums, f32[4,256,512]{2,1,0:T(8,128)S(1)} %get-tuple-element.40.b, f32[2,256,512]{2,1,0:T(8,128)S(1)} %get-tuple-element.57.s_mid, ...), custom_call_target="tpu_custom_call" | custom-call | flops 10485760 | bytes 7864320 | tf_op jit(solution)/shard_map/stencil_second_high/pallas_call | solution.py:619
  37.3 0.0 collective-permute-done.3.right
  37.3 1.8 %jump_second.1 = (f32[256,512]{1,0:T(8,128)S(1)}, f32[8,128]{1,0:T(8,128)S(1)}) custom-call(f32[8,128]{1,0:T(8,128)S(1)} %get-tuple-element.63.near_sums.high_sums, f32[256,512]{1,0:T(8,128)S(1)} %get-tuple-element.59.w_last, f32[256,512]{1,0:T(8,128)S(1)} %get-tuple-element.46.jump, f32[256,512]{1,0:T(8,128)S(1)} %collective-permute-done.3.right, ...), custom_call_target="tpu_custom_call" | custom-call | flops 939524096 | bytes 1835008 | tf_op jit(solution)/shard_map/jump_second/pallas_call | solution.py:630
  39.1 1.3 %back_second.1 = f32[256,512]{1,0:T(8,128)S(1)} custom-call(f32[256,512]{1,0:T(8,128)S(1)} %get-tuple-element.75.jump_next, bf16[1024,1024]{1,0:T(8,128)(2,1)S(1)} %get-tuple-element.50.puts, s32[1024,128]{1,0:T(8,128)S(1)} %get-tuple-element.44.codes, bf16[512,256]{1,0:T(8,128)(2,1)S(1)} %get-tuple-element.51.proj_n), custom_call_target="tpu_custom_call" | custom-call | flops 939524096 | bytes 1835008 | tf_op jit(solution)/shard_map/back_second/pallas_call | solution.py:658
  40.4 2.6 %collective-permute-start.10 = (f32[256,512]{1,0:T(8,128)S(1)}, f32[256,512]{1,0:T(8,128)S(1)}, u32[]{:S(2)}, u32[]{:S(2)}) collective-permute-start(f32[256,512]{1,0:T(8,128)S(1)} %back_second.1), channel_id=1, source_target_pairs={{0,4},{4,8},{8,12},{12,16},{16,20},{20,24},{24,28},{1,5},{5,9},{9,... | collective-permute-start | bytes 1572872 | tf_op jit(solution)/shard_map/ppermute | solution.py:531
  43.0 1.9 %collective-permute-done.4.recv = f32[264,512]{1,0:T(8,128)S(1)} collective-permute-done((f32[264,512]{1,0:T(8,128)S(1)}, f32[264,512]{1,0:T(8,128)S(1)}, u32[]{:S(2)}, u32[]{:S(2)}) %collective-permute-start.4) | collective-permute-done | bytes 540704 | tf_op jit(solution)/shard_map/ppermute | solution.py:531
  44.9 3.3 %stencil_second_low.1 = (f32[2,256,512]{2,1,0:T(8,128)S(1)}, f32[4,512]{1,0:T(4,128)S(1)}, f32[4,128]{1,0:T(4,128)S(1)}) custom-call(f32[8,128]{1,0:T(8,128)S(1)} %get-tuple-element.63.near_sums.high_sums, f32[8,128]{1,0:T(8,128)S(1)} %get-tuple-element.67.jump_sums, f32[4,256,512]{2,1,0:T(8,128)S(1)} %get-tuple-element.40.b, ...), custom_call_target="tpu_custom_call" | custom-call | flops 10485760 | bytes 7864320 | tf_op jit(solution)/shard_map/stencil_second_low/pallas_call | solution.py:642
  48.1 3.6 %collective-permute-start.5 = (f32[4,128]{1,0:T(4,128)S(1)}, f32[4,128]{1,0:T(4,128)S(1)}, u32[]{:S(2)}, u32[]{:S(2)}) collective-permute-start(f32[4,128]{1,0:T(4,128)S(1)} %get-tuple-element.71), channel_id=1, source_target_pairs={{0,1},{1,0},{2,3},{3,2},{4,5},{5,4},{6,7},{7,6},{8,9},{9,8},{10,11... | collective-permute-start | bytes 6152 | tf_op jit(solution)/shard_map/ppermute | solution.py:539
  51.8 0.8 %collective-permute-done.5 = f32[4,128]{1,0:T(4,128)S(1)} collective-permute-done((f32[4,128]{1,0:T(4,128)S(1)}, f32[4,128]{1,0:T(4,128)S(1)}, u32[]{:S(2)}, u32[]{:S(2)}) %collective-permute-start.5) | collective-permute-done | bytes 2080 | tf_op jit(solution)/shard_map/ppermute | solution.py:539
  52.6 0.9 %collective-permute-start.6 = (f32[4,128]{1,0:T(4,128)S(1)}, f32[4,128]{1,0:T(4,128)S(1)}, u32[]{:S(2)}, u32[]{:S(2)}) collective-permute-start(f32[4,128]{1,0:T(4,128)S(1)} %add.15), channel_id=1, source_target_pairs={{0,2},{1,3},{2,0},{3,1},{4,6},{5,7},{6,4},{7,5},{8,10},{9,11},{10,... | collective-permute-start | bytes 6152 | tf_op jit(solution)/shard_map/ppermute | solution.py:539
  53.5 2.7 %collective-permute-done.6 = f32[4,128]{1,0:T(4,128)S(1)} collective-permute-done((f32[4,128]{1,0:T(4,128)S(1)}, f32[4,128]{1,0:T(4,128)S(1)}, u32[]{:S(2)}, u32[]{:S(2)}) %collective-permute-start.6) | collective-permute-done | bytes 2080 | tf_op jit(solution)/shard_map/ppermute | solution.py:539
  56.2 2.6 %collective-permute-start.7 = (f32[4,128]{1,0:T(4,128)S(1)}, f32[4,128]{1,0:T(4,128)S(1)}, u32[]{:S(2)}, u32[]{:S(2)}) collective-permute-start(f32[4,128]{1,0:T(4,128)S(1)} %add.16), channel_id=1, source_target_pairs={{0,16},{4,20},{8,24},{12,28},{16,0},{20,4},{24,8},{28,12},{1,17},{... | collective-permute-start | bytes 6152 | tf_op jit(solution)/shard_map/ppermute | solution.py:539
  58.8 1.9 %collective-permute-done.7 = f32[4,128]{1,0:T(4,128)S(1)} collective-permute-done((f32[4,128]{1,0:T(4,128)S(1)}, f32[4,128]{1,0:T(4,128)S(1)}, u32[]{:S(2)}, u32[]{:S(2)}) %collective-permute-start.7) | collective-permute-done | bytes 2080 | tf_op jit(solution)/shard_map/ppermute | solution.py:539
  60.7 2.2 %collective-permute-start.8 = (f32[4,128]{1,0:T(4,128)S(1)}, f32[4,128]{1,0:T(4,128)S(1)}, u32[]{:S(2)}, u32[]{:S(2)}) collective-permute-start(f32[4,128]{1,0:T(4,128)S(1)} %add.17), channel_id=1, source_target_pairs={{0,8},{4,12},{8,0},{12,4},{16,24},{20,28},{24,16},{28,20},{1,9},{5... | collective-permute-start | bytes 6152 | tf_op jit(solution)/shard_map/ppermute | solution.py:539
  62.9 1.6 %collective-permute-done.8 = f32[4,128]{1,0:T(4,128)S(1)} collective-permute-done((f32[4,128]{1,0:T(4,128)S(1)}, f32[4,128]{1,0:T(4,128)S(1)}, u32[]{:S(2)}, u32[]{:S(2)}) %collective-permute-start.8) | collective-permute-done | bytes 2080 | tf_op jit(solution)/shard_map/ppermute | solution.py:539
  64.5 2.3 %collective-permute-start.9 = (f32[4,128]{1,0:T(4,128)S(1)}, f32[4,128]{1,0:T(4,128)S(1)}, u32[]{:S(2)}, u32[]{:S(2)}) collective-permute-start(f32[4,128]{1,0:T(4,128)S(1)} %add.18), channel_id=1, source_target_pairs={{0,4},{4,0},{8,12},{12,8},{16,20},{20,16},{24,28},{28,24},{1,5},{5... | collective-permute-start | bytes 6152 | tf_op jit(solution)/shard_map/ppermute | solution.py:539
  66.8 1.6 %collective-permute-done.9 = f32[4,128]{1,0:T(4,128)S(1)} collective-permute-done((f32[4,128]{1,0:T(4,128)S(1)}, f32[4,128]{1,0:T(4,128)S(1)}, u32[]{:S(2)}, u32[]{:S(2)}) %collective-permute-start.9) | collective-permute-done | bytes 2080 | tf_op jit(solution)/shard_map/ppermute | solution.py:539
  68.3 0.0 collective-permute-done.10.recv_next
  68.3 2.5 %final_update.1 = (f32[4,256,512]{2,1,0:T(8,128)}, f32[4,256,512]{2,1,0:T(8,128)}) custom-call(f32[4,128]{1,0:T(4,128)S(1)} %add.19.tables, f32[4,256,512]{2,1,0:T(8,128)S(1)} %get-tuple-element.40.b, f32[256,512]{1,0:T(8,128)S(1)} %get-tuple-element.68.s_first, f32[2,256,512]{2,1,0:T(8,128)S(1)} %get-tuple-element.57.s_mid, ...), custom_call_target="tpu_custom_call" | custom-call | flops 4194304 | bytes 11534336 | tf_op jit(solution)/shard_map/final_update/pallas_call | solution.py:669
  (5 shorter events, 0.0 us)
Async XLA Ops:
  0.6 3.1 %copy-start = (f32[4,128,128]{2,1,0:T(8,128)S(1)}, f32[4,128,128]{2,1,0:T(8,128)}, u32[]{:S(2)}) copy-start(f32[4,128,128]{2,1,0:T(8,128)} %proj.1) | copy-start | bytes 786436
  0.6 3.1 %copy-start.2 = (s32[1,1,1024]{2,1,0:T(1,128)S(1)}, s32[1,1,1024]{2,1,0:T(1,128)}, u32[]{:S(2)}) copy-start(s32[1,1,1024]{2,1,0:T(1,128)} %kind.1) | copy-start | bytes 12292
  0.7 3.1 %copy-start.1 = (s32[1,1,1024]{2,1,0:T(1,128)S(1)}, s32[1,1,1024]{2,1,0:T(1,128)}, u32[]{:S(2)}) copy-start(s32[1,1,1024]{2,1,0:T(1,128)} %perm.1) | copy-start | bytes 12292
  1.8 17.9 %collective-permute-start = (f32[264,512]{1,0:T(8,128)S(1)}, f32[264,512]{1,0:T(8,128)S(1)}, u32[]{:S(2)}, u32[]{:S(2)}) collective-permute-start(f32[264,512]{1,0:T(8,128)S(1)} %pack.1), channel_id=1, source_target_pairs={{4,0},{8,4},{12,8},{16,12},{20,16},{24,20},{28,24},{5,1},{9,5},{13... | collective-permute-start | bytes 1622024 | tf_op jit(solution)/shard_map/ppermute | solution.py:531
  9.1 28.2 %collective-permute-start.3 = (f32[256,512]{1,0:T(8,128)S(1)}, f32[256,512]{1,0:T(8,128)S(1)}, u32[]{:S(2)}, u32[]{:S(2)}) collective-permute-start(f32[256,512]{1,0:T(8,128)S(1)} %get-tuple-element.64), channel_id=1, source_target_pairs={{4,0},{8,4},{12,8},{16,12},{20,16},{24,20},{28,24},{5,1},{9,5},{13... | collective-permute-start | bytes 1572872 | tf_op jit(solution)/shard_map/ppermute | solution.py:531
  22.8 6.7 %collective-permute-start.1 = (f32[15,512]{1,0:T(8,128)S(1)}, f32[15,512]{1,0:T(8,128)S(1)}, u32[]{:S(2)}, u32[]{:S(2)}) collective-permute-start(f32[15,512]{1,0:T(8,128)S(1)} %get-tuple-element.52), channel_id=1, source_target_pairs={{0,1},{1,2},{2,3},{4,5},{5,6},{6,7},{8,9},{9,10},{10,11},{12,13},{... | collective-permute-start | bytes 92168 | tf_op jit(solution)/shard_map/ppermute | solution.py:531
  24.1 5.4 %collective-permute-start.2 = (f32[10,512]{1,0:T(8,128)S(1)}, f32[10,512]{1,0:T(8,128)S(1)}, u32[]{:S(2)}, u32[]{:S(2)}) collective-permute-start(f32[10,512]{1,0:T(8,128)S(1)} %get-tuple-element.53), channel_id=1, source_target_pairs={{1,0},{2,1},{3,2},{5,4},{6,5},{7,6},{9,8},{10,9},{11,10},{13,12},{... | collective-permute-start | bytes 61448 | tf_op jit(solution)/shard_map/ppermute | solution.py:531
  29.6 15.2 %collective-permute-start.4 = (f32[264,512]{1,0:T(8,128)S(1)}, f32[264,512]{1,0:T(8,128)S(1)}, u32[]{:S(2)}, u32[]{:S(2)}) collective-permute-start(f32[264,512]{1,0:T(8,128)S(1)} %get-tuple-element.66.back_before), channel_id=1, source_target_pairs={{0,4},{4,8},{8,12},{12,16},{16,20},{20,24},{24,28},{1,5},{5,9},{9,... | collective-permute-start | bytes 1622024 | tf_op jit(solution)/shard_map/ppermute | solution.py:531
  40.4 27.9 %collective-permute-start.10 = (f32[256,512]{1,0:T(8,128)S(1)}, f32[256,512]{1,0:T(8,128)S(1)}, u32[]{:S(2)}, u32[]{:S(2)}) collective-permute-start(f32[256,512]{1,0:T(8,128)S(1)} %back_second.1), channel_id=1, source_target_pairs={{0,4},{4,8},{8,12},{12,16},{16,20},{20,24},{24,28},{1,5},{5,9},{9,... | collective-permute-start | bytes 1572872 | tf_op jit(solution)/shard_map/ppermute | solution.py:531
  48.1 4.5 %collective-permute-start.5 = (f32[4,128]{1,0:T(4,128)S(1)}, f32[4,128]{1,0:T(4,128)S(1)}, u32[]{:S(2)}, u32[]{:S(2)}) collective-permute-start(f32[4,128]{1,0:T(4,128)S(1)} %get-tuple-element.71), channel_id=1, source_target_pairs={{0,1},{1,0},{2,3},{3,2},{4,5},{5,4},{6,7},{7,6},{8,9},{9,8},{10,11... | collective-permute-start | bytes 6152 | tf_op jit(solution)/shard_map/ppermute | solution.py:539
  52.6 3.6 %collective-permute-start.6 = (f32[4,128]{1,0:T(4,128)S(1)}, f32[4,128]{1,0:T(4,128)S(1)}, u32[]{:S(2)}, u32[]{:S(2)}) collective-permute-start(f32[4,128]{1,0:T(4,128)S(1)} %add.15), channel_id=1, source_target_pairs={{0,2},{1,3},{2,0},{3,1},{4,6},{5,7},{6,4},{7,5},{8,10},{9,11},{10,... | collective-permute-start | bytes 6152 | tf_op jit(solution)/shard_map/ppermute | solution.py:539
  56.2 4.5 %collective-permute-start.7 = (f32[4,128]{1,0:T(4,128)S(1)}, f32[4,128]{1,0:T(4,128)S(1)}, u32[]{:S(2)}, u32[]{:S(2)}) collective-permute-start(f32[4,128]{1,0:T(4,128)S(1)} %add.16), channel_id=1, source_target_pairs={{0,16},{4,20},{8,24},{12,28},{16,0},{20,4},{24,8},{28,12},{1,17},{... | collective-permute-start | bytes 6152 | tf_op jit(solution)/shard_map/ppermute | solution.py:539
  60.7 3.8 %collective-permute-start.8 = (f32[4,128]{1,0:T(4,128)S(1)}, f32[4,128]{1,0:T(4,128)S(1)}, u32[]{:S(2)}, u32[]{:S(2)}) collective-permute-start(f32[4,128]{1,0:T(4,128)S(1)} %add.17), channel_id=1, source_target_pairs={{0,8},{4,12},{8,0},{12,4},{16,24},{20,28},{24,16},{28,20},{1,9},{5... | collective-permute-start | bytes 6152 | tf_op jit(solution)/shard_map/ppermute | solution.py:539
  64.5 3.8 %collective-permute-start.9 = (f32[4,128]{1,0:T(4,128)S(1)}, f32[4,128]{1,0:T(4,128)S(1)}, u32[]{:S(2)}, u32[]{:S(2)}) collective-permute-start(f32[4,128]{1,0:T(4,128)S(1)} %add.18), channel_id=1, source_target_pairs={{0,4},{4,0},{8,12},{12,8},{16,20},{20,16},{24,28},{28,24},{1,5},{5... | collective-permute-start | bytes 6152 | tf_op jit(solution)/shard_map/ppermute | solution.py:539

commit v2 on v1

--- a/solution.py
+++ b/solution.py
@@ -183,10 +183,10 @@
 
 
 def edge_kernel(
-    sums_in, b, ty, right, up, down, s_first_in, s_mid_in, s_last_in, w_last_in, back_in,
-    s_first, s_mid, s_last, w_last, back, sums, right_edges, w_up, w_down,
+    sums_in, near_sums, b, right, up, down, tx, ty, tz, st, s_first_in, s_mid_in, s_last_in, w_last_in,
+    s_first, s_mid, s_last, w_last, sums, image_ends, ends_sums, right_edges, w_up, w_down,
 ):
-    layers, rows, _ = b.shape
+    layers, rows, depth = b.shape
     at_b, at_ty, at_w, at_back, at_right, at_right_ty = up_places(layers)
     product = 0.0
     for layer in range(layers):
@@ -205,14 +205,73 @@
         w_up[layer : layer + 1, :] = up[at_w + layer : at_w + layer + 1, :] - low
         w_down[layer : layer + 1, :] = down[layers + layer : layers + layer + 1, :] - high
     sums[...] = sums_in[...] + as_tile([0.0, jnp.sum(product)])
-    back[rows : rows + 1, :] = up[at_back : at_back + 1, :]
-    back[rows + 1 : rows + 2, :] = down[2 * layers : 2 * layers + 1, :]
     low, high = edge_terms(
         up[at_right : at_right + 1, :], right[0:1, :], right[rows - 1 : rows, :], down[2 * layers + 1 :, :],
         up[at_right_ty : at_right_ty + 1, :], right[rows + SUB - 1 :, :],
     )
     right_edges[0:1, :] = low
     right_edges[1:2, :] = high
+    near = from_tile(near_sums[...], 2)
+    own, read, plain = high_layers(layers, s_mid, s_last, w_last)
+    terms = None
+    for place, start in enumerate((0, rows - SUB)):
+        values = read(start)
+        if place == 0:
+            after, carry = read(SUB), [jnp.zeros((SUB, depth), F32)] * len(own)
+        else:
+            after, carry = None, flux_from(start - SUB, own, read, 1, ty)
+        new, _ = chunk_sums(
+            start, values, after, carry, own, near, b, plain, tx, ty, tz, st, image_ends, place * SUB
+        )
+        terms = new if terms is None else [old + more for old, more in zip(terms, new)]
+    ends_sums[...] = as_tile([0.0] * 3 + [jnp.sum(term) for term in terms])
+
+
+def high_layers(layers, s_mid, s_last, w_last):
+    split = layers // 2
+
+    def read(start):
+        here = pl.ds(start, SUB)
+        return [s_mid[layer - 1, here, :] for layer in range(split - 1, layers - 1)] + [w_last[here, :]]
+
+    def plain(layer, here):
+        return s_last[here, :] if layer == layers - 1 else s_mid[layer - 1, here, :]
+
+    return list(range(split, layers)), read, plain
+
+
+def flux_from(start, own, read, skip, ty):
+    row = None
+    carry = []
+    for layer, value, after in zip(own, read(start)[skip:], read(start + SUB)[skip:]):
+        row = tile_ids(0, value.shape)
+        follow = jnp.where(row == SUB - 1, pltpu.roll(after, SUB - 1, 0), pltpu.roll(value, SUB - 1, 0))
+        carry.append(pltpu.roll(ty[layer, pl.ds(start, SUB), :] * (value - follow), 1, 0))
+    return carry
+
+
+def chunk_sums(start, values, after, carry, own, near, b, plain, tx, ty, tz, st, image, target, summed=None):
+    layers = b.shape[0]
+    here = pl.ds(start, SUB)
+    below = (values[0], tx[own[0] - 1, here, :]) if own[0] > 0 else None
+    above = values[-1] if own[-1] < layers - 1 else None
+    skip = 0 if below is None else 1
+    mine = values[skip : skip + len(own)]
+    results, carry = stencil(
+        mine, None if after is None else after[skip : skip + len(own)],
+        *[[array[layer, here, :] for layer in own] for array in (tx, ty, tz, st)], carry, below, above,
+    )
+    terms = None
+    for place, layer in enumerate(own):
+        w, s = mine[place], results[place]
+        image[place, pl.ds(target, SUB), :] = s
+        if summed is not None and layer not in summed:
+            continue
+        u = b[layer, here, :] - near * w
+        q = plain(layer, here) - near * s
+        new = [u * u, u * w, w * w, u * q, u * s + w * q, w * s]
+        terms = new if terms is None else [old + more for old, more in zip(terms, new)]
+    return terms, carry
 
 
 def mm(left, right):
@@ -271,12 +330,10 @@
     sums[...] = as_tile([jnp.sum(square)])
 
 
-def back_first_kernel(jump, right, b, ty, s_first, s_mid, w_last, puts, codes, proj_n, back, up, down):
-    back_kernel(jump, puts, codes, proj_n, back)
+def rows_kernel(right, b, ty, s_first, s_mid, w_last, back, up, down):
     layers, rows, _ = b.shape
     at_b, at_ty, at_w, at_back, at_right, at_right_ty = up_places(layers)
     end = pl.ds(rows - 1, 1)
-    back[rows:, :] = jnp.zeros((SUB, back.shape[1]), F32)
     for layer in range(layers):
         image = s_first if layer == 0 else w_last if layer == layers - 1 else s_mid.at[layer - 1]
         up[at_b + layer : at_b + layer + 1, :] = b[layer, end, :]
@@ -292,13 +349,15 @@
 
 
 def jump_second_kernel(
-    near_sums, w_last, jump, right, right_edges, back_before, picks, codes, proj_t, jump_next, sums, field
+    near_sums, w_last, jump, right_before, right, right_edges, back_before, up, down, picks, codes, proj_t,
+    jump_next, sums, missing, field,
 ):
     width = proj_t.shape[1] // 2
     rows, depth = right.shape
+    layers = (up.shape[0] - 3) // 3
     parts = [pl.ds(group * width, width) for group in range(depth // width)]
     near = from_tile(near_sums[...], 2)
-    field[...] = right[...] + back_before[:rows, :]
+    field[...] = right[...] + back_before[...]
     field[0:1, :] += right_edges[0:1, :]
     field[rows - 1 :, :] += right_edges[1:2, :]
     faces = stack_parts([field[:, part] for part in parts])
@@ -309,7 +368,28 @@
         close = jump[:, part] - near * later
         totals = [total + new for total, new in zip(totals, (close * close, close * later, later * later))]
     found = [jnp.sum(total) for total in totals]
-    sums[...] = as_tile([0.0] * 6 + [penalty * found[0], 2.0 * penalty * found[1], penalty * found[2]])
+    found = [penalty * found[0], 2.0 * penalty * found[1], penalty * found[2]]
+    _, _, _, at_back, _, at_right_ty = up_places(layers)
+    low = -up[at_right_ty : at_right_ty + 1, :] * up[at_back : at_back + 1, :]
+    high = jnp.where(at_last_block(), 0.0, -right_before[rows + SUB - 1 :, :] * down[2 * layers : 2 * layers + 1, :])
+    missing[0:1, :] = low
+    missing[1:2, :] = high
+    extra = [0.0] * 3
+    for place, s in ((0, low), (rows - 1, high)):
+        w = field[place : place + 1, :]
+        u = right_before[place : place + 1, :] - near * w
+        extra = [old + more for old, more in zip(extra, [-near * u * s, u * s - near * w * s, w * s])]
+    sums[...] = as_tile([0.0] * 6 + [old + jnp.sum(more) for old, more in zip(found, extra)])
+
+
+def back_second_kernel(jump_next, missing, puts, codes, proj_n, back):
+    rows = jump_next.shape[0]
+    back_kernel(jump_next, puts, codes, proj_n, back)
+    back[rows : rows + 2, :] = missing[...]
+
+
+def hold_kernel(later, back_in, back):
+    back[back.shape[0] - SUB + 2 :, :] = jnp.zeros((SUB - 2, back.shape[1]), F32)
 
 
 def back_kernel(jump_next, puts, codes, proj_n, back):
@@ -322,88 +402,119 @@
         back[:rows, part] = put_back(group, backs, puts, rows)
 
 
-def stencil_sums(read, own, near, b, plain, tx, ty, tz, st, image, total):
+def stencil_sums(read, own, near, b, plain, tx, ty, tz, st, image, total, inner, summed=None):
     layers, rows, depth = b.shape
-    first, last = own[0], own[-1]
     total[...] = jnp.zeros_like(total)
-
-    def chunk(start, values, after, carry):
-        here = pl.ds(start, SUB)
-        below = (values[0], tx[first - 1, here, :]) if first > 0 else None
-        above = values[-1] if last < layers - 1 else None
-        skip = 0 if below is None else 1
-        mine = values[skip : skip + len(own)]
-        results, carry = stencil(
-            mine, None if after is None else after[skip : skip + len(own)],
-            *[[array[layer, here, :] for layer in own] for array in (tx, ty, tz, st)], carry, below, above,
-        )
-        terms = None
-        for place, layer in enumerate(own):
-            w, s = mine[place], results[place]
-            image[place, here, :] = s
-            u = b[layer, here, :] - near * w
-            q = plain(layer, here) - near * s
-            new = [u * u, u * w, w * w, u * q, u * s + w * q, w * s]
-            terms = new if terms is None else [old + more for old, more in zip(terms, new)]
-        return terms, carry
+    skip = 1 if own[0] > 0 else 0
 
     def several(start, count, carry, at_end=False):
-        values = [read(pl.multiple_of(start + SUB * place, SUB)) for place in range(count)]
-        values.append(None if at_end else read(pl.multiple_of(start + SUB * count, SUB)))
+        starts = [pl.multiple_of(start + SUB * place, SUB) for place in range(count + 1)]
+        values = [read(place) for place in starts[:-1]] + [None if at_end else read(starts[-1])]
         terms = None
         for place in range(count):
-            new, carry = chunk(pl.multiple_of(start + SUB * place, SUB), values[place], values[place + 1], carry)
+            new, carry = chunk_sums(
+                starts[place], values[place], values[place + 1], carry, own, near, b, plain, tx, ty, tz, st, image,
+                starts[place], summed,
+            )
             terms = new if terms is None else [old + more for old, more in zip(terms, new)]
         for place, term in enumerate(terms):
             total[place] += term
         return carry
 
     group = 2
+    if inner:
+        begin, count, carry = SUB, (rows // SUB - 2) // group, flux_from(0, own, read, skip, ty)
+    else:
+        begin, count, carry = 0, rows // (group * SUB) - 1, [jnp.zeros((SUB, depth), F32)] * len(own)
     carry = lax.fori_loop(
-        0, rows // (group * SUB) - 1,
-        lambda index, carry: tuple(several(pl.multiple_of(index * group * SUB, SUB), group, list(carry))),
-        (jnp.zeros((SUB, depth), F32),) * len(own),
+        0, count,
+        lambda index, carry: tuple(
+            several(pl.multiple_of(begin + index * group * SUB, SUB), group, list(carry))
+        ),
+        tuple(carry),
     )
-    several(rows - group * SUB, group, list(carry), True)
+    if not inner:
+        several(rows - group * SUB, group, list(carry), True)
     return [jnp.sum(total[place]) for place in range(total.shape[0])]
 
 
-def second_high_kernel(first_sums, jump_sums, b, s_mid, s_last, w_last, tx, ty, tz, st, image, sums, total):
-    layers = b.shape[0]
-    split = layers // 2
+def second_high_kernel(later, first_sums, jump_sums, b, s_mid, s_last, w_last, tx, ty, tz, st, image, sums, total):
     norm = from_tile(first_sums[...], 0)
     energy = from_tile(first_sums[...], 1) + penalty * from_tile(jump_sums[...], 0)
     safe = energy > 0.01 * norm
     ratio = jnp.full((SUB, LANES), norm, F32) / jnp.full((SUB, LANES), jnp.where(safe, energy, 1.0), F32)
     near = jnp.where(safe, jnp.max(ratio), 0.0)
+    own, read, plain = high_layers(b.shape[0], s_mid, s_last, w_last)
+    found = stencil_sums(read, own, near, b, plain, tx, ty, tz, st, image, total, True)
+    sums[...] = as_tile([0.0, 0.0, near] + found)
+
+
+def second_low_kernel(high_sums, b, s_first, s_mid, tx, ty, tz, st, image, sums, total):
+    layers = b.shape[0]
+    split = layers // 2
+    near = from_tile(high_sums[...], 2)
 
     def read(start):
         here = pl.ds(start, SUB)
-        return [s_mid[layer - 1, here, :] for layer in range(split - 1, layers - 1)] + [w_last[here, :]]
+        return [s_first[here, :]] + [s_mid[layer - 1, here, :] for layer in range(1, split + 1)]
 
     def plain(layer, here):
-        return s_last[here, :] if layer == layers - 1 else s_mid[layer - 1, here, :]
-
-    found = stencil_sums(read, list(range(split, layers)), near, b, plain, tx, ty, tz, st, image, total)
-    sums[...] = as_tile([norm, energy, near] + found)
-
-
-def second_low_kernel(
-    high_sums, jump_sums, b, s_first, s_mid, w_last, recv, w_up, w_down, up, tx, ty, tz, st,
-    image, edge_high, table, total,
+        return s_mid[layer - 1, here, :]
+
+    own = list(range(split))
+    found = stencil_sums(read, own, near, b, plain, tx, ty, tz, st, image, total, False, own[1:])
+    sums[...] = high_sums[...] + as_tile([0.0] * 3 + found)
+
+
+def second_added_kernel(
+    first_sums, jump_sums, low_sums, ends_sums, second_sums, b, s_first, s_mid, w_last, recv,
+    w_up, w_down, up, tx, ty, tz, st, image_in, image, edge_high, table, total,
 ):
     layers, rows, depth = b.shape
     split = layers // 2
-    near = from_tile(high_sums[...], 2)
-
-    def read(start):
-        here = pl.ds(start, SUB)
-        return [s_first[here, :] + recv[here, :]] + [s_mid[layer - 1, here, :] for layer in range(1, split + 1)]
-
-    def plain(layer, here):
-        return s_first[here, :] if layer == 0 else s_mid[layer - 1, here, :]
-
-    found = stencil_sums(read, list(range(split)), near, b, plain, tx, ty, tz, st, image, total)
+    near = from_tile(low_sums[...], 2)
+    total[...] = jnp.zeros_like(total)
+    first, second = 0, 1
+
+    def several(start, count, carry, at_end=False):
+        starts = [pl.multiple_of(start + SUB * place, SUB) for place in range(count + 1)]
+        added = [recv[pl.ds(place, SUB), :] for place in starts[:-1]]
+        added.append(None if at_end else recv[pl.ds(starts[-1], SUB), :])
+        terms = None
+        for place in range(count):
+            here = pl.ds(starts[place], SUB)
+            e, t_x = added[place], tx[first, here, :]
+            (s,), carry = stencil(
+                [e], None if added[place + 1] is None else [added[place + 1]], [t_x], [ty[first, here, :]],
+                [tz[first, here, :]], [st[first, here, :] + t_x], carry,
+            )
+            s = image_in[first, here, :] + s
+            image[first, here, :] = s
+            plain = s_first[here, :]
+            w = plain + e
+            u = b[first, here, :] - near * w
+            q = plain - near * s
+            new = [u * u, u * w, w * w, u * q, u * s + w * q, w * s]
+            added_s = -t_x * e
+            image[second, here, :] = image_in[second, here, :] + added_s
+            w = s_mid[second - 1, here, :]
+            u = b[second, here, :] - near * w
+            new[3] = new[3] - near * u * added_s
+            new[4] = new[4] + (u - near * w) * added_s
+            new[5] = new[5] + w * added_s
+            terms = new if terms is None else [old + more for old, more in zip(terms, new)]
+        for place, term in enumerate(terms):
+            total[place] += term
+        return carry
+
+    group = 4
+    carry = lax.fori_loop(
+        0, rows // (group * SUB) - 1,
+        lambda index, carry: several(pl.multiple_of(index * group * SUB, SUB), group, [carry])[0],
+        jnp.zeros((SUB, depth), F32),
+    )
+    several(rows - group * SUB, group, [carry], True)
+    found = [jnp.sum(total[place]) for place in range(total.shape[0])]
 
     def row(layer, place):
         here = pl.ds(place, 1)
@@ -411,26 +522,26 @@
             return s_first[here, :] + recv[here, :]
         return w_last[here, :] if layer == layers - 1 else s_mid[layer - 1, here, :]
 
-    extra = [0.0] * 3
+    extra = [jnp.zeros((1, depth), F32)] * 3
     for layer in range(layers):
-        before, beyond = w_up[layer : layer + 1, :], w_down[layer : layer + 1, :]
-        if layer == 0:
-            before, beyond = before + recv[rows : rows + 1, :], beyond + recv[rows + 1 : rows + 2, :]
         ends = row(layer, 0), row(layer, rows - 1)
         added = edge_terms(
-            before, *ends, beyond, up[layers + layer : layers + layer + 1, :], ty[layer, rows - 1 :, :]
+            w_up[layer : layer + 1, :], *ends, w_down[layer : layer + 1, :],
+            up[layers + layer : layers + layer + 1, :], ty[layer, rows - 1 :, :],
         )
         for side, (place, w, s) in enumerate(zip((0, rows - 1), ends, added)):
             u = b[layer, place : place + 1, :] - near * w
-            new = [-near * u * s, u * s - near * w * s, w * s]
-            extra = [old + more for old, more in zip(extra, new)]
+            extra = [old + more for old, more in zip(extra, [-near * u * s, u * s - near * w * s, w * s])]
             if layer < split:
                 image[layer, place : place + 1, :] += s
             else:
                 spot = side * (layers - split) + layer - split
                 edge_high[spot : spot + 1, :] = s
-    extra = [jnp.sum(value) for value in extra]
-    sums = high_sums[...] + jump_sums[...] + as_tile([0.0] * 3 + found) + as_tile([0.0] * 6 + extra)
+    found[3:] = [old + jnp.sum(more) for old, more in zip(found[3:], extra)]
+    norm = from_tile(first_sums[...], 0)
+    energy = from_tile(first_sums[...], 1) + penalty * from_tile(jump_sums[...], 0)
+    sums = low_sums[...] + ends_sums[...] + second_sums[...]
+    sums = sums + as_tile([norm, energy, 0.0] + found)
     mine = lax.axis_index("sub") * lax.axis_size("blk") + lax.axis_index("blk")
     device = tile_ids(0, table.shape) * (LANES // FIELDS) + lax.div(tile_ids(1, table.shape), FIELDS)
     field = lax.rem(tile_ids(1, table.shape), FIELDS)
@@ -441,7 +552,7 @@
 
 
 def final_kernel(
-    tables, b, s_first, s_mid, w_last, recv, image_low, image_high, edge_high, jump_next, recv_next, solution_hbm, residual_hbm,
+    tables, b, s_first, s_mid, w_last, recv, image_low, image_high, image_ends, edge_high, jump_next, recv_next, solution_hbm, residual_hbm,
     solution, residual, sems,
 ):
     layers, rows, depth = b.shape
@@ -473,12 +584,18 @@
         return pltpu.make_async_copy(source.at[:, part, :], target.at[:, part, :], sems.at[which, step])
 
     for step in range(rows // ROWS):
-
-        def one(index, done):
-            here = pl.ds(pl.multiple_of(step * ROWS + index * SUB, SUB), SUB)
+        for start in range(step * ROWS, (step + 1) * ROWS, SUB):
+            here = pl.ds(start, SUB)
             for layer in range(layers):
                 v = b[layer, here, :]
-                s = image_low[layer, here, :] if layer < split else image_high[layer - split, here, :]
+                if layer < split:
+                    s = image_low[layer, here, :]
+                elif start == 0:
+                    s = image_ends[layer - split, :SUB, :]
+                elif start == rows - SUB:
+                    s = image_ends[layer - split, SUB:, :]
+                else:
+                    s = image_high[layer - split, here, :]
                 if layer == 0:
                     w = s_first[here, :] + recv[here, :]
                     s = s + recv_next[here, :]
@@ -489,12 +606,10 @@
                     s = s + penalty * jump_next[here, :]
                 solution[layer, here, :] = c0 * v - c1 * w
                 residual[layer, here, :] = v - c2 * w + c1 * s
-            return done
-
-        lax.fori_loop(0, ROWS // SUB, one, 0, unroll=True)
         for side, last_step in enumerate((0, rows // ROWS - 1)):
             if step == last_step:
                 place = side * (rows - 1)
+                residual[0, place : place + 1, :] += c1[0:1, :] * recv_next[rows + side : rows + side + 1, :]
                 for layer in range(split, layers):
                     spot = side * (layers - split) + layer - split
                     residual[layer, place : place + 1, :] += c1[0:1, :] * edge_high[spot : spot + 1, :]
@@ -532,12 +647,19 @@
 
 
 def gather_rows(table):
-    for axis in ("blk", "sub"):
-        size = lax.axis_size(axis)
-        reach = 1 if axis == "blk" else size // 2
-        while 0 < reach < size:
-            table = table + lax.ppermute(table, axis, [(i, i ^ reach) for i in range(size)])
-            reach = reach * 2 if axis == "blk" else reach // 2
+    subs, blks = lax.axis_size("sub"), lax.axis_size("blk")
+    steps = [(0, 1)]
+    reach = 2
+    while reach < blks:
+        steps.append((0, reach + 1))
+        reach *= 2
+    reach = subs // 2
+    while reach > 0:
+        steps.append((reach, 1))
+        reach //= 2
+    for by_sub, by_blk in steps:
+        pairs = [(s * blks + t, (s ^ by_sub) * blks + (t ^ by_blk)) for s in range(subs) for t in range(blks)]
+        table = table + lax.ppermute(table, ("sub", "blk"), pairs)
     return table
 
 
@@ -591,91 +713,134 @@
         cost_estimate=mortar_cost,
         name="jump_first",
     )(*near_core(b, face_right, s_last, picks, codes, proj_t))
-    back, up_out, down_out = pl.pallas_call(
-        back_first_kernel,
-        in_specs=[VMEM] * 10,
-        out_specs=[VMEM] * 3,
-        out_shape=[held(rows + SUB, depth), held(3 * layers + 3, depth), held(2 * layers + 2, depth)],
+    (back,) = pl.pallas_call(
+        back_kernel,
+        in_specs=[VMEM] * 4,
+        out_specs=[VMEM],
+        out_shape=[held(rows, depth)],
         compiler_params=params(16),
         cost_estimate=mortar_cost,
         name="back_first",
-    )(*near_core(jump, face_right, b, ty, s_first, s_mid, w_last, puts, codes, proj_n))
-    up = shifted(up_out, "blk", 1)
-    down = shifted(down_out, "blk", -1)
-    s_first, s_mid, s_last, w_last, back, first_sums, right_edges, w_up, w_down = pl.pallas_call(
-        edge_kernel,
-        in_specs=[VMEM] * 11,
-        out_specs=[VMEM] * 9,
-        out_shape=[held(rows, depth), held(layers - 2, rows, depth), held(rows, depth), held(rows, depth)]
-        + [held(rows + SUB, depth), held(SUB, LANES), held(2, depth), held(layers, depth), held(layers, depth)],
-        input_output_aliases={6: 0, 7: 1, 8: 2, 9: 3, 10: 4},
-        compiler_params=params(2),
-        cost_estimate=cost(32 * depth, 64 * depth),
-        name="edges_first",
-    )(*near_core(first_sums, b, ty, face_right, up, down, s_first, s_mid, s_last, w_last, back))
+    )(*near_core(jump, puts, codes, proj_n))
     recv = shifted(back, "sub", 1)
 
     split = layers // 2
     image_high, high_sums = pl.pallas_call(
         second_high_kernel,
-        in_specs=[VMEM] * 10,
+        in_specs=[VMEM] * 11,
         out_specs=[VMEM] * 2,
         out_shape=[held(layers - split, rows, depth), held(SUB, LANES)],
         scratch_shapes=[pltpu.VMEM((6, SUB, depth), F32)],
         compiler_params=params(8),
         cost_estimate=cost(20 * cells, 15 * cells),
         name="stencil_second_high",
-    )(*near_core(first_sums, jump_sums, b, s_mid, s_last, w_last, tx, ty, tz, st))
-
-    jump_next, second_sums = pl.pallas_call(
+    )(*near_core(back, first_sums, jump_sums, b, s_mid, s_last, w_last, tx, ty, tz, st))
+    up_out, down_out = pl.pallas_call(
+        rows_kernel,
+        in_specs=[VMEM] * 7,
+        out_specs=[VMEM] * 2,
+        out_shape=[held(3 * layers + 3, depth), held(2 * layers + 2, depth)],
+        compiler_params=params(2),
+        cost_estimate=cost(0, 64 * depth),
+        name="rows",
+    )(*near_core(face_right, b, ty, s_first, s_mid, w_last, back))
+    up = shifted(up_out, "blk", 1)
+    down = shifted(down_out, "blk", -1)
+    s_first, s_mid, s_last, w_last, edge_sums, image_ends, ends_sums, right_edges, w_up, w_down = pl.pallas_call(
+        edge_kernel,
+        in_specs=[VMEM] * 14,
+        out_specs=[VMEM] * 10,
+        out_shape=[held(rows, depth), held(layers - 2, rows, depth), held(rows, depth), held(rows, depth)]
+        + [held(SUB, LANES), held(layers - split, 2 * SUB, depth), held(SUB, LANES)]
+        + [held(2, depth), held(layers, depth), held(layers, depth)],
+        input_output_aliases={10: 0, 11: 1, 12: 2, 13: 3},
+        compiler_params=params(4),
+        cost_estimate=cost(320 * depth, 640 * depth),
+        name="edges_first",
+    )(
+        *near_core(
+            first_sums, high_sums, b, face_right, up, down, tx, ty, tz, st, s_first, s_mid, s_last, w_last,
+        )
+    )
+
+    image_low, low_sums = pl.pallas_call(
+        second_low_kernel,
+        in_specs=[VMEM] * 8,
+        out_specs=[VMEM] * 2,
+        out_shape=[held(split, rows, depth), held(SUB, LANES)],
+        scratch_shapes=[pltpu.VMEM((6, SUB, depth), F32)],
+        compiler_params=params(8),
+        cost_estimate=cost(20 * cells, 15 * cells),
+        name="stencil_second_low",
+    )(*near_core(high_sums, b, s_first, s_mid, tx, ty, tz, st))
+
+    jump_next, second_sums, missing = pl.pallas_call(
         jump_second_kernel,
-        in_specs=[VMEM] * 9,
-        out_specs=[VMEM] * 2,
-        out_shape=[held(rows, depth), held(SUB, LANES)],
+        in_specs=[VMEM] * 12,
+        out_specs=[VMEM] * 3,
+        out_shape=[held(rows, depth), held(SUB, LANES), held(2, depth)],
         scratch_shapes=[pltpu.VMEM((rows, depth), F32)],
         compiler_params=params(16),
         cost_estimate=mortar_cost,
         name="jump_second",
-    )(*near_core(high_sums, w_last, jump, face_right_next, right_edges, back, picks, codes, proj_t))
+    )(
+        *near_core(
+            low_sums, w_last, jump, face_right, face_right_next, right_edges, back, up, down, picks, codes, proj_t,
+        )
+    )
+    (back_next,) = pl.pallas_call(
+        back_second_kernel,
+        in_specs=[VMEM] * 5,
+        out_specs=[VMEM],
+        out_shape=[held(rows + SUB, depth)],
+        compiler_params=params(16),
+        cost_estimate=mortar_cost,
+        name="back_second",
+    )(*near_core(jump_next, missing, puts, codes, proj_n))
+
+    (back_next,) = pl.pallas_call(
+        hold_kernel,
+        in_specs=[VMEM] * 2,
+        out_specs=[VMEM],
+        out_shape=[held(rows + SUB, depth)],
+        input_output_aliases={1: 0},
+        compiler_params=params(2),
+        cost_estimate=cost(0, 8 * depth),
+        name="hold",
+    )(*near_core(recv, back_next))
+    recv_next = shifted(back_next, "sub", 1)
 
     count = subs * blks
     image_low, edge_high, table = pl.pallas_call(
-        second_low_kernel,
-        in_specs=[VMEM] * 14,
+        second_added_kernel,
+        in_specs=[VMEM] * 18,
         out_specs=[VMEM] * 3,
-        out_shape=[held(split, rows, depth), held(2 * (layers - split), depth), held(-(-count * FIELDS // LANES), LANES)],
+        out_shape=[
+            held(split, rows, depth), held(2 * (layers - split), depth), held(-(-count * FIELDS // LANES), LANES),
+        ],
+        input_output_aliases={17: 0},
         scratch_shapes=[pltpu.VMEM((6, SUB, depth), F32)],
         compiler_params=params(8),
         cost_estimate=cost(20 * cells, 15 * cells),
-        name="stencil_second_low",
+        name="stencil_second_added",
     )(
         *near_core(
-            high_sums, second_sums, b, s_first, s_mid, w_last, recv, w_up, w_down, up, tx, ty, tz, st,
+            edge_sums, jump_sums, low_sums, ends_sums, second_sums, b, s_first, s_mid, w_last, recv,
+            w_up, w_down, up, tx, ty, tz, st, image_low,
         )
     )
     tables = gather_rows(table)
 
-    (back_next,) = pl.pallas_call(
-        back_kernel,
-        in_specs=[VMEM] * 4,
-        out_specs=[VMEM],
-        out_shape=[held(rows, depth)],
-        compiler_params=params(16),
-        cost_estimate=mortar_cost,
-        name="back_second",
-    )(*near_core(jump_next, puts, codes, proj_n))
-    recv_next = shifted(back_next, "sub", 1)
-
     return pl.pallas_call(
         final_kernel,
-        in_specs=[VMEM] * 11,
+        in_specs=[VMEM] * 12,
         out_specs=[HBM] * 2,
         out_shape=[jax.ShapeDtypeStruct((layers, rows, depth), F32)] * 2,
         scratch_shapes=[pltpu.VMEM((layers, rows, depth), F32)] * 2 + [pltpu.SemaphoreType.DMA((2, steps))],
         compiler_params=params(8),
         cost_estimate=cost(8 * cells, 22 * cells),
         name="final_update",
-    )(*near_core(tables, b, s_first, s_mid, w_last, recv, image_low, image_high, edge_high, jump_next, recv_next))
+    )(*near_core(tables, b, s_first, s_mid, w_last, recv, image_low, image_high, image_ends, edge_high, jump_next, recv_next))
 
 
 def solution(mesh):

time: 71.1 us -> 67.2 us (0.945)
  waiting for transfers between devices: 23.9 us -> 17.6 us
  Pallas kernels: 21.8 us -> 23.7 us
    ppermute x6, waiting for transfers between devices: 15.3 us -> 10.8 us  [shifted(): lax.ppermute(array, axis, [(i, i + by) for i in range(size) if 0 <= i + b...]
    ppermute x6, starting transfers between devices: 12.1 us -> 14.5 us  [shifted(): lax.ppermute(array, axis, [(i, i + by) for i in range(size) if 0 <= i + b...]
    ppermute x5, starting transfers between devices: 11.6 us -> 9.68 us  [gather_rows(): table = table + lax.ppermute(table, ('sub', 'blk'), pairs)]
    pallas_call x6 -> x9, Pallas kernels: 12.3 us -> 14.2 us  [the longest x1 3.17 us: body(): pl.pallas_call(second_high_kernel, in_specs=[VMEM] * 11, out_specs=[VMEM]...]
    ppermute x5, waiting for transfers between devices: 8.54 us -> 6.78 us  [gather_rows(): table = table + lax.ppermute(table, ('sub', 'blk'), pairs)]
  transfers between devices with their start and end apart: 11 -> 11, of which waited for: 8 -> 8; matrix products, arithmetic and copies ran while one was open for 0% -> 0% of each run, Pallas kernels for 26% -> 30%
where the time goes in v2:
time: 67.2 us; the launch traced here: 66.9 us
  starting transfers between devices  24.1 us (36%)
  Pallas kernels  23.7 us (35%)
  waiting for transfers between devices  17.6 us (26%)
  between operations  1.48 us (2%)
    ppermute x6, starting transfers between devices, shifted(): lax.ppermute(array, axis, [(i, i + by) for i in range(size) if 0 <= i + b...  14.5 us
    ppermute x6, waiting for transfers between devices, shifted(): lax.ppermute(array, axis, [(i, i + by) for i in range(size) if 0 <= i + b...  10.8 us
    ppermute x5, starting transfers between devices, gather_rows(): table = table + lax.ppermute(table, ('sub', 'blk'), pairs)  9.68 us
    ppermute x5, waiting for transfers between devices, gather_rows(): table = table + lax.ppermute(table, ('sub', 'blk'), pairs)  6.78 us
    pallas_call x1, Pallas kernels, body(): pl.pallas_call(first_kernel, in_specs=[SMEM] + [VMEM] * 3 + [HBM] * 5, ou...  5.35 us
    pallas_call x1, Pallas kernels, body(): pl.pallas_call(second_high_kernel, in_specs=[VMEM] * 11, out_specs=[VMEM]...  3.17 us
    pallas_call x1, Pallas kernels, body(): pl.pallas_call(second_low_kernel, in_specs=[VMEM] * 8, out_specs=[VMEM] *...  2.99 us
    pallas_call x1, Pallas kernels, body(): pl.pallas_call(final_kernel, in_specs=[VMEM] * 12, out_specs=[HBM] * 2, o...  2.47 us
  transfers between devices with their start and end apart: 11, of which 8 were waited for; matrix products, arithmetic and copies ran while one was open for 0% of the time, Pallas kernels for 30%

profile of v2, /device:TPU:0, one launch (start us, length us, event | category | flops | bytes accessed | tf_op | source)
XLA Modules:
  0.0 66.9 jit_solution(12885589330449645534)
XLA Ops:
  0.6 0.0 copy-start.1
  0.6 0.0 copy-start.2
  0.7 0.0 copy-start
  0.7 1.1 %pack.1 = f32[264,512]{1,0:T(8,128)S(1)} custom-call(f32[4,256,512]{2,1,0:T(8,128)} %b_hbm.3, f32[4,256,512]{2,1,0:T(8,128)} %ty_hbm.3), custom_call_target="tpu_custom_call" | custom-call | bytes 524288 | tf_op jit(solution)/shard_map/pack/pallas_call | solution.py:674
  1.8 1.3 %collective-permute-start = (f32[264,512]{1,0:T(8,128)S(1)}, f32[264,512]{1,0:T(8,128)S(1)}, u32[]{:S(2)}, u32[]{:S(2)}) collective-permute-start(f32[264,512]{1,0:T(8,128)S(1)} %pack.1), channel_id=1, source_target_pairs={{4,0},{8,4},{12,8},{16,12},{20,16},{24,20},{28,24},{5,1},{9,5},{13... | collective-permute-start | bytes 1622024 | tf_op jit(solution)/shard_map/ppermute | solution.py:646
  3.7 0.0 copy-done.1
  3.7 0.0 copy-done.2
  3.7 0.0 copy-done
  3.8 5.3 %stencil_first.1 = (f32[4,256,512]{2,1,0:T(8,128)S(1)}, f32[4,256,512]{2,1,0:T(8,128)S(1)}, f32[4,256,512]{2,1,0:T(8,128)S(1)}, f32[4,256,512]{2,1,0:T(8,128)S(1...) custom-call(s32[1,1]{1,0:T(1,128)S(6)} %copy.23.count, ...), custom_call_target="tpu_custom_call" | custom-call | flops 10485760 | bytes 12582912 | tf_op jit(solution)/shard_map/stencil_first/pallas_call | solution.py:686
  9.1 1.3 %collective-permute-start.3 = (f32[256,512]{1,0:T(8,128)S(1)}, f32[256,512]{1,0:T(8,128)S(1)}, u32[]{:S(2)}, u32[]{:S(2)}) collective-permute-start(f32[256,512]{1,0:T(8,128)S(1)} %get-tuple-element.67), channel_id=1, source_target_pairs={{4,0},{8,4},{12,8},{16,12},{20,16},{24,20},{28,24},{5,1},{9,5},{13... | collective-permute-start | bytes 1572872 | tf_op jit(solution)/shard_map/ppermute | solution.py:646
  10.4 9.3 %collective-permute-done.right.right_before = f32[264,512]{1,0:T(8,128)S(1)} collective-permute-done((f32[264,512]{1,0:T(8,128)S(1)}, f32[264,512]{1,0:T(8,128)S(1)}, u32[]{:S(2)}, u32[]{:S(2)}) %collective-permute-start) | collective-permute-done | bytes 540704 | tf_op jit(solution)/shard_map/ppermute | solution.py:646
  19.7 1.8 %jump_first.1 = (f32[256,512]{1,0:T(8,128)S(1)}, f32[256,512]{1,0:T(8,128)S(1)}, f32[8,128]{1,0:T(8,128)S(1)}) custom-call(f32[4,256,512]{2,1,0:T(8,128)S(1)} %get-tuple-element.42.b, f32[264,512]{1,0:T(8,128)S(1)} %collective-permute-done.right.right_before, f32[256,512]{1,0:T(8,128)S(1)} %get-tuple-element.43.s_last.s_last_in, ...), custom_call_target="tpu_custom_call" | custom-call | flops 939524096 | bytes 1835008 | tf_op jit(solution)/shard_map/jump_first/pallas_call | solution.py:707
  21.5 1.3 %back_first.1.later.back.back_before = f32[256,512]{1,0:T(8,128)S(1)} custom-call(f32[256,512]{1,0:T(8,128)S(1)} %get-tuple-element.47.jump_next.jump, bf16[1024,1024]{1,0:T(8,128)(2,1)S(1)} %get-tuple-element.48.puts, s32[1024,128]{1,0:T(8,128)S(1)} %get-tuple-element.45.codes, bf16[512,256]{1,0:T(8,128)(2,1)S(1)} %get-tuple-element.49.proj_n), custom_call_target="tpu_custom_call" | custom-call | flops 939524096 | bytes 1835008 | tf_op jit(solution)/shard_map/back_first/pallas_call | solution.py:716
  22.8 4.9 %collective-permute-start.4 = (f32[256,512]{1,0:T(8,128)S(1)}, f32[256,512]{1,0:T(8,128)S(1)}, u32[]{:S(2)}, u32[]{:S(2)}) collective-permute-start(f32[256,512]{1,0:T(8,128)S(1)} %back_first.1.later.back.back_before), channel_id=1, source_target_pairs={{0,4},{4,8},{8,12},{12,16},{16,20},{20,24},{24,28},{1,5},{5,9},{9,... | collective-permute-start | bytes 1572872 | tf_op jit(solution)/shard_map/ppermute | solution.py:646
  27.7 1.3 %collective-permute-start.1 = (f32[15,512]{1,0:T(8,128)S(1)}, f32[15,512]{1,0:T(8,128)S(1)}, u32[]{:S(2)}, u32[]{:S(2)}) collective-permute-start(f32[15,512]{1,0:T(8,128)S(1)} %get-tuple-element.59), channel_id=1, source_target_pairs={{0,1},{1,2},{2,3},{4,5},{5,6},{6,7},{8,9},{9,10},{10,11},{12,13},{... | collective-permute-start | bytes 92168 | tf_op jit(solution)/shard_map/ppermute | solution.py:646
  29.0 1.3 %collective-permute-start.2 = (f32[10,512]{1,0:T(8,128)S(1)}, f32[10,512]{1,0:T(8,128)S(1)}, u32[]{:S(2)}, u32[]{:S(2)}) collective-permute-start(f32[10,512]{1,0:T(8,128)S(1)} %get-tuple-element.60), channel_id=1, source_target_pairs={{1,0},{2,1},{3,2},{5,4},{6,5},{7,6},{9,8},{10,9},{11,10},{13,12},{... | collective-permute-start | bytes 61448 | tf_op jit(solution)/shard_map/ppermute | solution.py:646
  30.3 3.2 %stencil_second_high.1 = (f32[2,256,512]{2,1,0:T(8,128)S(1)}, f32[8,128]{1,0:T(8,128)S(1)}) custom-call(f32[256,512]{1,0:T(8,128)S(1)} %back_first.1.later.back.back_before, f32[8,128]{1,0:T(8,128)S(1)} %get-tuple-element.41.first_sums.sums_in, f32[8,128]{1,0:T(8,128)S(1)} %get-tuple-element.50.jump_sums, f32[4,256,512]{2,1,0:T(8,128)S(1)} %get-tuple-element.42.b, ...), custom_call_target="tpu_custom_call" | custom-call | flops 10485760 | bytes 7864320 | tf_op jit(solution)/shard_map/stencil_second_high/pallas_call | solution.py:728
  33.5 0.4 collective-permute-done.2.down
  33.8 0.0 collective-permute-done.1.up
  33.8 0.3 edges_first.1
  34.2 3.0 %stencil_second_low.1 = (f32[2,256,512]{2,1,0:T(8,128)S(1)}, f32[8,128]{1,0:T(8,128)S(1)}) custom-call(f32[8,128]{1,0:T(8,128)S(1)} %get-tuple-element.57.near_sums.high_sums, f32[4,256,512]{2,1,0:T(8,128)S(1)} %get-tuple-element.42.b, f32[256,512]{1,0:T(8,128)S(1)} %get-tuple-element.62.s_first, f32[2,256,512]{2,1,0:T(8,128)S(1)} %get-tuple-element.63.s_mid, ...), custom_call_target="tpu_custom_call" | custom-call | flops 10485760 | bytes 7864320 | tf_op jit(solution)/shard_map/stencil_second_low/pallas_call | solution.py:766
  37.2 0.0 collective-permute-done.3.right
  37.2 1.9 %jump_second.1 = (f32[256,512]{1,0:T(8,128)S(1)}, f32[8,128]{1,0:T(8,128)S(1)}, f32[2,512]{1,0:T(2,128)S(1)}) custom-call(f32[8,128]{1,0:T(8,128)S(1)} %get-tuple-element.64.near_sums.low_sums, f32[256,512]{1,0:T(8,128)S(1)} %get-tuple-element.66.w_last, f32[256,512]{1,0:T(8,128)S(1)} %get-tuple-element.47.jump_next.jump, ...), custom_call_target="tpu_custom_call" | custom-call | flops 939524096 | bytes 1835008 | tf_op jit(solution)/shard_map/jump_second/pallas_call | solution.py:777
  39.1 1.3 %back_second.1.back_in = f32[264,512]{1,0:T(8,128)S(1)} custom-call(f32[256,512]{1,0:T(8,128)S(1)} %get-tuple-element.78.jump_next, f32[2,512]{1,0:T(2,128)S(1)} %get-tuple-element.79.missing, bf16[1024,1024]{1,0:T(8,128)(2,1)S(1)} %get-tuple-element.48.puts, s32[1024,128]{1,0:T(8,128)S(1)} %get-tuple-element.45.codes, ...), custom_call_target="tpu_custom_call" | custom-call | flops 939524096 | bytes 1835008 | tf_op jit(solution)/shard_map/back_second/pallas_call | solution.py:791
  40.4 1.1 %collective-permute-done.4.recv.later = f32[256,512]{1,0:T(8,128)S(1)} collective-permute-done((f32[256,512]{1,0:T(8,128)S(1)}, f32[256,512]{1,0:T(8,128)S(1)}, u32[]{:S(2)}, u32[]{:S(2)}) %collective-permute-start.4) | collective-permute-done | bytes 524320 | tf_op jit(solution)/shard_map/ppermute | solution.py:646
  41.5 4.4 %collective-permute-start.10 = (f32[264,512]{1,0:T(8,128)S(1)}, f32[264,512]{1,0:T(8,128)S(1)}, u32[]{:S(2)}, u32[]{:S(2)}) collective-permute-start(f32[264,512]{1,0:T(8,128)S(1)} %hold.1), channel_id=1, source_target_pairs={{0,4},{4,8},{8,12},{12,16},{16,20},{20,24},{24,28},{1,5},{5,9},{9,... | collective-permute-start | bytes 1622024 | tf_op jit(solution)/shard_map/ppermute | solution.py:646
  45.9 2.0 %stencil_second_added.1 = (f32[2,256,512]{2,1,0:T(8,128)S(1)}, f32[4,512]{1,0:T(4,128)S(1)}, f32[4,128]{1,0:T(4,128)S(1)}) custom-call(f32[8,128]{1,0:T(8,128)S(1)} %get-tuple-element.61.first_sums, f32[8,128]{1,0:T(8,128)S(1)} %get-tuple-element.50.jump_sums, f32[8,128]{1,0:T(8,128)S(1)} %get-tuple-element.64.near_sums.low_sums, ...), custom_call_target="tpu_custom_call", output_to_operand_aliasing={{0}: (17, {})} | custom-call | flops 10485760 | bytes 7864320 | tf_op jit(solution)/shard_map/stencil_second_added/pallas_call | solution.py:814
  48.0 0.1 collective-permute-start.5
  48.1 1.1 %collective-permute-done.5 = f32[4,128]{1,0:T(4,128)S(1)} collective-permute-done((f32[4,128]{1,0:T(4,128)S(1)}, f32[4,128]{1,0:T(4,128)S(1)}, u32[]{:S(2)}, u32[]{:S(2)}) %collective-permute-start.5) | collective-permute-done | bytes 2080 | tf_op jit(solution)/shard_map/ppermute | solution.py:662
  49.2 1.3 %collective-permute-start.6 = (f32[4,128]{1,0:T(4,128)S(1)}, f32[4,128]{1,0:T(4,128)S(1)}, u32[]{:S(2)}, u32[]{:S(2)}) collective-permute-start(f32[4,128]{1,0:T(4,128)S(1)} %add.15), channel_id=1, source_target_pairs={{0,3},{1,2},{2,1},{3,0},{4,7},{5,6},{6,5},{7,4},{8,11},{9,10},{10,... | collective-permute-start | bytes 6152 | tf_op jit(solution)/shard_map/ppermute | solution.py:662
  50.5 1.7 %collective-permute-done.6 = f32[4,128]{1,0:T(4,128)S(1)} collective-permute-done((f32[4,128]{1,0:T(4,128)S(1)}, f32[4,128]{1,0:T(4,128)S(1)}, u32[]{:S(2)}, u32[]{:S(2)}) %collective-permute-start.6) | collective-permute-done | bytes 2080 | tf_op jit(solution)/shard_map/ppermute | solution.py:662
  52.2 3.4 %collective-permute-start.7 = (f32[4,128]{1,0:T(4,128)S(1)}, f32[4,128]{1,0:T(4,128)S(1)}, u32[]{:S(2)}, u32[]{:S(2)}) collective-permute-start(f32[4,128]{1,0:T(4,128)S(1)} %add.16), channel_id=1, source_target_pairs={{0,17},{1,16},{2,19},{3,18},{4,21},{5,20},{6,23},{7,22},{8,25},{9,... | collective-permute-start | bytes 6152 | tf_op jit(solution)/shard_map/ppermute | solution.py:662
  55.7 1.3 %collective-permute-done.7 = f32[4,128]{1,0:T(4,128)S(1)} collective-permute-done((f32[4,128]{1,0:T(4,128)S(1)}, f32[4,128]{1,0:T(4,128)S(1)}, u32[]{:S(2)}, u32[]{:S(2)}) %collective-permute-start.7) | collective-permute-done | bytes 2080 | tf_op jit(solution)/shard_map/ppermute | solution.py:662
  57.0 1.9 %collective-permute-start.8 = (f32[4,128]{1,0:T(4,128)S(1)}, f32[4,128]{1,0:T(4,128)S(1)}, u32[]{:S(2)}, u32[]{:S(2)}) collective-permute-start(f32[4,128]{1,0:T(4,128)S(1)} %add.17), channel_id=1, source_target_pairs={{0,9},{1,8},{2,11},{3,10},{4,13},{5,12},{6,15},{7,14},{8,1},{9,0},... | collective-permute-start | bytes 6152 | tf_op jit(solution)/shard_map/ppermute | solution.py:662
  58.9 1.3 %collective-permute-done.8 = f32[4,128]{1,0:T(4,128)S(1)} collective-permute-done((f32[4,128]{1,0:T(4,128)S(1)}, f32[4,128]{1,0:T(4,128)S(1)}, u32[]{:S(2)}, u32[]{:S(2)}) %collective-permute-start.8) | collective-permute-done | bytes 2080 | tf_op jit(solution)/shard_map/ppermute | solution.py:662
  60.2 3.0 %collective-permute-start.9 = (f32[4,128]{1,0:T(4,128)S(1)}, f32[4,128]{1,0:T(4,128)S(1)}, u32[]{:S(2)}, u32[]{:S(2)}) collective-permute-start(f32[4,128]{1,0:T(4,128)S(1)} %add.18), channel_id=1, source_target_pairs={{0,5},{1,4},{2,7},{3,6},{4,1},{5,0},{6,3},{7,2},{8,13},{9,12},{10,... | collective-permute-start | bytes 6152 | tf_op jit(solution)/shard_map/ppermute | solution.py:662
  63.2 1.3 %collective-permute-done.9 = f32[4,128]{1,0:T(4,128)S(1)} collective-permute-done((f32[4,128]{1,0:T(4,128)S(1)}, f32[4,128]{1,0:T(4,128)S(1)}, u32[]{:S(2)}, u32[]{:S(2)}) %collective-permute-start.9) | collective-permute-done | bytes 2080 | tf_op jit(solution)/shard_map/ppermute | solution.py:662
  64.5 0.0 collective-permute-done.10.recv_next
  64.5 2.5 %final_update.1 = (f32[4,256,512]{2,1,0:T(8,128)}, f32[4,256,512]{2,1,0:T(8,128)}) custom-call(f32[4,128]{1,0:T(4,128)S(1)} %add.19.tables, f32[4,256,512]{2,1,0:T(8,128)S(1)} %get-tuple-element.42.b, f32[256,512]{1,0:T(8,128)S(1)} %get-tuple-element.62.s_first, f32[2,256,512]{2,1,0:T(8,128)S(1)} %get-tuple-element.63.s_mid, ...), custom_call_target="tpu_custom_call" | custom-call | flops 4194304 | bytes 11534336 | tf_op jit(solution)/shard_map/final_update/pallas_call | solution.py:834
  (7 shorter events, 0.0 us)
Async XLA Ops:
  0.6 3.1 %copy-start.1 = (s32[1,1,1024]{2,1,0:T(1,128)S(1)}, s32[1,1,1024]{2,1,0:T(1,128)}, u32[]{:S(2)}) copy-start(s32[1,1,1024]{2,1,0:T(1,128)} %perm.1) | copy-start | bytes 12292
  0.6 3.1 %copy-start.2 = (s32[1,1,1024]{2,1,0:T(1,128)S(1)}, s32[1,1,1024]{2,1,0:T(1,128)}, u32[]{:S(2)}) copy-start(s32[1,1,1024]{2,1,0:T(1,128)} %kind.1) | copy-start | bytes 12292
  0.7 3.1 %copy-start = (f32[4,128,128]{2,1,0:T(8,128)S(1)}, f32[4,128,128]{2,1,0:T(8,128)}, u32[]{:S(2)}) copy-start(f32[4,128,128]{2,1,0:T(8,128)} %proj.1) | copy-start | bytes 786436
  1.8 17.9 %collective-permute-start = (f32[264,512]{1,0:T(8,128)S(1)}, f32[264,512]{1,0:T(8,128)S(1)}, u32[]{:S(2)}, u32[]{:S(2)}) collective-permute-start(f32[264,512]{1,0:T(8,128)S(1)} %pack.1), channel_id=1, source_target_pairs={{4,0},{8,4},{12,8},{16,12},{20,16},{24,20},{28,24},{5,1},{9,5},{13... | collective-permute-start | bytes 1622024 | tf_op jit(solution)/shard_map/ppermute | solution.py:646
  9.1 28.1 %collective-permute-start.3 = (f32[256,512]{1,0:T(8,128)S(1)}, f32[256,512]{1,0:T(8,128)S(1)}, u32[]{:S(2)}, u32[]{:S(2)}) collective-permute-start(f32[256,512]{1,0:T(8,128)S(1)} %get-tuple-element.67), channel_id=1, source_target_pairs={{4,0},{8,4},{12,8},{16,12},{20,16},{24,20},{28,24},{5,1},{9,5},{13... | collective-permute-start | bytes 1572872 | tf_op jit(solution)/shard_map/ppermute | solution.py:646
  22.8 18.7 %collective-permute-start.4 = (f32[256,512]{1,0:T(8,128)S(1)}, f32[256,512]{1,0:T(8,128)S(1)}, u32[]{:S(2)}, u32[]{:S(2)}) collective-permute-start(f32[256,512]{1,0:T(8,128)S(1)} %back_first.1.later.back.back_before), channel_id=1, source_target_pairs={{0,4},{4,8},{8,12},{12,16},{16,20},{20,24},{24,28},{1,5},{5,9},{9,... | collective-permute-start | bytes 1572872 | tf_op jit(solution)/shard_map/ppermute | solution.py:646
  27.7 6.2 %collective-permute-start.1 = (f32[15,512]{1,0:T(8,128)S(1)}, f32[15,512]{1,0:T(8,128)S(1)}, u32[]{:S(2)}, u32[]{:S(2)}) collective-permute-start(f32[15,512]{1,0:T(8,128)S(1)} %get-tuple-element.59), channel_id=1, source_target_pairs={{0,1},{1,2},{2,3},{4,5},{5,6},{6,7},{8,9},{9,10},{10,11},{12,13},{... | collective-permute-start | bytes 92168 | tf_op jit(solution)/shard_map/ppermute | solution.py:646
  29.0 4.9 %collective-permute-start.2 = (f32[10,512]{1,0:T(8,128)S(1)}, f32[10,512]{1,0:T(8,128)S(1)}, u32[]{:S(2)}, u32[]{:S(2)}) collective-permute-start(f32[10,512]{1,0:T(8,128)S(1)} %get-tuple-element.60), channel_id=1, source_target_pairs={{1,0},{2,1},{3,2},{5,4},{6,5},{7,6},{9,8},{10,9},{11,10},{13,12},{... | collective-permute-start | bytes 61448 | tf_op jit(solution)/shard_map/ppermute | solution.py:646
  41.5 23.0 %collective-permute-start.10 = (f32[264,512]{1,0:T(8,128)S(1)}, f32[264,512]{1,0:T(8,128)S(1)}, u32[]{:S(2)}, u32[]{:S(2)}) collective-permute-start(f32[264,512]{1,0:T(8,128)S(1)} %hold.1), channel_id=1, source_target_pairs={{0,4},{4,8},{8,12},{12,16},{16,20},{20,24},{24,28},{1,5},{5,9},{9,... | collective-permute-start | bytes 1622024 | tf_op jit(solution)/shard_map/ppermute | solution.py:646
  48.0 1.2 %collective-permute-start.5 = (f32[4,128]{1,0:T(4,128)S(1)}, f32[4,128]{1,0:T(4,128)S(1)}, u32[]{:S(2)}, u32[]{:S(2)}) collective-permute-start(f32[4,128]{1,0:T(4,128)S(1)} %get-tuple-element.73), channel_id=1, source_target_pairs={{0,1},{1,0},{2,3},{3,2},{4,5},{5,4},{6,7},{7,6},{8,9},{9,8},{10,11... | collective-permute-start | bytes 6152 | tf_op jit(solution)/shard_map/ppermute | solution.py:662
  49.2 3.0 %collective-permute-start.6 = (f32[4,128]{1,0:T(4,128)S(1)}, f32[4,128]{1,0:T(4,128)S(1)}, u32[]{:S(2)}, u32[]{:S(2)}) collective-permute-start(f32[4,128]{1,0:T(4,128)S(1)} %add.15), channel_id=1, source_target_pairs={{0,3},{1,2},{2,1},{3,0},{4,7},{5,6},{6,5},{7,4},{8,11},{9,10},{10,... | collective-permute-start | bytes 6152 | tf_op jit(solution)/shard_map/ppermute | solution.py:662
  52.2 4.8 %collective-permute-start.7 = (f32[4,128]{1,0:T(4,128)S(1)}, f32[4,128]{1,0:T(4,128)S(1)}, u32[]{:S(2)}, u32[]{:S(2)}) collective-permute-start(f32[4,128]{1,0:T(4,128)S(1)} %add.16), channel_id=1, source_target_pairs={{0,17},{1,16},{2,19},{3,18},{4,21},{5,20},{6,23},{7,22},{8,25},{9,... | collective-permute-start | bytes 6152 | tf_op jit(solution)/shard_map/ppermute | solution.py:662
  57.0 3.2 %collective-permute-start.8 = (f32[4,128]{1,0:T(4,128)S(1)}, f32[4,128]{1,0:T(4,128)S(1)}, u32[]{:S(2)}, u32[]{:S(2)}) collective-permute-start(f32[4,128]{1,0:T(4,128)S(1)} %add.17), channel_id=1, source_target_pairs={{0,9},{1,8},{2,11},{3,10},{4,13},{5,12},{6,15},{7,14},{8,1},{9,0},... | collective-permute-start | bytes 6152 | tf_op jit(solution)/shard_map/ppermute | solution.py:662
  60.2 4.3 %collective-permute-start.9 = (f32[4,128]{1,0:T(4,128)S(1)}, f32[4,128]{1,0:T(4,128)S(1)}, u32[]{:S(2)}, u32[]{:S(2)}) collective-permute-start(f32[4,128]{1,0:T(4,128)S(1)} %add.18), channel_id=1, source_target_pairs={{0,5},{1,4},{2,7},{3,6},{4,1},{5,0},{6,3},{7,2},{8,13},{9,12},{10,... | collective-permute-start | bytes 6152 | tf_op jit(solution)/shard_map/ppermute | solution.py:662

commit v3 on v2

--- a/solution.py
+++ b/solution.py
@@ -29,6 +29,13 @@
 def from_tile(tile, place):
     pick = (tile_ids(1, tile.shape) == place) & (tile_ids(0, tile.shape) == 0)
     return jnp.sum(jnp.where(pick, tile, 0.0))
+
+
+def fold(array):
+    parts = [array[:, place : place + LANES] for place in range(0, array.shape[1], LANES)]
+    while len(parts) > 1:
+        parts = [one + other for one, other in zip(parts[::2], parts[1::2])]
+    return parts[0]
 
 
 def at(array, layers, start):
@@ -88,7 +95,7 @@
     return high, (array - high.astype(F32)).astype(BF16)
 
 
-def prepare_pairs(perm, kind, count, proj, rows, groups, picks, puts, codes, proj_t, proj_n):
+def prepare_pairs(perm, kind, count, proj, rows, groups, picks, puts, codes, code_row, proj_t, proj_n):
     kinds, width, _ = proj.shape
     blocks = rows * groups
     lane = tile_ids(1, (1, blocks))
@@ -109,14 +116,16 @@
         ).astype(jnp.int32)
         column = jnp.broadcast_to(column, (rows, LANES))
         here = pl.ds(group * rows, rows)
+        for place in range(rows // LANES):
+            turned = jnp.transpose(column[place * LANES : (place + 1) * LANES].astype(F32))
+            across.append(turned[0:1, :].astype(jnp.int32))
         codes[here, :] = column & ((1 << shift) - 1)
         column = column >> shift
         for place in range(blocks // LANES):
             picks[here, pl.ds(place * LANES, LANES)] = jnp.where(column == lanes + place * LANES, 1.0, 0.0).astype(BF16)
-        for place in range(rows // LANES):
-            turned = jnp.transpose(column[place * LANES : (place + 1) * LANES].astype(F32))
-            across.append(turned[0:1, :].astype(jnp.int32))
     across = jnp.concatenate(across, axis=1)
+    code_row[...] = (kinds - (across & ((1 << shift) - 1))).astype(F32)
+    across = across >> shift
     down = tile_ids(0, (rows, blocks))
     for group in range(groups):
         puts[pl.ds(group * rows, rows), :] = jnp.where(across == down + group * rows, 1.0, 0.0).astype(BF16)
@@ -128,7 +137,7 @@
 
 def first_kernel(
     count, perm, kind, proj, b_hbm, tx_hbm, ty_hbm, tz_hbm, st_hbm,
-    b, tx, ty, tz, st, face_next, s_first, s_mid, s_last, sums, picks, puts, codes, proj_t, proj_n, total, sems,
+    b, tx, ty, tz, st, face_next, s_first, s_mid, s_last, sums, picks, puts, codes, code_row, proj_t, proj_n, total, sems,
 ):
     layers, rows, depth = b.shape
     steps = rows // ROWS
@@ -145,7 +154,7 @@
             copy(which, step).start()
     width = proj.shape[1]
     prepare_pairs(
-        perm[0], kind[0], count[0, 0], proj, rows, depth // width, picks, puts, codes, proj_t, proj_n
+        perm[0], kind[0], count[0, 0], proj, rows, depth // width, picks, puts, codes, code_row, proj_t, proj_n
     )
     total[...] = jnp.zeros_like(total)
     copy(0, 0).wait()
@@ -158,8 +167,8 @@
         for layer in range(1, layers):
             squares = squares + values[layer] * values[layer]
             products = products + values[layer] * results[layer]
-        total[0] += squares
-        total[1] += products
+        total[0] += fold(squares)
+        total[1] += fold(products)
         face_next[here, :] = results[0]
         s_first[here, :] = results[0]
         for layer in range(1, layers - 1):
@@ -183,8 +192,8 @@
 
 
 def edge_kernel(
-    sums_in, near_sums, b, right, up, down, tx, ty, tz, st, s_first_in, s_mid_in, s_last_in, w_last_in,
-    s_first, s_mid, s_last, w_last, sums, image_ends, ends_sums, right_edges, w_up, w_down,
+    sums_in, near_sums, b, right, up, down, tx, ty, tz, st, s_first_in, s_mid_in, s_last_in, w_last_in, image_low_in,
+    s_first, s_mid, s_last, w_last, image_low, sums, image_ends, ends_sums, right_edges, missing, w_up, w_down,
 ):
     layers, rows, depth = b.shape
     at_b, at_ty, at_w, at_back, at_right, at_right_ty = up_places(layers)
@@ -211,6 +220,10 @@
     )
     right_edges[0:1, :] = low
     right_edges[1:2, :] = high
+    missing[0:1, :] = -up[at_right_ty : at_right_ty + 1, :] * up[at_back : at_back + 1, :]
+    missing[1:2, :] = jnp.where(
+        at_last_block(), 0.0, -right[rows + SUB - 1 :, :] * down[2 * layers : 2 * layers + 1, :]
+    )
     near = from_tile(near_sums[...], 2)
     own, read, plain = high_layers(layers, s_mid, s_last, w_last)
     terms = None
@@ -225,6 +238,11 @@
         )
         terms = new if terms is None else [old + more for old, more in zip(terms, new)]
     ends_sums[...] = as_tile([0.0] * 3 + [jnp.sum(term) for term in terms])
+    own, read = low_layers(layers, s_first, s_mid)
+    zero = [jnp.zeros((SUB, depth), F32)] * len(own)
+    low_chunk(0, read(0), read(SUB), zero, own, tx, ty, tz, st, image_low)
+    carry = flux_from(rows - 2 * SUB, own, read, 0, ty)
+    low_chunk(rows - SUB, read(rows - SUB), None, carry, own, tx, ty, tz, st, image_low)
 
 
 def high_layers(layers, s_mid, s_last, w_last):
@@ -269,7 +287,7 @@
             continue
         u = b[layer, here, :] - near * w
         q = plain(layer, here) - near * s
-        new = [u * u, u * w, w * w, u * q, u * s + w * q, w * s]
+        new = [fold(term) for term in (u * u, u * w, w * w, u * q, u * s + w * q, w * s)]
         terms = new if terms is None else [old + more for old, more in zip(terms, new)]
     return terms, carry
 
@@ -316,7 +334,7 @@
     return jnp.concatenate(two_parts(jnp.concatenate(parts, axis=0)), axis=1)
 
 
-def jump_first_kernel(b, right, s_last, picks, codes, proj_t, w_last, jump_face, sums):
+def jump_first_kernel(earlier, b, right, s_last, picks, codes, proj_t, w_last, jump_face, sums):
     width = proj_t.shape[1] // 2
     layers, rows, depth = b.shape
     parts = [pl.ds(group * width, width) for group in range(depth // width)]
@@ -328,6 +346,14 @@
         jump_face[:, part] = jump
         w_last[:, part] = s_last[:, part] + penalty * jump
     sums[...] = as_tile([jnp.sum(square)])
+
+
+def kinds_kernel(code_row, picks, kinds_by_block):
+    depth = kinds_by_block.shape[1]
+    row = mm(jnp.broadcast_to(code_row[...], (2 * SUB, code_row.shape[1])).astype(BF16), picks[...])
+    kinds_by_block[...] = jnp.zeros_like(kinds_by_block)
+    for place in range(row.shape[1] // depth):
+        kinds_by_block[place : place + 1, :] = row[0:1, place * depth : (place + 1) * depth]
 
 
 def rows_kernel(right, b, ty, s_first, s_mid, w_last, back, up, down):
@@ -349,15 +375,14 @@
 
 
 def jump_second_kernel(
-    near_sums, w_last, jump, right_before, right, right_edges, back_before, up, down, picks, codes, proj_t,
-    jump_next, sums, missing, field,
+    near_sums, w_last, jump, right_before, right, right_edges, back_before, missing, picks, codes, proj_t,
+    jump_next, sums, field,
 ):
     width = proj_t.shape[1] // 2
     rows, depth = right.shape
-    layers = (up.shape[0] - 3) // 3
     parts = [pl.ds(group * width, width) for group in range(depth // width)]
     near = from_tile(near_sums[...], 2)
-    field[...] = right[...] + back_before[...]
+    field[...] = right[...] + back_before[:rows, :]
     field[0:1, :] += right_edges[0:1, :]
     field[rows - 1 :, :] += right_edges[1:2, :]
     faces = stack_parts([field[:, part] for part in parts])
@@ -369,23 +394,42 @@
         totals = [total + new for total, new in zip(totals, (close * close, close * later, later * later))]
     found = [jnp.sum(total) for total in totals]
     found = [penalty * found[0], 2.0 * penalty * found[1], penalty * found[2]]
-    _, _, _, at_back, _, at_right_ty = up_places(layers)
-    low = -up[at_right_ty : at_right_ty + 1, :] * up[at_back : at_back + 1, :]
-    high = jnp.where(at_last_block(), 0.0, -right_before[rows + SUB - 1 :, :] * down[2 * layers : 2 * layers + 1, :])
-    missing[0:1, :] = low
-    missing[1:2, :] = high
     extra = [0.0] * 3
-    for place, s in ((0, low), (rows - 1, high)):
+    for side, place in enumerate((0, rows - 1)):
+        s = missing[side : side + 1, :]
         w = field[place : place + 1, :]
         u = right_before[place : place + 1, :] - near * w
         extra = [old + more for old, more in zip(extra, [-near * u * s, u * s - near * w * s, w * s])]
     sums[...] = as_tile([0.0] * 6 + [old + jnp.sum(more) for old, more in zip(found, extra)])
 
 
-def back_second_kernel(jump_next, missing, puts, codes, proj_n, back):
-    rows = jump_next.shape[0]
-    back_kernel(jump_next, puts, codes, proj_n, back)
+def back_first_kernel(jump, kinds_by_block, puts, codes, proj_n, back):
+    rows = jump.shape[0]
+    back_kernel(jump, puts, codes, proj_n, back)
+    back[rows:, :] = kinds_by_block[...]
+
+
+def back_second_kernel(w_last, missing, puts, codes, proj_n, back):
+    rows = w_last.shape[0]
+    back_kernel(w_last, puts, codes, proj_n, back)
     back[rows : rows + 2, :] = missing[...]
+
+
+def own_second_kernel(s_first, recv, proj_t, proj_n, own):
+    rows, depth = own.shape
+    width = proj_t.shape[1] // 2
+    kinds = proj_t.shape[0] // width
+    for group in range(depth // width):
+        part = pl.ds(group * width, width)
+        codes = []
+        for place in range(rows // LANES):
+            start = group * rows + place * LANES
+            row = recv[rows + start // depth : rows + start // depth + 1, start % depth : start % depth + LANES]
+            codes.append(jnp.transpose(jnp.broadcast_to(row, (LANES, LANES))))
+        codes = kinds - jnp.concatenate(codes, axis=0).astype(jnp.int32)
+        field = s_first[:, part] + recv[:rows, part]
+        projected = apply_proj(codes, *two_parts(field), proj_t, kinds, width)
+        own[:, part] = penalty * apply_proj(codes, *two_parts(projected), proj_n, kinds, width)
 
 
 def hold_kernel(later, back_in, back):
@@ -449,30 +493,51 @@
     sums[...] = as_tile([0.0, 0.0, near] + found)
 
 
-def second_low_kernel(high_sums, b, s_first, s_mid, tx, ty, tz, st, image, sums, total):
-    layers = b.shape[0]
+def low_layers(layers, s_first, s_mid):
     split = layers // 2
-    near = from_tile(high_sums[...], 2)
 
     def read(start):
         here = pl.ds(start, SUB)
         return [s_first[here, :]] + [s_mid[layer - 1, here, :] for layer in range(1, split + 1)]
 
-    def plain(layer, here):
-        return s_mid[layer - 1, here, :]
-
-    own = list(range(split))
-    found = stencil_sums(read, own, near, b, plain, tx, ty, tz, st, image, total, False, own[1:])
-    sums[...] = high_sums[...] + as_tile([0.0] * 3 + found)
+    return list(range(split)), read
+
+
+def low_chunk(start, values, after, carry, own, tx, ty, tz, st, image):
+    here = pl.ds(start, SUB)
+    results, carry = stencil(
+        values[:-1], None if after is None else after[:-1],
+        *[[array[layer, here, :] for layer in own] for array in (tx, ty, tz, st)], carry, None, values[-1],
+    )
+    for layer in own:
+        image[layer, here, :] = results[layer]
+    return carry
+
+
+def second_low_kernel(s_first, s_mid, tx, ty, tz, st, image):
+    layers, rows = tx.shape[:2]
+    own, read = low_layers(layers, s_first, s_mid)
+    group = 3
+
+    def several(index, carry):
+        start = pl.multiple_of(SUB + index * group * SUB, SUB)
+        starts = [pl.multiple_of(start + SUB * place, SUB) for place in range(group + 1)]
+        values = [read(place) for place in starts]
+        carry = list(carry)
+        for place in range(group):
+            carry = low_chunk(starts[place], values[place], values[place + 1], carry, own, tx, ty, tz, st, image)
+        return tuple(carry)
+
+    lax.fori_loop(0, (rows // SUB - 2) // group, several, tuple(flux_from(0, own, read, 0, ty)))
 
 
 def second_added_kernel(
-    first_sums, jump_sums, low_sums, ends_sums, second_sums, b, s_first, s_mid, w_last, recv,
+    first_sums, jump_sums, high_sums, ends_sums, second_sums, b, s_first, s_mid, w_last, recv,
     w_up, w_down, up, tx, ty, tz, st, image_in, image, edge_high, table, total,
 ):
     layers, rows, depth = b.shape
     split = layers // 2
-    near = from_tile(low_sums[...], 2)
+    near = from_tile(high_sums[...], 2)
     total[...] = jnp.zeros_like(total)
     first, second = 0, 1
 
@@ -495,13 +560,13 @@
             u = b[first, here, :] - near * w
             q = plain - near * s
             new = [u * u, u * w, w * w, u * q, u * s + w * q, w * s]
-            added_s = -t_x * e
-            image[second, here, :] = image_in[second, here, :] + added_s
+            s = image_in[second, here, :] - t_x * e
+            image[second, here, :] = s
             w = s_mid[second - 1, here, :]
             u = b[second, here, :] - near * w
-            new[3] = new[3] - near * u * added_s
-            new[4] = new[4] + (u - near * w) * added_s
-            new[5] = new[5] + w * added_s
+            q = w - near * s
+            more = [u * u, u * w, w * w, u * q, u * s + w * q, w * s]
+            new = [fold(one + other) for one, other in zip(new, more)]
             terms = new if terms is None else [old + more for old, more in zip(terms, new)]
         for place, term in enumerate(terms):
             total[place] += term
@@ -540,7 +605,7 @@
     found[3:] = [old + jnp.sum(more) for old, more in zip(found[3:], extra)]
     norm = from_tile(first_sums[...], 0)
     energy = from_tile(first_sums[...], 1) + penalty * from_tile(jump_sums[...], 0)
-    sums = low_sums[...] + ends_sums[...] + second_sums[...]
+    sums = high_sums[...] + ends_sums[...] + second_sums[...]
     sums = sums + as_tile([norm, energy, 0.0] + found)
     mine = lax.axis_index("sub") * lax.axis_size("blk") + lax.axis_index("blk")
     device = tile_ids(0, table.shape) * (LANES // FIELDS) + lax.div(tile_ids(1, table.shape), FIELDS)
@@ -552,7 +617,7 @@
 
 
 def final_kernel(
-    tables, b, s_first, s_mid, w_last, recv, image_low, image_high, image_ends, edge_high, jump_next, recv_next, solution_hbm, residual_hbm,
+    tables, b, s_first, s_mid, w_last, recv, image_low, image_high, image_ends, edge_high, jump_next, recv_next, own_next, solution_hbm, residual_hbm,
     solution, residual, sems,
 ):
     layers, rows, depth = b.shape
@@ -598,7 +663,7 @@
                     s = image_high[layer - split, here, :]
                 if layer == 0:
                     w = s_first[here, :] + recv[here, :]
-                    s = s + recv_next[here, :]
+                    s = s + (recv_next[here, :] + own_next[here, :])
                 elif layer < layers - 1:
                     w = s_mid[layer - 1, here, :]
                 else:
@@ -637,6 +702,12 @@
     return [pltpu.with_memory_space_constraint(array, pltpu.HBM) for array in arrays]
 
 
+def scaled(estimate, by):
+    return pl.CostEstimate(
+        flops=int(estimate.flops * by) + 1, bytes_accessed=int(estimate.bytes_accessed * by) + 1, transcendentals=0
+    )
+
+
 def params(mib):
     return pltpu.CompilerParams(vmem_limit_bytes=mib * 1024 * 1024)
 
@@ -678,24 +749,24 @@
         out_shape=[held(rows + SUB, depth)],
         scratch_shapes=[pltpu.SemaphoreType.DMA((2,))],
         compiler_params=params(2),
-        cost_estimate=cost(0, 4 * rows * depth),
+        cost_estimate=scaled(cost(0, 4 * rows * depth), 100),
         name="pack",
     )(*in_hbm(right_side, trans_y))
     face_right = shifted(face, "sub", -1)
 
-    b, tx, ty, tz, st, face_next, s_first, s_mid, s_last, first_sums, picks, puts, codes, proj_t, proj_n = pl.pallas_call(
+    b, tx, ty, tz, st, face_next, s_first, s_mid, s_last, first_sums, picks, puts, codes, code_row, proj_t, proj_n = pl.pallas_call(
         first_kernel,
         in_specs=[SMEM] + [VMEM] * 3 + [HBM] * 5,
-        out_specs=[VMEM] * 15,
+        out_specs=[VMEM] * 16,
         out_shape=[held(layers, rows, depth)] * 5
         + [
             held(rows, depth), held(rows, depth), held(layers - 2, rows, depth), held(rows, depth), held(SUB, LANES),
-            held(blocks, blocks, dtype=BF16), held(blocks, blocks, dtype=BF16), held(blocks, width, dtype=jnp.int32),
+            held(blocks, blocks, dtype=BF16), held(blocks, blocks, dtype=BF16), held(blocks, width, dtype=jnp.int32), held(1, blocks),
             held(kinds * width, 2 * width, dtype=BF16), held(kinds * width, 2 * width, dtype=BF16),
         ],
-        scratch_shapes=[pltpu.VMEM((2, SUB, depth), F32), pltpu.SemaphoreType.DMA((5, steps))],
+        scratch_shapes=[pltpu.VMEM((2, SUB, LANES), F32), pltpu.SemaphoreType.DMA((5, steps))],
         compiler_params=params(16),
-        cost_estimate=cost(20 * cells, 24 * cells),
+        cost_estimate=scaled(cost(20 * cells, 24 * cells), 1),
         name="stencil_first",
     )(
         pair_count, pair_perm, pair_type, proj,
@@ -703,25 +774,45 @@
     )
     face_right_next = shifted(face_next, "sub", -1)
 
+    split = layers // 2
+    (image_low,) = pl.pallas_call(
+        second_low_kernel,
+        in_specs=[VMEM] * 6,
+        out_specs=[VMEM],
+        out_shape=[held(split, rows, depth)],
+        compiler_params=params(8),
+        cost_estimate=scaled(cost(20 * cells, 15 * cells), 0),
+        name="stencil_second_low",
+    )(*near_core(s_first, s_mid, tx, ty, tz, st))
+
     mortar_cost = cost(4 * blocks * blocks * width + 6 * kinds * blocks * width * width, 14 * rows * depth)
     w_last, jump, jump_sums = pl.pallas_call(
         jump_first_kernel,
-        in_specs=[VMEM] * 6,
+        in_specs=[VMEM] * 7,
         out_specs=[VMEM] * 3,
         out_shape=[held(rows, depth), held(rows, depth), held(SUB, LANES)],
         compiler_params=params(16),
-        cost_estimate=mortar_cost,
+        cost_estimate=scaled(mortar_cost, 100),
         name="jump_first",
-    )(*near_core(b, face_right, s_last, picks, codes, proj_t))
+    )(*near_core(image_low, b, face_right, s_last, picks, codes, proj_t))
+    (kinds_by_block,) = pl.pallas_call(
+        kinds_kernel,
+        in_specs=[VMEM] * 2,
+        out_specs=[VMEM],
+        out_shape=[held(SUB, depth)],
+        compiler_params=params(8),
+        cost_estimate=scaled(cost(16 * blocks * blocks, 2 * blocks * blocks), 3),
+        name="kinds",
+    )(*near_core(code_row, picks))
     (back,) = pl.pallas_call(
-        back_kernel,
-        in_specs=[VMEM] * 4,
+        back_first_kernel,
+        in_specs=[VMEM] * 5,
         out_specs=[VMEM],
-        out_shape=[held(rows, depth)],
+        out_shape=[held(rows + SUB, depth)],
         compiler_params=params(16),
-        cost_estimate=mortar_cost,
+        cost_estimate=scaled(mortar_cost, 1),
         name="back_first",
-    )(*near_core(jump, puts, codes, proj_n))
+    )(*near_core(jump, kinds_by_block, puts, codes, proj_n))
     recv = shifted(back, "sub", 1)
 
     split = layers // 2
@@ -730,9 +821,9 @@
         in_specs=[VMEM] * 11,
         out_specs=[VMEM] * 2,
         out_shape=[held(layers - split, rows, depth), held(SUB, LANES)],
-        scratch_shapes=[pltpu.VMEM((6, SUB, depth), F32)],
+        scratch_shapes=[pltpu.VMEM((6, SUB, LANES), F32)],
         compiler_params=params(8),
-        cost_estimate=cost(20 * cells, 15 * cells),
+        cost_estimate=scaled(cost(20 * cells, 15 * cells), 10),
         name="stencil_second_high",
     )(*near_core(back, first_sums, jump_sums, b, s_mid, s_last, w_last, tx, ty, tz, st))
     up_out, down_out = pl.pallas_call(
@@ -741,51 +832,40 @@
         out_specs=[VMEM] * 2,
         out_shape=[held(3 * layers + 3, depth), held(2 * layers + 2, depth)],
         compiler_params=params(2),
-        cost_estimate=cost(0, 64 * depth),
+        cost_estimate=scaled(cost(0, 64 * depth), 1),
         name="rows",
     )(*near_core(face_right, b, ty, s_first, s_mid, w_last, back))
     up = shifted(up_out, "blk", 1)
     down = shifted(down_out, "blk", -1)
-    s_first, s_mid, s_last, w_last, edge_sums, image_ends, ends_sums, right_edges, w_up, w_down = pl.pallas_call(
+    s_first, s_mid, s_last, w_last, image_low, edge_sums, image_ends, ends_sums, right_edges, missing, w_up, w_down = pl.pallas_call(
         edge_kernel,
-        in_specs=[VMEM] * 14,
-        out_specs=[VMEM] * 10,
+        in_specs=[VMEM] * 15,
+        out_specs=[VMEM] * 12,
         out_shape=[held(rows, depth), held(layers - 2, rows, depth), held(rows, depth), held(rows, depth)]
-        + [held(SUB, LANES), held(layers - split, 2 * SUB, depth), held(SUB, LANES)]
-        + [held(2, depth), held(layers, depth), held(layers, depth)],
-        input_output_aliases={10: 0, 11: 1, 12: 2, 13: 3},
+        + [held(split, rows, depth), held(SUB, LANES), held(layers - split, 2 * SUB, depth), held(SUB, LANES)]
+        + [held(2, depth), held(2, depth), held(layers, depth), held(layers, depth)],
+        input_output_aliases={10: 0, 11: 1, 12: 2, 13: 3, 14: 4},
         compiler_params=params(4),
-        cost_estimate=cost(320 * depth, 640 * depth),
+        cost_estimate=scaled(cost(320 * depth, 640 * depth), 3),
         name="edges_first",
     )(
         *near_core(
-            first_sums, high_sums, b, face_right, up, down, tx, ty, tz, st, s_first, s_mid, s_last, w_last,
+            first_sums, high_sums, b, face_right, up, down, tx, ty, tz, st, s_first, s_mid, s_last, w_last, image_low,
         )
     )
 
-    image_low, low_sums = pl.pallas_call(
-        second_low_kernel,
-        in_specs=[VMEM] * 8,
+    jump_next, second_sums = pl.pallas_call(
+        jump_second_kernel,
+        in_specs=[VMEM] * 11,
         out_specs=[VMEM] * 2,
-        out_shape=[held(split, rows, depth), held(SUB, LANES)],
-        scratch_shapes=[pltpu.VMEM((6, SUB, depth), F32)],
-        compiler_params=params(8),
-        cost_estimate=cost(20 * cells, 15 * cells),
-        name="stencil_second_low",
-    )(*near_core(high_sums, b, s_first, s_mid, tx, ty, tz, st))
-
-    jump_next, second_sums, missing = pl.pallas_call(
-        jump_second_kernel,
-        in_specs=[VMEM] * 12,
-        out_specs=[VMEM] * 3,
-        out_shape=[held(rows, depth), held(SUB, LANES), held(2, depth)],
+        out_shape=[held(rows, depth), held(SUB, LANES)],
         scratch_shapes=[pltpu.VMEM((rows, depth), F32)],
         compiler_params=params(16),
-        cost_estimate=mortar_cost,
+        cost_estimate=scaled(mortar_cost, 0.3),
         name="jump_second",
     )(
         *near_core(
-            low_sums, w_last, jump, face_right, face_right_next, right_edges, back, up, down, picks, codes, proj_t,
+            high_sums, w_last, jump, face_right, face_right_next, right_edges, back, missing, picks, codes, proj_t,
         )
     )
     (back_next,) = pl.pallas_call(
@@ -794,20 +874,10 @@
         out_specs=[VMEM],
         out_shape=[held(rows + SUB, depth)],
         compiler_params=params(16),
-        cost_estimate=mortar_cost,
+        cost_estimate=scaled(mortar_cost, 0.3),
         name="back_second",
-    )(*near_core(jump_next, missing, puts, codes, proj_n))
-
-    (back_next,) = pl.pallas_call(
-        hold_kernel,
-        in_specs=[VMEM] * 2,
-        out_specs=[VMEM],
-        out_shape=[held(rows + SUB, depth)],
-        input_output_aliases={1: 0},
-        compiler_params=params(2),
-        cost_estimate=cost(0, 8 * depth),
-        name="hold",
-    )(*near_core(recv, back_next))
+    )(*near_core(w_last, missing, puts, codes, proj_n))
+
     recv_next = shifted(back_next, "sub", 1)
 
     count = subs * blks
@@ -819,28 +889,37 @@
             held(split, rows, depth), held(2 * (layers - split), depth), held(-(-count * FIELDS // LANES), LANES),
         ],
         input_output_aliases={17: 0},
-        scratch_shapes=[pltpu.VMEM((6, SUB, depth), F32)],
+        scratch_shapes=[pltpu.VMEM((6, SUB, LANES), F32)],
         compiler_params=params(8),
-        cost_estimate=cost(20 * cells, 15 * cells),
+        cost_estimate=scaled(cost(20 * cells, 15 * cells), 0.3),
         name="stencil_second_added",
     )(
         *near_core(
-            edge_sums, jump_sums, low_sums, ends_sums, second_sums, b, s_first, s_mid, w_last, recv,
+            edge_sums, jump_sums, high_sums, ends_sums, second_sums, b, s_first, s_mid, w_last, recv,
             w_up, w_down, up, tx, ty, tz, st, image_low,
         )
     )
+    (own_next,) = pl.pallas_call(
+        own_second_kernel,
+        in_specs=[VMEM] * 4,
+        out_specs=[VMEM],
+        out_shape=[held(rows, depth)],
+        compiler_params=params(16),
+        cost_estimate=scaled(mortar_cost, 1),
+        name="own_second",
+    )(*near_core(s_first, recv, proj_t, proj_n))
     tables = gather_rows(table)
 
     return pl.pallas_call(
         final_kernel,
-        in_specs=[VMEM] * 12,
+        in_specs=[VMEM] * 13,
         out_specs=[HBM] * 2,
         out_shape=[jax.ShapeDtypeStruct((layers, rows, depth), F32)] * 2,
         scratch_shapes=[pltpu.VMEM((layers, rows, depth), F32)] * 2 + [pltpu.SemaphoreType.DMA((2, steps))],
         compiler_params=params(8),
-        cost_estimate=cost(8 * cells, 22 * cells),
+        cost_estimate=scaled(cost(8 * cells, 22 * cells), 1),
         name="final_update",
-    )(*near_core(tables, b, s_first, s_mid, w_last, recv, image_low, image_high, image_ends, edge_high, jump_next, recv_next))
+    )(*near_core(tables, b, s_first, s_mid, w_last, recv, image_low, image_high, image_ends, edge_high, jump_next, recv_next, own_next))
 
 
 def solution(mesh):

time: 67.2 us -> 74.4 us (1.11)
  starting transfers between devices: 24.1 us -> 32.2 us
  waiting for transfers between devices: 17.6 us -> 15.3 us
  Pallas kernels: 23.7 us -> 25 us
    ppermute x5, starting transfers between devices: 9.68 us -> 19.4 us  [gather_rows(): table = table + lax.ppermute(table, ('sub', 'blk'), pairs)]
    ppermute x6, waiting for transfers between devices: 10.8 us -> 8.96 us  [shifted(): lax.ppermute(array, axis, [(i, i + by) for i in range(size) if 0 <= i + b...]
    ppermute x6, starting transfers between devices: 14.5 us -> 12.8 us  [shifted(): lax.ppermute(array, axis, [(i, i + by) for i in range(size) if 0 <= i + b...]
    pallas_call x7 -> x8, Pallas kernels: 10.7 us -> 11.6 us  [the longest x1 2.46 us: body(): pl.pallas_call(final_kernel, in_specs=[VMEM] * 13, out_specs=[HBM] * 2, o...]
  transfers between devices with their start and end apart: 11 -> 11, of which waited for: 8 -> 8; matrix products, arithmetic and copies ran while one was open for 0% -> 0% of each run, Pallas kernels for 30% -> 29%
where the time goes in v3:
time: 74.4 us; the launch traced here: 74.1 us
  starting transfers between devices  32.2 us (43%)
  Pallas kernels  25 us (34%)
  waiting for transfers between devices  15.3 us (21%)
  between operations  1.64 us (2%)
    ppermute x5, starting transfers between devices, gather_rows(): table = table + lax.ppermute(table, ('sub', 'blk'), pairs)  19.4 us
    ppermute x6, starting transfers between devices, shifted(): lax.ppermute(array, axis, [(i, i + by) for i in range(size) if 0 <= i + b...  12.8 us
    ppermute x6, waiting for transfers between devices, shifted(): lax.ppermute(array, axis, [(i, i + by) for i in range(size) if 0 <= i + b...  8.96 us
    ppermute x5, waiting for transfers between devices, gather_rows(): table = table + lax.ppermute(table, ('sub', 'blk'), pairs)  6.35 us
    pallas_call x1, Pallas kernels, body(): pl.pallas_call(first_kernel, in_specs=[SMEM] + [VMEM] * 3 + [HBM] * 5, ou...  5.76 us
    pallas_call x1, Pallas kernels, body(): pl.pallas_call(second_high_kernel, in_specs=[VMEM] * 11, out_specs=[VMEM]...  3.13 us
    pallas_call x1, Pallas kernels, body(): pl.pallas_call(final_kernel, in_specs=[VMEM] * 13, out_specs=[HBM] * 2, o...  2.46 us
    pallas_call x1, Pallas kernels, body(): pl.pallas_call(second_added_kernel, in_specs=[VMEM] * 18, out_specs=[VMEM...  2.13 us
  transfers between devices with their start and end apart: 11, of which 8 were waited for; matrix products, arithmetic and copies ran while one was open for 0% of the time, Pallas kernels for 29%

profile of v3, /device:TPU:0, one launch (start us, length us, event | category | flops | bytes accessed | tf_op | source)
XLA Modules:
  0.0 74.1 jit_solution(3770789295267545074)
XLA Ops:
  0.6 0.0 copy-start.1
  0.6 0.0 copy-start.2
  0.7 0.0 copy-start
  0.7 1.1 %pack.1 = f32[264,512]{1,0:T(8,128)S(1)} custom-call(f32[4,256,512]{2,1,0:T(8,128)} %b_hbm.3, f32[4,256,512]{2,1,0:T(8,128)} %ty_hbm.3), custom_call_target="tpu_custom_call" | custom-call | flops 1 | bytes 52428800 | tf_op jit(solution)/shard_map/pack/pallas_call | solution.py:745
  1.8 1.3 %collective-permute-start = (f32[264,512]{1,0:T(8,128)S(1)}, f32[264,512]{1,0:T(8,128)S(1)}, u32[]{:S(2)}, u32[]{:S(2)}) collective-permute-start(f32[264,512]{1,0:T(8,128)S(1)} %pack.1), channel_id=1, source_target_pairs={{4,0},{8,4},{12,8},{16,12},{20,16},{24,20},{28,24},{5,1},{9,5},{13... | collective-permute-start | bytes 1622024 | tf_op jit(solution)/shard_map/ppermute | solution.py:717
  3.7 0.0 copy-done.1
  3.7 0.0 copy-done.2
  3.7 0.0 copy-done
  3.8 5.8 %stencil_first.1 = (f32[4,256,512]{2,1,0:T(8,128)S(1)}, f32[4,256,512]{2,1,0:T(8,128)S(1)}, f32[4,256,512]{2,1,0:T(8,128)S(1)}, f32[4,256,512]{2,1,0:T(8,128)S(1...) custom-call(s32[1,1]{1,0:T(1,128)S(6)} %copy.23.count, ...), custom_call_target="tpu_custom_call" | custom-call | flops 10485761 | bytes 12582913 | tf_op jit(solution)/shard_map/stencil_first/pallas_call | solution.py:757
  9.5 1.3 %collective-permute-start.3 = (f32[256,512]{1,0:T(8,128)S(1)}, f32[256,512]{1,0:T(8,128)S(1)}, u32[]{:S(2)}, u32[]{:S(2)}) collective-permute-start(f32[256,512]{1,0:T(8,128)S(1)} %get-tuple-element.65), channel_id=1, source_target_pairs={{4,0},{8,4},{12,8},{16,12},{20,16},{24,20},{28,24},{5,1},{9,5},{13... | collective-permute-start | bytes 1572872 | tf_op jit(solution)/shard_map/ppermute | solution.py:717
  10.8 1.9 %stencil_second_low.1.earlier.image_low_in = f32[2,256,512]{2,1,0:T(8,128)S(1)} custom-call(f32[256,512]{1,0:T(8,128)S(1)} %get-tuple-element.42.s_first.s_first_in, f32[2,256,512]{2,1,0:T(8,128)S(1)} %get-tuple-element.43.s_mid.s_mid_in, f32[4,256,512]{2,1,0:T(8,128)S(1)} %get-tuple-element.44.tx, f32[4,256,512]{2,1,0:T(8,128)S(1)} %get-tuple-element.45.ty, ...), custom_call_target="tpu_custom_call" | custom-call | flops 1 | bytes 1 | tf_op jit(solution)/shard_map/stencil_second_low/pallas_call | solution.py:778
  12.7 0.4 kinds.1.kinds_by_block
  13.1 6.6 %collective-permute-done.right.right_before = f32[264,512]{1,0:T(8,128)S(1)} collective-permute-done((f32[264,512]{1,0:T(8,128)S(1)}, f32[264,512]{1,0:T(8,128)S(1)}, u32[]{:S(2)}, u32[]{:S(2)}) %collective-permute-start) | collective-permute-done | bytes 540704 | tf_op jit(solution)/shard_map/ppermute | solution.py:717
  19.7 1.8 %jump_first.1 = (f32[256,512]{1,0:T(8,128)S(1)}, f32[256,512]{1,0:T(8,128)S(1)}, f32[8,128]{1,0:T(8,128)S(1)}) custom-call(f32[2,256,512]{2,1,0:T(8,128)S(1)} %stencil_second_low.1.earlier.image_low_in, f32[4,256,512]{2,1,0:T(8,128)S(1)} %get-tuple-element.48.b, f32[264,512]{1,0:T(8,128)S(1)} %collective-permute-done.right.right_before, ...), custom_call_target="tpu_custom_call" | custom-call | flops 93952409600 | bytes 183500800 | tf_op jit(solution)/shard_map/jump_first/pallas_call | solution.py:789
  21.5 1.3 %back_first.1.later.back.back_before = f32[264,512]{1,0:T(8,128)S(1)} custom-call(f32[256,512]{1,0:T(8,128)S(1)} %get-tuple-element.53.jump, f32[8,512]{1,0:T(8,128)S(1)} %kinds.1.kinds_by_block, bf16[1024,1024]{1,0:T(8,128)(2,1)S(1)} %get-tuple-element.55.puts, s32[1024,128]{1,0:T(8,128)S(1)} %get-tuple-element.51.codes, ...), custom_call_target="tpu_custom_call" | custom-call | flops 939524096 | bytes 1835009 | tf_op jit(solution)/shard_map/back_first/pallas_call | solution.py:807
  22.8 4.9 %collective-permute-start.4 = (f32[264,512]{1,0:T(8,128)S(1)}, f32[264,512]{1,0:T(8,128)S(1)}, u32[]{:S(2)}, u32[]{:S(2)}) collective-permute-start(f32[264,512]{1,0:T(8,128)S(1)} %back_first.1.later.back.back_before), channel_id=1, source_target_pairs={{0,4},{4,8},{8,12},{12,16},{16,20},{20,24},{24,28},{1,5},{5,9},{9,... | collective-permute-start | bytes 1622024 | tf_op jit(solution)/shard_map/ppermute | solution.py:717
  27.7 1.3 %collective-permute-start.1 = (f32[15,512]{1,0:T(8,128)S(1)}, f32[15,512]{1,0:T(8,128)S(1)}, u32[]{:S(2)}, u32[]{:S(2)}) collective-permute-start(f32[15,512]{1,0:T(8,128)S(1)} %get-tuple-element.60), channel_id=1, source_target_pairs={{0,1},{1,2},{2,3},{4,5},{5,6},{6,7},{8,9},{9,10},{10,11},{12,13},{... | collective-permute-start | bytes 92168 | tf_op jit(solution)/shard_map/ppermute | solution.py:717
  29.0 1.3 %collective-permute-start.2 = (f32[10,512]{1,0:T(8,128)S(1)}, f32[10,512]{1,0:T(8,128)S(1)}, u32[]{:S(2)}, u32[]{:S(2)}) collective-permute-start(f32[10,512]{1,0:T(8,128)S(1)} %get-tuple-element.61), channel_id=1, source_target_pairs={{1,0},{2,1},{3,2},{5,4},{6,5},{7,6},{9,8},{10,9},{11,10},{13,12},{... | collective-permute-start | bytes 61448 | tf_op jit(solution)/shard_map/ppermute | solution.py:717
  30.3 3.1 %stencil_second_high.1 = (f32[2,256,512]{2,1,0:T(8,128)S(1)}, f32[8,128]{1,0:T(8,128)S(1)}) custom-call(f32[264,512]{1,0:T(8,128)S(1)} %back_first.1.later.back.back_before, f32[8,128]{1,0:T(8,128)S(1)} %get-tuple-element.41.first_sums.sums_in, f32[8,128]{1,0:T(8,128)S(1)} %get-tuple-element.57.jump_sums, f32[4,256,512]{2,1,0:T(8,128)S(1)} %get-tuple-element.48.b, ...), custom_call_target="tpu_custom_call" | custom-call | flops 104857600 | bytes 78643200 | tf_op jit(solution)/shard_map/stencil_second_high/pallas_call | solution.py:819
  33.4 0.4 collective-permute-done.2.down
  33.8 0.0 collective-permute-done.1.up
  33.8 0.3 edges_first.1
  34.2 1.3 %back_second.1 = f32[264,512]{1,0:T(8,128)S(1)} custom-call(f32[256,512]{1,0:T(8,128)S(1)} %get-tuple-element.64.w_last, f32[2,512]{1,0:T(2,128)S(1)} %get-tuple-element.67.missing, bf16[1024,1024]{1,0:T(8,128)(2,1)S(1)} %get-tuple-element.55.puts, s32[1024,128]{1,0:T(8,128)S(1)} %get-tuple-element.51.codes, bf16[512,256]{1,0:T(8,128)(2,1)S(1)} %get-tuple-element.56.proj_n), custom_call_target="tpu_custom_call" | custom-call | flops 281857216 | bytes 550503 | tf_op jit(solution)/shard_map/back_second/pallas_call | solution.py:871
  35.4 2.7 %collective-permute-start.10 = (f32[264,512]{1,0:T(8,128)S(1)}, f32[264,512]{1,0:T(8,128)S(1)}, u32[]{:S(2)}, u32[]{:S(2)}) collective-permute-start(f32[264,512]{1,0:T(8,128)S(1)} %back_second.1), channel_id=1, source_target_pairs={{0,4},{4,8},{8,12},{12,16},{16,20},{20,24},{24,28},{1,5},{5,9},{9,... | collective-permute-start | bytes 1622024 | tf_op jit(solution)/shard_map/ppermute | solution.py:717
  38.2 0.0 collective-permute-done.3.right
  38.2 1.8 %jump_second.1 = (f32[256,512]{1,0:T(8,128)S(1)}, f32[8,128]{1,0:T(8,128)S(1)}) custom-call(f32[8,128]{1,0:T(8,128)S(1)} %get-tuple-element.59.near_sums.high_sums, f32[256,512]{1,0:T(8,128)S(1)} %get-tuple-element.64.w_last, f32[256,512]{1,0:T(8,128)S(1)} %get-tuple-element.53.jump, f32[264,512]{1,0:T(8,128)S(1)} %collective-permute-done.right.right_before, ...), custom_call_target="tpu_custom_call" | custom-call | flops 281857216 | bytes 550503 | tf_op jit(solution)/shard_map/jump_second/pallas_call | solution.py:857
  40.1 1.9 %collective-permute-done.4.recv = f32[264,512]{1,0:T(8,128)S(1)} collective-permute-done((f32[264,512]{1,0:T(8,128)S(1)}, f32[264,512]{1,0:T(8,128)S(1)}, u32[]{:S(2)}, u32[]{:S(2)}) %collective-permute-start.4) | collective-permute-done | bytes 540704 | tf_op jit(solution)/shard_map/ppermute | solution.py:717
  42.0 2.1 %stencil_second_added.1 = (f32[2,256,512]{2,1,0:T(8,128)S(1)}, f32[4,512]{1,0:T(4,128)S(1)}, f32[4,128]{1,0:T(4,128)S(1)}) custom-call(f32[8,128]{1,0:T(8,128)S(1)} %get-tuple-element.62.first_sums, f32[8,128]{1,0:T(8,128)S(1)} %get-tuple-element.57.jump_sums, f32[8,128]{1,0:T(8,128)S(1)} %get-tuple-element.59.near_sums.high_sums, ...), custom_call_target="tpu_custom_call", output_to_operand_aliasing={{0}: (17, {})} | custom-call | flops 3145729 | bytes 2359297 | tf_op jit(solution)/shard_map/stencil_second_added/pallas_call | solution.py:884
  44.1 0.8 %collective-permute-start.5 = (f32[4,128]{1,0:T(4,128)S(1)}, f32[4,128]{1,0:T(4,128)S(1)}, u32[]{:S(2)}, u32[]{:S(2)}) collective-permute-start(f32[4,128]{1,0:T(4,128)S(1)} %get-tuple-element.74), channel_id=1, source_target_pairs={{0,1},{1,0},{2,3},{3,2},{4,5},{5,4},{6,7},{7,6},{8,9},{9,8},{10,11... | collective-permute-start | bytes 6152 | tf_op jit(solution)/shard_map/ppermute | solution.py:733
  44.9 0.8 %collective-permute-done.5 = f32[4,128]{1,0:T(4,128)S(1)} collective-permute-done((f32[4,128]{1,0:T(4,128)S(1)}, f32[4,128]{1,0:T(4,128)S(1)}, u32[]{:S(2)}, u32[]{:S(2)}) %collective-permute-start.5) | collective-permute-done | bytes 2080 | tf_op jit(solution)/shard_map/ppermute | solution.py:733
  45.7 1.6 %collective-permute-start.6 = (f32[4,128]{1,0:T(4,128)S(1)}, f32[4,128]{1,0:T(4,128)S(1)}, u32[]{:S(2)}, u32[]{:S(2)}) collective-permute-start(f32[4,128]{1,0:T(4,128)S(1)} %add.15), channel_id=1, source_target_pairs={{0,3},{1,2},{2,1},{3,0},{4,7},{5,6},{6,5},{7,4},{8,11},{9,10},{10,... | collective-permute-start | bytes 6152 | tf_op jit(solution)/shard_map/ppermute | solution.py:733
  47.3 1.4 %collective-permute-done.6 = f32[4,128]{1,0:T(4,128)S(1)} collective-permute-done((f32[4,128]{1,0:T(4,128)S(1)}, f32[4,128]{1,0:T(4,128)S(1)}, u32[]{:S(2)}, u32[]{:S(2)}) %collective-permute-start.6) | collective-permute-done | bytes 2080 | tf_op jit(solution)/shard_map/ppermute | solution.py:733
  48.8 15.4 %collective-permute-start.7 = (f32[4,128]{1,0:T(4,128)S(1)}, f32[4,128]{1,0:T(4,128)S(1)}, u32[]{:S(2)}, u32[]{:S(2)}) collective-permute-start(f32[4,128]{1,0:T(4,128)S(1)} %add.16), channel_id=1, source_target_pairs={{0,17},{1,16},{2,19},{3,18},{4,21},{5,20},{6,23},{7,22},{8,25},{9,... | collective-permute-start | bytes 6152 | tf_op jit(solution)/shard_map/ppermute | solution.py:733
  64.2 1.3 %collective-permute-done.7 = f32[4,128]{1,0:T(4,128)S(1)} collective-permute-done((f32[4,128]{1,0:T(4,128)S(1)}, f32[4,128]{1,0:T(4,128)S(1)}, u32[]{:S(2)}, u32[]{:S(2)}) %collective-permute-start.7) | collective-permute-done | bytes 2080 | tf_op jit(solution)/shard_map/ppermute | solution.py:733
  65.5 1.6 %collective-permute-start.8 = (f32[4,128]{1,0:T(4,128)S(1)}, f32[4,128]{1,0:T(4,128)S(1)}, u32[]{:S(2)}, u32[]{:S(2)}) collective-permute-start(f32[4,128]{1,0:T(4,128)S(1)} %add.17), channel_id=1, source_target_pairs={{0,9},{1,8},{2,11},{3,10},{4,13},{5,12},{6,15},{7,14},{8,1},{9,0},... | collective-permute-start | bytes 6152 | tf_op jit(solution)/shard_map/ppermute | solution.py:733
  67.1 1.4 %collective-permute-done.8 = f32[4,128]{1,0:T(4,128)S(1)} collective-permute-done((f32[4,128]{1,0:T(4,128)S(1)}, f32[4,128]{1,0:T(4,128)S(1)}, u32[]{:S(2)}, u32[]{:S(2)}) %collective-permute-start.8) | collective-permute-done | bytes 2080 | tf_op jit(solution)/shard_map/ppermute | solution.py:733
  68.5 0.0 collective-permute-start.9
  68.5 1.6 %own_second.1.own_next = f32[256,512]{1,0:T(8,128)S(1)} custom-call(f32[256,512]{1,0:T(8,128)S(1)} %get-tuple-element.69.s_first, f32[264,512]{1,0:T(8,128)S(1)} %collective-permute-done.4.recv, bf16[512,256]{1,0:T(8,128)(2,1)S(1)} %get-tuple-element.52.proj_t, bf16[512,256]{1,0:T(8,128)(2,1)S(1)} %get-tuple-element.56.proj_n), custom_call_target="tpu_custom_call" | custom-call | flops 939524096 | bytes 1835009 | tf_op jit(solution)/shard_map/own_second/pallas_call | solution.py:902
  70.1 1.4 %collective-permute-done.9 = f32[4,128]{1,0:T(4,128)S(1)} collective-permute-done((f32[4,128]{1,0:T(4,128)S(1)}, f32[4,128]{1,0:T(4,128)S(1)}, u32[]{:S(2)}, u32[]{:S(2)}) %collective-permute-start.9) | collective-permute-done | bytes 2080 | tf_op jit(solution)/shard_map/ppermute | solution.py:733
  71.5 0.0 collective-permute-done.10.recv_next
  71.5 2.5 %final_update.1 = (f32[4,256,512]{2,1,0:T(8,128)}, f32[4,256,512]{2,1,0:T(8,128)}) custom-call(f32[4,128]{1,0:T(4,128)S(1)} %add.19.tables, f32[4,256,512]{2,1,0:T(8,128)S(1)} %get-tuple-element.48.b, f32[256,512]{1,0:T(8,128)S(1)} %get-tuple-element.69.s_first, f32[2,256,512]{2,1,0:T(8,128)S(1)} %get-tuple-element.70.s_mid, ...), custom_call_target="tpu_custom_call" | custom-call | flops 4194305 | bytes 11534337 | tf_op jit(solution)/shard_map/final_update/pallas_call | solution.py:913
  (6 shorter events, 0.0 us)
Async XLA Ops:
  0.6 3.1 %copy-start.1 = (s32[1,1,1024]{2,1,0:T(1,128)S(1)}, s32[1,1,1024]{2,1,0:T(1,128)}, u32[]{:S(2)}) copy-start(s32[1,1,1024]{2,1,0:T(1,128)} %perm.1) | copy-start | bytes 12292
  0.6 3.1 %copy-start.2 = (s32[1,1,1024]{2,1,0:T(1,128)S(1)}, s32[1,1,1024]{2,1,0:T(1,128)}, u32[]{:S(2)}) copy-start(s32[1,1,1024]{2,1,0:T(1,128)} %kind.1) | copy-start | bytes 12292
  0.7 3.1 %copy-start = (f32[4,128,128]{2,1,0:T(8,128)S(1)}, f32[4,128,128]{2,1,0:T(8,128)}, u32[]{:S(2)}) copy-start(f32[4,128,128]{2,1,0:T(8,128)} %proj.1) | copy-start | bytes 786436
  1.8 17.9 %collective-permute-start = (f32[264,512]{1,0:T(8,128)S(1)}, f32[264,512]{1,0:T(8,128)S(1)}, u32[]{:S(2)}, u32[]{:S(2)}) collective-permute-start(f32[264,512]{1,0:T(8,128)S(1)} %pack.1), channel_id=1, source_target_pairs={{4,0},{8,4},{12,8},{16,12},{20,16},{24,20},{28,24},{5,1},{9,5},{13... | collective-permute-start | bytes 1622024 | tf_op jit(solution)/shard_map/ppermute | solution.py:717
  9.5 28.7 %collective-permute-start.3 = (f32[256,512]{1,0:T(8,128)S(1)}, f32[256,512]{1,0:T(8,128)S(1)}, u32[]{:S(2)}, u32[]{:S(2)}) collective-permute-start(f32[256,512]{1,0:T(8,128)S(1)} %get-tuple-element.65), channel_id=1, source_target_pairs={{4,0},{8,4},{12,8},{16,12},{20,16},{24,20},{28,24},{5,1},{9,5},{13... | collective-permute-start | bytes 1572872 | tf_op jit(solution)/shard_map/ppermute | solution.py:717
  22.8 19.2 %collective-permute-start.4 = (f32[264,512]{1,0:T(8,128)S(1)}, f32[264,512]{1,0:T(8,128)S(1)}, u32[]{:S(2)}, u32[]{:S(2)}) collective-permute-start(f32[264,512]{1,0:T(8,128)S(1)} %back_first.1.later.back.back_before), channel_id=1, source_target_pairs={{0,4},{4,8},{8,12},{12,16},{16,20},{20,24},{24,28},{1,5},{5,9},{9,... | collective-permute-start | bytes 1622024 | tf_op jit(solution)/shard_map/ppermute | solution.py:717
  27.7 6.2 %collective-permute-start.1 = (f32[15,512]{1,0:T(8,128)S(1)}, f32[15,512]{1,0:T(8,128)S(1)}, u32[]{:S(2)}, u32[]{:S(2)}) collective-permute-start(f32[15,512]{1,0:T(8,128)S(1)} %get-tuple-element.60), channel_id=1, source_target_pairs={{0,1},{1,2},{2,3},{4,5},{5,6},{6,7},{8,9},{9,10},{10,11},{12,13},{... | collective-permute-start | bytes 92168 | tf_op jit(solution)/shard_map/ppermute | solution.py:717
  29.0 4.9 %collective-permute-start.2 = (f32[10,512]{1,0:T(8,128)S(1)}, f32[10,512]{1,0:T(8,128)S(1)}, u32[]{:S(2)}, u32[]{:S(2)}) collective-permute-start(f32[10,512]{1,0:T(8,128)S(1)} %get-tuple-element.61), channel_id=1, source_target_pairs={{1,0},{2,1},{3,2},{5,4},{6,5},{7,6},{9,8},{10,9},{11,10},{13,12},{... | collective-permute-start | bytes 61448 | tf_op jit(solution)/shard_map/ppermute | solution.py:717
  35.4 36.1 %collective-permute-start.10 = (f32[264,512]{1,0:T(8,128)S(1)}, f32[264,512]{1,0:T(8,128)S(1)}, u32[]{:S(2)}, u32[]{:S(2)}) collective-permute-start(f32[264,512]{1,0:T(8,128)S(1)} %back_second.1), channel_id=1, source_target_pairs={{0,4},{4,8},{8,12},{12,16},{16,20},{20,24},{24,28},{1,5},{5,9},{9,... | collective-permute-start | bytes 1622024 | tf_op jit(solution)/shard_map/ppermute | solution.py:717
  44.1 1.6 %collective-permute-start.5 = (f32[4,128]{1,0:T(4,128)S(1)}, f32[4,128]{1,0:T(4,128)S(1)}, u32[]{:S(2)}, u32[]{:S(2)}) collective-permute-start(f32[4,128]{1,0:T(4,128)S(1)} %get-tuple-element.74), channel_id=1, source_target_pairs={{0,1},{1,0},{2,3},{3,2},{4,5},{5,4},{6,7},{7,6},{8,9},{9,8},{10,11... | collective-permute-start | bytes 6152 | tf_op jit(solution)/shard_map/ppermute | solution.py:733
  45.7 3.0 %collective-permute-start.6 = (f32[4,128]{1,0:T(4,128)S(1)}, f32[4,128]{1,0:T(4,128)S(1)}, u32[]{:S(2)}, u32[]{:S(2)}) collective-permute-start(f32[4,128]{1,0:T(4,128)S(1)} %add.15), channel_id=1, source_target_pairs={{0,3},{1,2},{2,1},{3,0},{4,7},{5,6},{6,5},{7,4},{8,11},{9,10},{10,... | collective-permute-start | bytes 6152 | tf_op jit(solution)/shard_map/ppermute | solution.py:733
  48.8 16.7 %collective-permute-start.7 = (f32[4,128]{1,0:T(4,128)S(1)}, f32[4,128]{1,0:T(4,128)S(1)}, u32[]{:S(2)}, u32[]{:S(2)}) collective-permute-start(f32[4,128]{1,0:T(4,128)S(1)} %add.16), channel_id=1, source_target_pairs={{0,17},{1,16},{2,19},{3,18},{4,21},{5,20},{6,23},{7,22},{8,25},{9,... | collective-permute-start | bytes 6152 | tf_op jit(solution)/shard_map/ppermute | solution.py:733
  65.5 3.0 %collective-permute-start.8 = (f32[4,128]{1,0:T(4,128)S(1)}, f32[4,128]{1,0:T(4,128)S(1)}, u32[]{:S(2)}, u32[]{:S(2)}) collective-permute-start(f32[4,128]{1,0:T(4,128)S(1)} %add.17), channel_id=1, source_target_pairs={{0,9},{1,8},{2,11},{3,10},{4,13},{5,12},{6,15},{7,14},{8,1},{9,0},... | collective-permute-start | bytes 6152 | tf_op jit(solution)/shard_map/ppermute | solution.py:733
  68.5 3.0 %collective-permute-start.9 = (f32[4,128]{1,0:T(4,128)S(1)}, f32[4,128]{1,0:T(4,128)S(1)}, u32[]{:S(2)}, u32[]{:S(2)}) collective-permute-start(f32[4,128]{1,0:T(4,128)S(1)} %add.18), channel_id=1, source_target_pairs={{0,5},{1,4},{2,7},{3,6},{4,1},{5,0},{6,3},{7,2},{8,13},{9,12},{10,... | collective-permute-start | bytes 6152 | tf_op jit(solution)/shard_map/ppermute | solution.py:733

commit v4 on v3

--- a/solution.py
+++ b/solution.py
@@ -616,6 +616,10 @@
     table[...] = filled
 
 
+def add_kernel(earlier, one, other, both):
+    both[...] = one[...] + other[...]
+
+
 def final_kernel(
     tables, b, s_first, s_mid, w_last, recv, image_low, image_high, image_ends, edge_high, jump_next, recv_next, own_next, solution_hbm, residual_hbm,
     solution, residual, sems,
@@ -702,10 +706,8 @@
     return [pltpu.with_memory_space_constraint(array, pltpu.HBM) for array in arrays]
 
 
-def scaled(estimate, by):
-    return pl.CostEstimate(
-        flops=int(estimate.flops * by) + 1, bytes_accessed=int(estimate.bytes_accessed * by) + 1, transcendentals=0
-    )
+def cost(flops, size):
+    return pl.CostEstimate(flops=int(flops), bytes_accessed=int(size), transcendentals=0)
 
 
 def params(mib):
@@ -717,7 +719,7 @@
     return lax.ppermute(array, axis, [(i, i + by) for i in range(size) if 0 <= i + by < size])
 
 
-def gather_rows(table):
+def gather_rows(table, own):
     subs, blks = lax.axis_size("sub"), lax.axis_size("blk")
     steps = [(0, 1)]
     reach = 2
@@ -728,9 +730,21 @@
     while reach > 0:
         steps.append((reach, 1))
         reach //= 2
-    for by_sub, by_blk in steps:
+    for place, (by_sub, by_blk) in enumerate(steps):
         pairs = [(s * blks + t, (s ^ by_sub) * blks + (t ^ by_blk)) for s in range(subs) for t in range(blks)]
-        table = table + lax.ppermute(table, ("sub", "blk"), pairs)
+        other = lax.ppermute(table, ("sub", "blk"), pairs)
+        if place == 0:
+            (table,) = pl.pallas_call(
+                add_kernel,
+                in_specs=[VMEM] * 3,
+                out_specs=[VMEM],
+                out_shape=[held(*table.shape)],
+                compiler_params=params(2),
+                cost_estimate=cost(table.size, 12 * table.size),
+                name="add",
+            )(*near_core(own, table, other))
+        else:
+            table = table + other
     return table
 
 
@@ -740,7 +754,6 @@
     subs, blks = lax.axis_size("sub"), lax.axis_size("blk")
     steps = rows // ROWS
     cells = layers * rows * depth
-    cost = lambda flops, size: pl.CostEstimate(flops=int(flops), bytes_accessed=int(size), transcendentals=0)
 
     (face,) = pl.pallas_call(
         pack_kernel,
@@ -749,7 +762,7 @@
         out_shape=[held(rows + SUB, depth)],
         scratch_shapes=[pltpu.SemaphoreType.DMA((2,))],
         compiler_params=params(2),
-        cost_estimate=scaled(cost(0, 4 * rows * depth), 100),
+        cost_estimate=cost(0, 4 * rows * depth),
         name="pack",
     )(*in_hbm(right_side, trans_y))
     face_right = shifted(face, "sub", -1)
@@ -766,7 +779,7 @@
         ],
         scratch_shapes=[pltpu.VMEM((2, SUB, LANES), F32), pltpu.SemaphoreType.DMA((5, steps))],
         compiler_params=params(16),
-        cost_estimate=scaled(cost(20 * cells, 24 * cells), 1),
+        cost_estimate=cost(20 * cells, 24 * cells),
         name="stencil_first",
     )(
         pair_count, pair_perm, pair_type, proj,
@@ -781,7 +794,7 @@
         out_specs=[VMEM],
         out_shape=[held(split, rows, depth)],
         compiler_params=params(8),
-        cost_estimate=scaled(cost(20 * cells, 15 * cells), 0),
+        cost_estimate=cost(20 * cells, 15 * cells),
         name="stencil_second_low",
     )(*near_core(s_first, s_mid, tx, ty, tz, st))
 
@@ -792,7 +805,7 @@
         out_specs=[VMEM] * 3,
         out_shape=[held(rows, depth), held(rows, depth), held(SUB, LANES)],
         compiler_params=params(16),
-        cost_estimate=scaled(mortar_cost, 100),
+        cost_estimate=mortar_cost,
         name="jump_first",
     )(*near_core(image_low, b, face_right, s_last, picks, codes, proj_t))
     (kinds_by_block,) = pl.pallas_call(
@@ -801,7 +814,7 @@
         out_specs=[VMEM],
         out_shape=[held(SUB, depth)],
         compiler_params=params(8),
-        cost_estimate=scaled(cost(16 * blocks * blocks, 2 * blocks * blocks), 3),
+        cost_estimate=cost(16 * blocks * blocks, 2 * blocks * blocks),
         name="kinds",
     )(*near_core(code_row, picks))
     (back,) = pl.pallas_call(
@@ -810,7 +823,7 @@
         out_specs=[VMEM],
         out_shape=[held(rows + SUB, depth)],
         compiler_params=params(16),
-        cost_estimate=scaled(mortar_cost, 1),
+        cost_estimate=mortar_cost,
         name="back_first",
     )(*near_core(jump, kinds_by_block, puts, codes, proj_n))
     recv = shifted(back, "sub", 1)
@@ -823,7 +836,7 @@
         out_shape=[held(layers - split, rows, depth), held(SUB, LANES)],
         scratch_shapes=[pltpu.VMEM((6, SUB, LANES), F32)],
         compiler_params=params(8),
-        cost_estimate=scaled(cost(20 * cells, 15 * cells), 10),
+        cost_estimate=cost(20 * cells, 15 * cells),
         name="stencil_second_high",
     )(*near_core(back, first_sums, jump_sums, b, s_mid, s_last, w_last, tx, ty, tz, st))
     up_out, down_out = pl.pallas_call(
@@ -832,7 +845,7 @@
         out_specs=[VMEM] * 2,
         out_shape=[held(3 * layers + 3, depth), held(2 * layers + 2, depth)],
         compiler_params=params(2),
-        cost_estimate=scaled(cost(0, 64 * depth), 1),
+        cost_estimate=cost(0, 64 * depth),
         name="rows",
     )(*near_core(face_right, b, ty, s_first, s_mid, w_last, back))
     up = shifted(up_out, "blk", 1)
@@ -846,7 +859,7 @@
         + [held(2, depth), held(2, depth), held(layers, depth), held(layers, depth)],
         input_output_aliases={10: 0, 11: 1, 12: 2, 13: 3, 14: 4},
         compiler_params=params(4),
-        cost_estimate=scaled(cost(320 * depth, 640 * depth), 3),
+        cost_estimate=cost(320 * depth, 640 * depth),
         name="edges_first",
     )(
         *near_core(
@@ -861,7 +874,7 @@
         out_shape=[held(rows, depth), held(SUB, LANES)],
         scratch_shapes=[pltpu.VMEM((rows, depth), F32)],
         compiler_params=params(16),
-        cost_estimate=scaled(mortar_cost, 0.3),
+        cost_estimate=mortar_cost,
         name="jump_second",
     )(
         *near_core(
@@ -874,10 +887,20 @@
         out_specs=[VMEM],
         out_shape=[held(rows + SUB, depth)],
         compiler_params=params(16),
-        cost_estimate=scaled(mortar_cost, 0.3),
+        cost_estimate=mortar_cost,
         name="back_second",
     )(*near_core(w_last, missing, puts, codes, proj_n))
 
+    (back_next,) = pl.pallas_call(
+        hold_kernel,
+        in_specs=[VMEM] * 2,
+        out_specs=[VMEM],
+        out_shape=[held(rows + SUB, depth)],
+        input_output_aliases={1: 0},
+        compiler_params=params(2),
+        cost_estimate=cost(0, 8 * depth),
+        name="hold",
+    )(*near_core(second_sums, back_next))
     recv_next = shifted(back_next, "sub", 1)
 
     count = subs * blks
@@ -891,7 +914,7 @@
         input_output_aliases={17: 0},
         scratch_shapes=[pltpu.VMEM((6, SUB, LANES), F32)],
         compiler_params=params(8),
-        cost_estimate=scaled(cost(20 * cells, 15 * cells), 0.3),
+        cost_estimate=cost(20 * cells, 15 * cells),
         name="stencil_second_added",
     )(
         *near_core(
@@ -905,10 +928,10 @@
         out_specs=[VMEM],
         out_shape=[held(rows, depth)],
         compiler_params=params(16),
-        cost_estimate=scaled(mortar_cost, 1),
+        cost_estimate=mortar_cost,
         name="own_second",
     )(*near_core(s_first, recv, proj_t, proj_n))
-    tables = gather_rows(table)
+    tables = gather_rows(table, own_next)
 
     return pl.pallas_call(
         final_kernel,
@@ -917,7 +940,7 @@
         out_shape=[jax.ShapeDtypeStruct((layers, rows, depth), F32)] * 2,
         scratch_shapes=[pltpu.VMEM((layers, rows, depth), F32)] * 2 + [pltpu.SemaphoreType.DMA((2, steps))],
         compiler_params=params(8),
-        cost_estimate=scaled(cost(8 * cells, 22 * cells), 1),
+        cost_estimate=cost(8 * cells, 22 * cells),
         name="final_update",
     )(*near_core(tables, b, s_first, s_mid, w_last, recv, image_low, image_high, image_ends, edge_high, jump_next, recv_next, own_next))
 

time: 74.4 us -> 66.3 us (0.89)
  starting transfers between devices: 32.2 us -> 25.9 us
  waiting for transfers between devices: 15.3 us -> 13.3 us
    ppermute x5, starting transfers between devices: 19.4 us -> 13.1 us  [gather_rows(): other = lax.ppermute(table, ('sub', 'blk'), pairs)]
    ppermute x6, waiting for transfers between devices: 8.96 us -> 7.89 us  [shifted(): lax.ppermute(array, axis, [(i, i + by) for i in range(size) if 0 <= i + b...]
    ppermute x5, waiting for transfers between devices: 6.35 us -> 5.43 us  [gather_rows(): other = lax.ppermute(table, ('sub', 'blk'), pairs)]
  transfers between devices with their start and end apart: 11 -> 11, of which waited for: 8 -> 6; matrix products, arithmetic and copies ran while one was open for 0% -> 0% of each run, Pallas kernels for 29% -> 32%
where the time goes in v4:
time: 66.3 us; the launch traced here: 65.9 us
  starting transfers between devices  25.9 us (39%)
  Pallas kernels  25 us (38%)
  waiting for transfers between devices  13.3 us (20%)
  between operations  1.68 us (3%)
    ppermute x5, starting transfers between devices, gather_rows(): other = lax.ppermute(table, ('sub', 'blk'), pairs)  13.1 us
    ppermute x6, starting transfers between devices, shifted(): lax.ppermute(array, axis, [(i, i + by) for i in range(size) if 0 <= i + b...  12.8 us
    ppermute x6, waiting for transfers between devices, shifted(): lax.ppermute(array, axis, [(i, i + by) for i in range(size) if 0 <= i + b...  7.89 us
    pallas_call x1, Pallas kernels, body(): pl.pallas_call(first_kernel, in_specs=[SMEM] + [VMEM] * 3 + [HBM] * 5, ou...  5.76 us
    ppermute x5, waiting for transfers between devices, gather_rows(): other = lax.ppermute(table, ('sub', 'blk'), pairs)  5.43 us
    pallas_call x1, Pallas kernels, body(): pl.pallas_call(second_high_kernel, in_specs=[VMEM] * 11, out_specs=[VMEM]...  3.13 us
    pallas_call x1, Pallas kernels, body(): pl.pallas_call(final_kernel, in_specs=[VMEM] * 13, out_specs=[HBM] * 2, o...  2.46 us
    pallas_call x1, Pallas kernels, body(): pl.pallas_call(second_added_kernel, in_specs=[VMEM] * 18, out_specs=[VMEM...  2.13 us
  transfers between devices with their start and end apart: 11, of which 6 were waited for; matrix products, arithmetic and copies ran while one was open for 0% of the time, Pallas kernels for 32%

profile of v4, /device:TPU:0, one launch (start us, length us, event | category | flops | bytes accessed | tf_op | source)
XLA Modules:
  0.0 65.9 jit_solution(14356548661351804751)
XLA Ops:
  0.6 0.0 copy-start.1
  0.6 0.0 copy-start.2
  0.7 0.0 copy-start
  0.7 1.1 %pack.1 = f32[264,512]{1,0:T(8,128)S(1)} custom-call(f32[4,256,512]{2,1,0:T(8,128)} %b_hbm.3, f32[4,256,512]{2,1,0:T(8,128)} %ty_hbm.3), custom_call_target="tpu_custom_call" | custom-call | bytes 524288 | tf_op jit(solution)/shard_map/pack/pallas_call | solution.py:758
  1.8 1.3 %collective-permute-start = (f32[264,512]{1,0:T(8,128)S(1)}, f32[264,512]{1,0:T(8,128)S(1)}, u32[]{:S(2)}, u32[]{:S(2)}) collective-permute-start(f32[264,512]{1,0:T(8,128)S(1)} %pack.1), channel_id=1, source_target_pairs={{4,0},{8,4},{12,8},{16,12},{20,16},{24,20},{28,24},{5,1},{9,5},{13... | collective-permute-start | bytes 1622024 | tf_op jit(solution)/shard_map/ppermute | solution.py:719
  3.7 0.0 copy-done.1
  3.7 0.0 copy-done.2
  3.7 0.0 copy-done
  3.8 5.8 %stencil_first.1 = (f32[4,256,512]{2,1,0:T(8,128)S(1)}, f32[4,256,512]{2,1,0:T(8,128)S(1)}, f32[4,256,512]{2,1,0:T(8,128)S(1)}, f32[4,256,512]{2,1,0:T(8,128)S(1...) custom-call(s32[1,1]{1,0:T(1,128)S(6)} %copy.25.count, ...), custom_call_target="tpu_custom_call" | custom-call | flops 10485760 | bytes 12582912 | tf_op jit(solution)/shard_map/stencil_first/pallas_call | solution.py:770
  9.5 1.3 %collective-permute-start.4 = (f32[256,512]{1,0:T(8,128)S(1)}, f32[256,512]{1,0:T(8,128)S(1)}, u32[]{:S(2)}, u32[]{:S(2)}) collective-permute-start(f32[256,512]{1,0:T(8,128)S(1)} %get-tuple-element.66), channel_id=1, source_target_pairs={{4,0},{8,4},{12,8},{16,12},{20,16},{24,20},{28,24},{5,1},{9,5},{13... | collective-permute-start | bytes 1572872 | tf_op jit(solution)/shard_map/ppermute | solution.py:719
  10.8 1.9 %stencil_second_low.1.earlier.image_low_in = f32[2,256,512]{2,1,0:T(8,128)S(1)} custom-call(f32[256,512]{1,0:T(8,128)S(1)} %get-tuple-element.42.s_first.s_first_in, f32[2,256,512]{2,1,0:T(8,128)S(1)} %get-tuple-element.43.s_mid.s_mid_in, f32[4,256,512]{2,1,0:T(8,128)S(1)} %get-tuple-element.44.tx, f32[4,256,512]{2,1,0:T(8,128)S(1)} %get-tuple-element.45.ty, ...), custom_call_target="tpu_custom_call" | custom-call | flops 10485760 | bytes 7864320 | tf_op jit(solution)/shard_map/stencil_second_low/pallas_call | solution.py:791
  12.7 0.4 kinds.1.kinds_by_block
  13.1 6.6 %collective-permute-done.right.right_before = f32[264,512]{1,0:T(8,128)S(1)} collective-permute-done((f32[264,512]{1,0:T(8,128)S(1)}, f32[264,512]{1,0:T(8,128)S(1)}, u32[]{:S(2)}, u32[]{:S(2)}) %collective-permute-start) | collective-permute-done | bytes 540704 | tf_op jit(solution)/shard_map/ppermute | solution.py:719
  19.7 1.8 %jump_first.1 = (f32[256,512]{1,0:T(8,128)S(1)}, f32[256,512]{1,0:T(8,128)S(1)}, f32[8,128]{1,0:T(8,128)S(1)}) custom-call(f32[2,256,512]{2,1,0:T(8,128)S(1)} %stencil_second_low.1.earlier.image_low_in, f32[4,256,512]{2,1,0:T(8,128)S(1)} %get-tuple-element.48.b, f32[264,512]{1,0:T(8,128)S(1)} %collective-permute-done.right.right_before, ...), custom_call_target="tpu_custom_call" | custom-call | flops 939524096 | bytes 1835008 | tf_op jit(solution)/shard_map/jump_first/pallas_call | solution.py:802
  21.5 1.3 %back_first.1.later.back.back_before = f32[264,512]{1,0:T(8,128)S(1)} custom-call(f32[256,512]{1,0:T(8,128)S(1)} %get-tuple-element.53.jump, f32[8,512]{1,0:T(8,128)S(1)} %kinds.1.kinds_by_block, bf16[1024,1024]{1,0:T(8,128)(2,1)S(1)} %get-tuple-element.55.puts, s32[1024,128]{1,0:T(8,128)S(1)} %get-tuple-element.51.codes, ...), custom_call_target="tpu_custom_call" | custom-call | flops 939524096 | bytes 1835008 | tf_op jit(solution)/shard_map/back_first/pallas_call | solution.py:820
  22.8 1.3 %collective-permute-start.1 = (f32[15,512]{1,0:T(8,128)S(1)}, f32[15,512]{1,0:T(8,128)S(1)}, u32[]{:S(2)}, u32[]{:S(2)}) collective-permute-start(f32[15,512]{1,0:T(8,128)S(1)} %get-tuple-element.60), channel_id=1, source_target_pairs={{0,1},{1,2},{2,3},{4,5},{5,6},{6,7},{8,9},{9,10},{10,11},{12,13},{... | collective-permute-start | bytes 92168 | tf_op jit(solution)/shard_map/ppermute | solution.py:719
  24.1 1.3 %collective-permute-start.2 = (f32[10,512]{1,0:T(8,128)S(1)}, f32[10,512]{1,0:T(8,128)S(1)}, u32[]{:S(2)}, u32[]{:S(2)}) collective-permute-start(f32[10,512]{1,0:T(8,128)S(1)} %get-tuple-element.61), channel_id=1, source_target_pairs={{1,0},{2,1},{3,2},{5,4},{6,5},{7,6},{9,8},{10,9},{11,10},{13,12},{... | collective-permute-start | bytes 61448 | tf_op jit(solution)/shard_map/ppermute | solution.py:719
  25.4 4.9 %collective-permute-start.3 = (f32[264,512]{1,0:T(8,128)S(1)}, f32[264,512]{1,0:T(8,128)S(1)}, u32[]{:S(2)}, u32[]{:S(2)}) collective-permute-start(f32[264,512]{1,0:T(8,128)S(1)} %back_first.1.later.back.back_before), channel_id=1, source_target_pairs={{0,4},{4,8},{8,12},{12,16},{16,20},{20,24},{24,28},{1,5},{5,9},{9,... | collective-permute-start | bytes 1622024 | tf_op jit(solution)/shard_map/ppermute | solution.py:719
  30.3 3.1 %stencil_second_high.1 = (f32[2,256,512]{2,1,0:T(8,128)S(1)}, f32[8,128]{1,0:T(8,128)S(1)}) custom-call(f32[264,512]{1,0:T(8,128)S(1)} %back_first.1.later.back.back_before, f32[8,128]{1,0:T(8,128)S(1)} %get-tuple-element.41.first_sums.sums_in, f32[8,128]{1,0:T(8,128)S(1)} %get-tuple-element.57.jump_sums, f32[4,256,512]{2,1,0:T(8,128)S(1)} %get-tuple-element.48.b, ...), custom_call_target="tpu_custom_call" | custom-call | flops 10485760 | bytes 7864320 | tf_op jit(solution)/shard_map/stencil_second_high/pallas_call | solution.py:832
  33.4 0.0 collective-permute-done.2.down
  33.4 0.0 collective-permute-done.1.up
  33.4 0.3 edges_first.1
  33.8 1.3 %back_second.1.back_in = f32[264,512]{1,0:T(8,128)S(1)} custom-call(f32[256,512]{1,0:T(8,128)S(1)} %get-tuple-element.65.w_last, f32[2,512]{1,0:T(2,128)S(1)} %get-tuple-element.68.missing, bf16[1024,1024]{1,0:T(8,128)(2,1)S(1)} %get-tuple-element.55.puts, s32[1024,128]{1,0:T(8,128)S(1)} %get-tuple-element.51.codes, ...), custom_call_target="tpu_custom_call" | custom-call | flops 939524096 | bytes 1835008 | tf_op jit(solution)/shard_map/back_second/pallas_call | solution.py:884
  35.0 0.0 collective-permute-done.4.right
  35.1 1.8 %jump_second.1 = (f32[256,512]{1,0:T(8,128)S(1)}, f32[8,128]{1,0:T(8,128)S(1)}) custom-call(f32[8,128]{1,0:T(8,128)S(1)} %get-tuple-element.59.near_sums.high_sums, f32[256,512]{1,0:T(8,128)S(1)} %get-tuple-element.65.w_last, f32[256,512]{1,0:T(8,128)S(1)} %get-tuple-element.53.jump, f32[264,512]{1,0:T(8,128)S(1)} %collective-permute-done.right.right_before, ...), custom_call_target="tpu_custom_call" | custom-call | flops 939524096 | bytes 1835008 | tf_op jit(solution)/shard_map/jump_second/pallas_call | solution.py:870
  36.9 2.7 %collective-permute-start.10 = (f32[264,512]{1,0:T(8,128)S(1)}, f32[264,512]{1,0:T(8,128)S(1)}, u32[]{:S(2)}, u32[]{:S(2)}) collective-permute-start(f32[264,512]{1,0:T(8,128)S(1)} %hold.1), channel_id=1, source_target_pairs={{0,4},{4,8},{8,12},{12,16},{16,20},{20,24},{24,28},{1,5},{5,9},{9,... | collective-permute-start | bytes 1622024 | tf_op jit(solution)/shard_map/ppermute | solution.py:719
  39.7 1.2 %collective-permute-done.3.recv = f32[264,512]{1,0:T(8,128)S(1)} collective-permute-done((f32[264,512]{1,0:T(8,128)S(1)}, f32[264,512]{1,0:T(8,128)S(1)}, u32[]{:S(2)}, u32[]{:S(2)}) %collective-permute-start.3) | collective-permute-done | bytes 540704 | tf_op jit(solution)/shard_map/ppermute | solution.py:719
  40.9 2.1 %stencil_second_added.1 = (f32[2,256,512]{2,1,0:T(8,128)S(1)}, f32[4,512]{1,0:T(4,128)S(1)}, f32[4,128]{1,0:T(4,128)S(1)}) custom-call(f32[8,128]{1,0:T(8,128)S(1)} %get-tuple-element.63.first_sums, f32[8,128]{1,0:T(8,128)S(1)} %get-tuple-element.57.jump_sums, f32[8,128]{1,0:T(8,128)S(1)} %get-tuple-element.59.near_sums.high_sums, ...), custom_call_target="tpu_custom_call", output_to_operand_aliasing={{0}: (17, {})} | custom-call | flops 10485760 | bytes 7864320 | tf_op jit(solution)/shard_map/stencil_second_added/pallas_call | solution.py:907
  43.0 4.1 %collective-permute-start.5 = (f32[4,128]{1,0:T(4,128)S(1)}, f32[4,128]{1,0:T(4,128)S(1)}, u32[]{:S(2)}, u32[]{:S(2)}) collective-permute-start(f32[4,128]{1,0:T(4,128)S(1)} %get-tuple-element.74.one), channel_id=1, source_target_pairs={{0,1},{1,0},{2,3},{3,2},{4,5},{5,4},{6,7},{7,6},{8,9},{9,8},{10,11... | collective-permute-start | bytes 6152 | tf_op jit(solution)/shard_map/ppermute | solution.py:735
  47.2 1.6 %own_second.1.earlier.own_next = f32[256,512]{1,0:T(8,128)S(1)} custom-call(f32[256,512]{1,0:T(8,128)S(1)} %get-tuple-element.62.s_first, f32[264,512]{1,0:T(8,128)S(1)} %collective-permute-done.3.recv, bf16[512,256]{1,0:T(8,128)(2,1)S(1)} %get-tuple-element.52.proj_t, bf16[512,256]{1,0:T(8,128)(2,1)S(1)} %get-tuple-element.56.proj_n), custom_call_target="tpu_custom_call" | custom-call | flops 939524096 | bytes 1835008 | tf_op jit(solution)/shard_map/own_second/pallas_call | solution.py:925
  48.8 0.0 collective-permute-done.5.other
  48.8 2.7 %collective-permute-start.6 = (f32[4,128]{1,0:T(4,128)S(1)}, f32[4,128]{1,0:T(4,128)S(1)}, u32[]{:S(2)}, u32[]{:S(2)}) collective-permute-start(f32[4,128]{1,0:T(4,128)S(1)} %add.17), channel_id=1, source_target_pairs={{0,3},{1,2},{2,1},{3,0},{4,7},{5,6},{6,5},{7,4},{8,11},{9,10},{10,... | collective-permute-start | bytes 6152 | tf_op jit(solution)/shard_map/ppermute | solution.py:735
  51.5 1.3 %collective-permute-done.6 = f32[4,128]{1,0:T(4,128)S(1)} collective-permute-done((f32[4,128]{1,0:T(4,128)S(1)}, f32[4,128]{1,0:T(4,128)S(1)}, u32[]{:S(2)}, u32[]{:S(2)}) %collective-permute-start.6) | collective-permute-done | bytes 2080 | tf_op jit(solution)/shard_map/ppermute | solution.py:735
  52.8 2.4 %collective-permute-start.7 = (f32[4,128]{1,0:T(4,128)S(1)}, f32[4,128]{1,0:T(4,128)S(1)}, u32[]{:S(2)}, u32[]{:S(2)}) collective-permute-start(f32[4,128]{1,0:T(4,128)S(1)} %add.13), channel_id=1, source_target_pairs={{0,17},{1,16},{2,19},{3,18},{4,21},{5,20},{6,23},{7,22},{8,25},{9,... | collective-permute-start | bytes 6152 | tf_op jit(solution)/shard_map/ppermute | solution.py:735
  55.3 1.5 %collective-permute-done.7 = f32[4,128]{1,0:T(4,128)S(1)} collective-permute-done((f32[4,128]{1,0:T(4,128)S(1)}, f32[4,128]{1,0:T(4,128)S(1)}, u32[]{:S(2)}, u32[]{:S(2)}) %collective-permute-start.7) | collective-permute-done | bytes 2080 | tf_op jit(solution)/shard_map/ppermute | solution.py:735
  56.7 2.2 %collective-permute-start.8 = (f32[4,128]{1,0:T(4,128)S(1)}, f32[4,128]{1,0:T(4,128)S(1)}, u32[]{:S(2)}, u32[]{:S(2)}) collective-permute-start(f32[4,128]{1,0:T(4,128)S(1)} %add.14), channel_id=1, source_target_pairs={{0,9},{1,8},{2,11},{3,10},{4,13},{5,12},{6,15},{7,14},{8,1},{9,0},... | collective-permute-start | bytes 6152 | tf_op jit(solution)/shard_map/ppermute | solution.py:735
  59.0 1.3 %collective-permute-done.8 = f32[4,128]{1,0:T(4,128)S(1)} collective-permute-done((f32[4,128]{1,0:T(4,128)S(1)}, f32[4,128]{1,0:T(4,128)S(1)}, u32[]{:S(2)}, u32[]{:S(2)}) %collective-permute-start.8) | collective-permute-done | bytes 2080 | tf_op jit(solution)/shard_map/ppermute | solution.py:735
  60.3 1.7 %collective-permute-start.9 = (f32[4,128]{1,0:T(4,128)S(1)}, f32[4,128]{1,0:T(4,128)S(1)}, u32[]{:S(2)}, u32[]{:S(2)}) collective-permute-start(f32[4,128]{1,0:T(4,128)S(1)} %add.15), channel_id=1, source_target_pairs={{0,5},{1,4},{2,7},{3,6},{4,1},{5,0},{6,3},{7,2},{8,13},{9,12},{10,... | collective-permute-start | bytes 6152 | tf_op jit(solution)/shard_map/ppermute | solution.py:735
  61.9 1.3 %collective-permute-done.9 = f32[4,128]{1,0:T(4,128)S(1)} collective-permute-done((f32[4,128]{1,0:T(4,128)S(1)}, f32[4,128]{1,0:T(4,128)S(1)}, u32[]{:S(2)}, u32[]{:S(2)}) %collective-permute-start.9) | collective-permute-done | bytes 2080 | tf_op jit(solution)/shard_map/ppermute | solution.py:735
  63.3 0.0 collective-permute-done.10.recv_next
  63.3 2.5 %final_update.1 = (f32[4,256,512]{2,1,0:T(8,128)}, f32[4,256,512]{2,1,0:T(8,128)}) custom-call(f32[4,128]{1,0:T(4,128)S(1)} %add.16.tables, f32[4,256,512]{2,1,0:T(8,128)S(1)} %get-tuple-element.48.b, f32[256,512]{1,0:T(8,128)S(1)} %get-tuple-element.62.s_first, f32[2,256,512]{2,1,0:T(8,128)S(1)} %get-tuple-element.70.s_mid, ...), custom_call_target="tpu_custom_call" | custom-call | flops 4194304 | bytes 11534336 | tf_op jit(solution)/shard_map/final_update/pallas_call | solution.py:936
  (7 shorter events, 0.0 us)
Async XLA Ops:
  0.6 3.1 %copy-start.1 = (s32[1,1,1024]{2,1,0:T(1,128)S(1)}, s32[1,1,1024]{2,1,0:T(1,128)}, u32[]{:S(2)}) copy-start(s32[1,1,1024]{2,1,0:T(1,128)} %perm.1) | copy-start | bytes 12292
  0.6 3.1 %copy-start.2 = (s32[1,1,1024]{2,1,0:T(1,128)S(1)}, s32[1,1,1024]{2,1,0:T(1,128)}, u32[]{:S(2)}) copy-start(s32[1,1,1024]{2,1,0:T(1,128)} %kind.1) | copy-start | bytes 12292
  0.7 3.1 %copy-start = (f32[4,128,128]{2,1,0:T(8,128)S(1)}, f32[4,128,128]{2,1,0:T(8,128)}, u32[]{:S(2)}) copy-start(f32[4,128,128]{2,1,0:T(8,128)} %proj.1) | copy-start | bytes 786436
  1.8 17.9 %collective-permute-start = (f32[264,512]{1,0:T(8,128)S(1)}, f32[264,512]{1,0:T(8,128)S(1)}, u32[]{:S(2)}, u32[]{:S(2)}) collective-permute-start(f32[264,512]{1,0:T(8,128)S(1)} %pack.1), channel_id=1, source_target_pairs={{4,0},{8,4},{12,8},{16,12},{20,16},{24,20},{28,24},{5,1},{9,5},{13... | collective-permute-start | bytes 1622024 | tf_op jit(solution)/shard_map/ppermute | solution.py:719
  9.5 25.5 %collective-permute-start.4 = (f32[256,512]{1,0:T(8,128)S(1)}, f32[256,512]{1,0:T(8,128)S(1)}, u32[]{:S(2)}, u32[]{:S(2)}) collective-permute-start(f32[256,512]{1,0:T(8,128)S(1)} %get-tuple-element.66), channel_id=1, source_target_pairs={{4,0},{8,4},{12,8},{16,12},{20,16},{24,20},{28,24},{5,1},{9,5},{13... | collective-permute-start | bytes 1572872 | tf_op jit(solution)/shard_map/ppermute | solution.py:719
  22.8 10.6 %collective-permute-start.1 = (f32[15,512]{1,0:T(8,128)S(1)}, f32[15,512]{1,0:T(8,128)S(1)}, u32[]{:S(2)}, u32[]{:S(2)}) collective-permute-start(f32[15,512]{1,0:T(8,128)S(1)} %get-tuple-element.60), channel_id=1, source_target_pairs={{0,1},{1,2},{2,3},{4,5},{5,6},{6,7},{8,9},{9,10},{10,11},{12,13},{... | collective-permute-start | bytes 92168 | tf_op jit(solution)/shard_map/ppermute | solution.py:719
  24.1 9.3 %collective-permute-start.2 = (f32[10,512]{1,0:T(8,128)S(1)}, f32[10,512]{1,0:T(8,128)S(1)}, u32[]{:S(2)}, u32[]{:S(2)}) collective-permute-start(f32[10,512]{1,0:T(8,128)S(1)} %get-tuple-element.61), channel_id=1, source_target_pairs={{1,0},{2,1},{3,2},{5,4},{6,5},{7,6},{9,8},{10,9},{11,10},{13,12},{... | collective-permute-start | bytes 61448 | tf_op jit(solution)/shard_map/ppermute | solution.py:719
  25.4 15.5 %collective-permute-start.3 = (f32[264,512]{1,0:T(8,128)S(1)}, f32[264,512]{1,0:T(8,128)S(1)}, u32[]{:S(2)}, u32[]{:S(2)}) collective-permute-start(f32[264,512]{1,0:T(8,128)S(1)} %back_first.1.later.back.back_before), channel_id=1, source_target_pairs={{0,4},{4,8},{8,12},{12,16},{16,20},{20,24},{24,28},{1,5},{5,9},{9,... | collective-permute-start | bytes 1622024 | tf_op jit(solution)/shard_map/ppermute | solution.py:719
  36.9 26.4 %collective-permute-start.10 = (f32[264,512]{1,0:T(8,128)S(1)}, f32[264,512]{1,0:T(8,128)S(1)}, u32[]{:S(2)}, u32[]{:S(2)}) collective-permute-start(f32[264,512]{1,0:T(8,128)S(1)} %hold.1), channel_id=1, source_target_pairs={{0,4},{4,8},{8,12},{12,16},{16,20},{20,24},{24,28},{1,5},{5,9},{9,... | collective-permute-start | bytes 1622024 | tf_op jit(solution)/shard_map/ppermute | solution.py:719
  43.0 5.8 %collective-permute-start.5 = (f32[4,128]{1,0:T(4,128)S(1)}, f32[4,128]{1,0:T(4,128)S(1)}, u32[]{:S(2)}, u32[]{:S(2)}) collective-permute-start(f32[4,128]{1,0:T(4,128)S(1)} %get-tuple-element.74.one), channel_id=1, source_target_pairs={{0,1},{1,0},{2,3},{3,2},{4,5},{5,4},{6,7},{7,6},{8,9},{9,8},{10,11... | collective-permute-start | bytes 6152 | tf_op jit(solution)/shard_map/ppermute | solution.py:735
  48.8 4.0 %collective-permute-start.6 = (f32[4,128]{1,0:T(4,128)S(1)}, f32[4,128]{1,0:T(4,128)S(1)}, u32[]{:S(2)}, u32[]{:S(2)}) collective-permute-start(f32[4,128]{1,0:T(4,128)S(1)} %add.17), channel_id=1, source_target_pairs={{0,3},{1,2},{2,1},{3,0},{4,7},{5,6},{6,5},{7,4},{8,11},{9,10},{10,... | collective-permute-start | bytes 6152 | tf_op jit(solution)/shard_map/ppermute | solution.py:735
  52.8 3.9 %collective-permute-start.7 = (f32[4,128]{1,0:T(4,128)S(1)}, f32[4,128]{1,0:T(4,128)S(1)}, u32[]{:S(2)}, u32[]{:S(2)}) collective-permute-start(f32[4,128]{1,0:T(4,128)S(1)} %add.13), channel_id=1, source_target_pairs={{0,17},{1,16},{2,19},{3,18},{4,21},{5,20},{6,23},{7,22},{8,25},{9,... | collective-permute-start | bytes 6152 | tf_op jit(solution)/shard_map/ppermute | solution.py:735
  56.7 3.5 %collective-permute-start.8 = (f32[4,128]{1,0:T(4,128)S(1)}, f32[4,128]{1,0:T(4,128)S(1)}, u32[]{:S(2)}, u32[]{:S(2)}) collective-permute-start(f32[4,128]{1,0:T(4,128)S(1)} %add.14), channel_id=1, source_target_pairs={{0,9},{1,8},{2,11},{3,10},{4,13},{5,12},{6,15},{7,14},{8,1},{9,0},... | collective-permute-start | bytes 6152 | tf_op jit(solution)/shard_map/ppermute | solution.py:735
  60.3 3.0 %collective-permute-start.9 = (f32[4,128]{1,0:T(4,128)S(1)}, f32[4,128]{1,0:T(4,128)S(1)}, u32[]{:S(2)}, u32[]{:S(2)}) collective-permute-start(f32[4,128]{1,0:T(4,128)S(1)} %add.15), channel_id=1, source_target_pairs={{0,5},{1,4},{2,7},{3,6},{4,1},{5,0},{6,3},{7,2},{8,13},{9,12},{10,... | collective-permute-start | bytes 6152 | tf_op jit(solution)/shard_map/ppermute | solution.py:735

commit v5 on v4

--- a/solution.py
+++ b/solution.py
@@ -432,7 +432,12 @@
         own[:, part] = penalty * apply_proj(codes, *two_parts(projected), proj_n, kinds, width)
 
 
-def hold_kernel(later, back_in, back):
+def wait_kernel(earlier, back_in, back):
+    last = pl.ds(back.shape[0] - SUB, SUB)
+    back[last, :] = back_in[last, :]
+
+
+def hold_kernel(later, much_later, back_in, back):
     back[back.shape[0] - SUB + 2 :, :] = jnp.zeros((SUB - 2, back.shape[1]), F32)
 
 
@@ -826,7 +831,6 @@
         cost_estimate=mortar_cost,
         name="back_first",
     )(*near_core(jump, kinds_by_block, puts, codes, proj_n))
-    recv = shifted(back, "sub", 1)
 
     split = layers // 2
     image_high, high_sums = pl.pallas_call(
@@ -848,6 +852,17 @@
         cost_estimate=cost(0, 64 * depth),
         name="rows",
     )(*near_core(face_right, b, ty, s_first, s_mid, w_last, back))
+    (back,) = pl.pallas_call(
+        wait_kernel,
+        in_specs=[VMEM] * 2,
+        out_specs=[VMEM],
+        out_shape=[held(rows + SUB, depth)],
+        input_output_aliases={1: 0},
+        compiler_params=params(2),
+        cost_estimate=cost(0, 8 * depth),
+        name="wait",
+    )(*near_core(up_out, back))
+    recv = shifted(back, "sub", 1)
     up = shifted(up_out, "blk", 1)
     down = shifted(down_out, "blk", -1)
     s_first, s_mid, s_last, w_last, image_low, edge_sums, image_ends, ends_sums, right_edges, missing, w_up, w_down = pl.pallas_call(
@@ -893,14 +908,14 @@
 
     (back_next,) = pl.pallas_call(
         hold_kernel,
-        in_specs=[VMEM] * 2,
+        in_specs=[VMEM] * 3,
         out_specs=[VMEM],
         out_shape=[held(rows + SUB, depth)],
-        input_output_aliases={1: 0},
+        input_output_aliases={2: 0},
         compiler_params=params(2),
         cost_estimate=cost(0, 8 * depth),
         name="hold",
-    )(*near_core(second_sums, back_next))
+    )(*near_core(second_sums, recv, back_next))
     recv_next = shifted(back_next, "sub", 1)
 
     count = subs * blks

time: 66.3 us -> 67.5 us (1.018)
  waiting for transfers between devices: 13.3 us -> 16.9 us
  starting transfers between devices: 25.9 us -> 23.6 us
    ppermute x5, starting transfers between devices: 13.1 us -> 8.98 us  [gather_rows(): other = lax.ppermute(table, ('sub', 'blk'), pairs)]
    ppermute x6, waiting for transfers between devices: 7.89 us -> 11.6 us  [shifted(): lax.ppermute(array, axis, [(i, i + by) for i in range(size) if 0 <= i + b...]
    ppermute x6, starting transfers between devices: 12.8 us -> 14.6 us  [shifted(): lax.ppermute(array, axis, [(i, i + by) for i in range(size) if 0 <= i + b...]
  transfers between devices with their start and end apart: 11 -> 11, of which waited for: 6 -> 7; matrix products, arithmetic and copies ran while one was open for 0% -> 0% of each run, Pallas kernels for 32% -> 32%
where the time goes in v5:
time: 67.5 us; the launch traced here: 67.2 us
  Pallas kernels  25 us (37%)
  starting transfers between devices  23.6 us (35%)
  waiting for transfers between devices  16.9 us (25%)
  between operations  1.67 us (2%)
    ppermute x6, starting transfers between devices, shifted(): lax.ppermute(array, axis, [(i, i + by) for i in range(size) if 0 <= i + b...  14.6 us
    ppermute x6, waiting for transfers between devices, shifted(): lax.ppermute(array, axis, [(i, i + by) for i in range(size) if 0 <= i + b...  11.6 us
    ppermute x5, starting transfers between devices, gather_rows(): other = lax.ppermute(table, ('sub', 'blk'), pairs)  8.98 us
    pallas_call x1, Pallas kernels, body(): pl.pallas_call(first_kernel, in_specs=[SMEM] + [VMEM] * 3 + [HBM] * 5, ou...  5.76 us
    ppermute x5, waiting for transfers between devices, gather_rows(): other = lax.ppermute(table, ('sub', 'blk'), pairs)  5.32 us
    pallas_call x1, Pallas kernels, body(): pl.pallas_call(second_high_kernel, in_specs=[VMEM] * 11, out_specs=[VMEM]...  3.13 us
    pallas_call x1, Pallas kernels, body(): pl.pallas_call(final_kernel, in_specs=[VMEM] * 13, out_specs=[HBM] * 2, o...  2.46 us
    pallas_call x1, Pallas kernels, body(): pl.pallas_call(second_added_kernel, in_specs=[VMEM] * 18, out_specs=[VMEM...  2.13 us
  transfers between devices with their start and end apart: 11, of which 7 were waited for; matrix products, arithmetic and copies ran while one was open for 0% of the time, Pallas kernels for 32%

profile of v5, /device:TPU:0, one launch (start us, length us, event | category | flops | bytes accessed | tf_op | source)
XLA Modules:
  0.0 67.2 jit_solution(17076094219758323223)
XLA Ops:
  0.6 0.0 copy-start
  0.6 0.0 copy-start.2
  0.7 0.0 copy-start.1
  0.7 1.1 %pack.1 = f32[264,512]{1,0:T(8,128)S(1)} custom-call(f32[4,256,512]{2,1,0:T(8,128)} %b_hbm.3, f32[4,256,512]{2,1,0:T(8,128)} %ty_hbm.3), custom_call_target="tpu_custom_call" | custom-call | bytes 524288 | tf_op jit(solution)/shard_map/pack/pallas_call | solution.py:763
  1.8 1.3 %collective-permute-start = (f32[264,512]{1,0:T(8,128)S(1)}, f32[264,512]{1,0:T(8,128)S(1)}, u32[]{:S(2)}, u32[]{:S(2)}) collective-permute-start(f32[264,512]{1,0:T(8,128)S(1)} %pack.1), channel_id=1, source_target_pairs={{4,0},{8,4},{12,8},{16,12},{20,16},{24,20},{28,24},{5,1},{9,5},{13... | collective-permute-start | bytes 1622024 | tf_op jit(solution)/shard_map/ppermute | solution.py:724
  3.7 0.0 copy-done
  3.7 0.0 copy-done.2
  3.7 0.0 copy-done.1
  3.7 5.8 %stencil_first.1 = (f32[4,256,512]{2,1,0:T(8,128)S(1)}, f32[4,256,512]{2,1,0:T(8,128)S(1)}, f32[4,256,512]{2,1,0:T(8,128)S(1)}, f32[4,256,512]{2,1,0:T(8,128)S(1...) custom-call(s32[1,1]{1,0:T(1,128)S(6)} %copy.27.count, ...), custom_call_target="tpu_custom_call" | custom-call | flops 10485760 | bytes 12582912 | tf_op jit(solution)/shard_map/stencil_first/pallas_call | solution.py:775
  9.5 1.3 %collective-permute-start.4 = (f32[256,512]{1,0:T(8,128)S(1)}, f32[256,512]{1,0:T(8,128)S(1)}, u32[]{:S(2)}, u32[]{:S(2)}) collective-permute-start(f32[256,512]{1,0:T(8,128)S(1)} %get-tuple-element.66), channel_id=1, source_target_pairs={{4,0},{8,4},{12,8},{16,12},{20,16},{24,20},{28,24},{5,1},{9,5},{13... | collective-permute-start | bytes 1572872 | tf_op jit(solution)/shard_map/ppermute | solution.py:724
  10.8 1.9 %stencil_second_low.1.earlier.image_low_in = f32[2,256,512]{2,1,0:T(8,128)S(1)} custom-call(f32[256,512]{1,0:T(8,128)S(1)} %get-tuple-element.42.s_first.s_first_in, f32[2,256,512]{2,1,0:T(8,128)S(1)} %get-tuple-element.43.s_mid.s_mid_in, f32[4,256,512]{2,1,0:T(8,128)S(1)} %get-tuple-element.44.tx, f32[4,256,512]{2,1,0:T(8,128)S(1)} %get-tuple-element.45.ty, ...), custom_call_target="tpu_custom_call" | custom-call | flops 10485760 | bytes 7864320 | tf_op jit(solution)/shard_map/stencil_second_low/pallas_call | solution.py:796
  12.7 0.4 kinds.1.kinds_by_block
  13.1 6.6 %collective-permute-done.right.right_before = f32[264,512]{1,0:T(8,128)S(1)} collective-permute-done((f32[264,512]{1,0:T(8,128)S(1)}, f32[264,512]{1,0:T(8,128)S(1)}, u32[]{:S(2)}, u32[]{:S(2)}) %collective-permute-start) | collective-permute-done | bytes 540704 | tf_op jit(solution)/shard_map/ppermute | solution.py:724
  19.7 1.8 %jump_first.1 = (f32[256,512]{1,0:T(8,128)S(1)}, f32[256,512]{1,0:T(8,128)S(1)}, f32[8,128]{1,0:T(8,128)S(1)}) custom-call(f32[2,256,512]{2,1,0:T(8,128)S(1)} %stencil_second_low.1.earlier.image_low_in, f32[4,256,512]{2,1,0:T(8,128)S(1)} %get-tuple-element.48.b, f32[264,512]{1,0:T(8,128)S(1)} %collective-permute-done.right.right_before, ...), custom_call_target="tpu_custom_call" | custom-call | flops 939524096 | bytes 1835008 | tf_op jit(solution)/shard_map/jump_first/pallas_call | solution.py:807
  21.5 1.3 %back_first.1.later.back.back_in = f32[264,512]{1,0:T(8,128)S(1)} custom-call(f32[256,512]{1,0:T(8,128)S(1)} %get-tuple-element.53.jump, f32[8,512]{1,0:T(8,128)S(1)} %kinds.1.kinds_by_block, bf16[1024,1024]{1,0:T(8,128)(2,1)S(1)} %get-tuple-element.55.puts, s32[1024,128]{1,0:T(8,128)S(1)} %get-tuple-element.51.codes, ...), custom_call_target="tpu_custom_call" | custom-call | flops 939524096 | bytes 1835008 | tf_op jit(solution)/shard_map/back_first/pallas_call | solution.py:825
  22.8 3.1 %stencil_second_high.1 = (f32[2,256,512]{2,1,0:T(8,128)S(1)}, f32[8,128]{1,0:T(8,128)S(1)}) custom-call(f32[264,512]{1,0:T(8,128)S(1)} %back_first.1.later.back.back_in, f32[8,128]{1,0:T(8,128)S(1)} %get-tuple-element.41.first_sums.sums_in, f32[8,128]{1,0:T(8,128)S(1)} %get-tuple-element.57.jump_sums, f32[4,256,512]{2,1,0:T(8,128)S(1)} %get-tuple-element.48.b, ...), custom_call_target="tpu_custom_call" | custom-call | flops 10485760 | bytes 7864320 | tf_op jit(solution)/shard_map/stencil_second_high/pallas_call | solution.py:836
  25.9 4.9 %collective-permute-start.3 = (f32[264,512]{1,0:T(8,128)S(1)}, f32[264,512]{1,0:T(8,128)S(1)}, u32[]{:S(2)}, u32[]{:S(2)}) collective-permute-start(f32[264,512]{1,0:T(8,128)S(1)} %wait.1.back_before), channel_id=1, source_target_pairs={{0,4},{4,8},{8,12},{12,16},{16,20},{20,24},{24,28},{1,5},{5,9},{9,... | collective-permute-start | bytes 1622024 | tf_op jit(solution)/shard_map/ppermute | solution.py:724
  30.8 1.3 %collective-permute-start.1 = (f32[15,512]{1,0:T(8,128)S(1)}, f32[15,512]{1,0:T(8,128)S(1)}, u32[]{:S(2)}, u32[]{:S(2)}) collective-permute-start(f32[15,512]{1,0:T(8,128)S(1)} %get-tuple-element.60.earlier), channel_id=1, source_target_pairs={{0,1},{1,2},{2,3},{4,5},{5,6},{6,7},{8,9},{9,10},{10,11},{12,13},{... | collective-permute-start | bytes 92168 | tf_op jit(solution)/shard_map/ppermute | solution.py:724
  32.1 1.3 %collective-permute-start.2 = (f32[10,512]{1,0:T(8,128)S(1)}, f32[10,512]{1,0:T(8,128)S(1)}, u32[]{:S(2)}, u32[]{:S(2)}) collective-permute-start(f32[10,512]{1,0:T(8,128)S(1)} %get-tuple-element.61), channel_id=1, source_target_pairs={{1,0},{2,1},{3,2},{5,4},{6,5},{7,6},{9,8},{10,9},{11,10},{13,12},{... | collective-permute-start | bytes 61448 | tf_op jit(solution)/shard_map/ppermute | solution.py:724
  33.4 3.6 %collective-permute-done.2.down = f32[10,512]{1,0:T(8,128)S(1)} collective-permute-done((f32[10,512]{1,0:T(8,128)S(1)}, f32[10,512]{1,0:T(8,128)S(1)}, u32[]{:S(2)}, u32[]{:S(2)}) %collective-permute-start.2) | collective-permute-done | bytes 20512 | tf_op jit(solution)/shard_map/ppermute | solution.py:724
  37.0 0.0 collective-permute-done.1.up
  37.0 0.3 edges_first.1
  37.3 1.3 %back_second.1.back_in = f32[264,512]{1,0:T(8,128)S(1)} custom-call(f32[256,512]{1,0:T(8,128)S(1)} %get-tuple-element.65.w_last, f32[2,512]{1,0:T(2,128)S(1)} %get-tuple-element.68.missing, bf16[1024,1024]{1,0:T(8,128)(2,1)S(1)} %get-tuple-element.55.puts, s32[1024,128]{1,0:T(8,128)S(1)} %get-tuple-element.51.codes, ...), custom_call_target="tpu_custom_call" | custom-call | flops 939524096 | bytes 1835008 | tf_op jit(solution)/shard_map/back_second/pallas_call | solution.py:899
  38.6 0.0 collective-permute-done.4.right
  38.6 1.8 %jump_second.1 = (f32[256,512]{1,0:T(8,128)S(1)}, f32[8,128]{1,0:T(8,128)S(1)}) custom-call(f32[8,128]{1,0:T(8,128)S(1)} %get-tuple-element.59.near_sums.high_sums, f32[256,512]{1,0:T(8,128)S(1)} %get-tuple-element.65.w_last, f32[256,512]{1,0:T(8,128)S(1)} %get-tuple-element.53.jump, f32[264,512]{1,0:T(8,128)S(1)} %collective-permute-done.right.right_before, ...), custom_call_target="tpu_custom_call" | custom-call | flops 939524096 | bytes 1835008 | tf_op jit(solution)/shard_map/jump_second/pallas_call | solution.py:885
  40.4 1.4 %collective-permute-done.3.recv.much_later = f32[264,512]{1,0:T(8,128)S(1)} collective-permute-done((f32[264,512]{1,0:T(8,128)S(1)}, f32[264,512]{1,0:T(8,128)S(1)}, u32[]{:S(2)}, u32[]{:S(2)}) %collective-permute-start.3) | collective-permute-done | bytes 540704 | tf_op jit(solution)/shard_map/ppermute | solution.py:724
  41.9 4.6 %collective-permute-start.10 = (f32[264,512]{1,0:T(8,128)S(1)}, f32[264,512]{1,0:T(8,128)S(1)}, u32[]{:S(2)}, u32[]{:S(2)}) collective-permute-start(f32[264,512]{1,0:T(8,128)S(1)} %hold.1), channel_id=1, source_target_pairs={{0,4},{4,8},{8,12},{12,16},{16,20},{20,24},{24,28},{1,5},{5,9},{9,... | collective-permute-start | bytes 1622024 | tf_op jit(solution)/shard_map/ppermute | solution.py:724
  46.5 2.1 %stencil_second_added.1 = (f32[2,256,512]{2,1,0:T(8,128)S(1)}, f32[4,512]{1,0:T(4,128)S(1)}, f32[4,128]{1,0:T(4,128)S(1)}) custom-call(f32[8,128]{1,0:T(8,128)S(1)} %get-tuple-element.63.first_sums, f32[8,128]{1,0:T(8,128)S(1)} %get-tuple-element.57.jump_sums, f32[8,128]{1,0:T(8,128)S(1)} %get-tuple-element.59.near_sums.high_sums, ...), custom_call_target="tpu_custom_call", output_to_operand_aliasing={{0}: (17, {})} | custom-call | flops 10485760 | bytes 7864320 | tf_op jit(solution)/shard_map/stencil_second_added/pallas_call | solution.py:922
  48.6 0.1 collective-permute-start.5
  48.7 1.6 %own_second.1.earlier.own_next = f32[256,512]{1,0:T(8,128)S(1)} custom-call(f32[256,512]{1,0:T(8,128)S(1)} %get-tuple-element.62.s_first, f32[264,512]{1,0:T(8,128)S(1)} %collective-permute-done.3.recv.much_later, bf16[512,256]{1,0:T(8,128)(2,1)S(1)} %get-tuple-element.52.proj_t, bf16[512,256]{1,0:T(8,128)(2,1)S(1)} %get-tuple-element.56.proj_n), custom_call_target="tpu_custom_call" | custom-call | flops 939524096 | bytes 1835008 | tf_op jit(solution)/shard_map/own_second/pallas_call | solution.py:940
  50.3 0.0 collective-permute-done.5.other
  50.3 1.7 %collective-permute-start.6 = (f32[4,128]{1,0:T(4,128)S(1)}, f32[4,128]{1,0:T(4,128)S(1)}, u32[]{:S(2)}, u32[]{:S(2)}) collective-permute-start(f32[4,128]{1,0:T(4,128)S(1)} %add.17), channel_id=1, source_target_pairs={{0,3},{1,2},{2,1},{3,0},{4,7},{5,6},{6,5},{7,4},{8,11},{9,10},{10,... | collective-permute-start | bytes 6152 | tf_op jit(solution)/shard_map/ppermute | solution.py:740
  52.0 1.4 %collective-permute-done.6 = f32[4,128]{1,0:T(4,128)S(1)} collective-permute-done((f32[4,128]{1,0:T(4,128)S(1)}, f32[4,128]{1,0:T(4,128)S(1)}, u32[]{:S(2)}, u32[]{:S(2)}) %collective-permute-start.6) | collective-permute-done | bytes 2080 | tf_op jit(solution)/shard_map/ppermute | solution.py:740
  53.4 3.0 %collective-permute-start.7 = (f32[4,128]{1,0:T(4,128)S(1)}, f32[4,128]{1,0:T(4,128)S(1)}, u32[]{:S(2)}, u32[]{:S(2)}) collective-permute-start(f32[4,128]{1,0:T(4,128)S(1)} %add.13), channel_id=1, source_target_pairs={{0,17},{1,16},{2,19},{3,18},{4,21},{5,20},{6,23},{7,22},{8,25},{9,... | collective-permute-start | bytes 6152 | tf_op jit(solution)/shard_map/ppermute | solution.py:740
  56.4 1.3 %collective-permute-done.7 = f32[4,128]{1,0:T(4,128)S(1)} collective-permute-done((f32[4,128]{1,0:T(4,128)S(1)}, f32[4,128]{1,0:T(4,128)S(1)}, u32[]{:S(2)}, u32[]{:S(2)}) %collective-permute-start.7) | collective-permute-done | bytes 2080 | tf_op jit(solution)/shard_map/ppermute | solution.py:740
  57.7 1.9 %collective-permute-start.8 = (f32[4,128]{1,0:T(4,128)S(1)}, f32[4,128]{1,0:T(4,128)S(1)}, u32[]{:S(2)}, u32[]{:S(2)}) collective-permute-start(f32[4,128]{1,0:T(4,128)S(1)} %add.14), channel_id=1, source_target_pairs={{0,9},{1,8},{2,11},{3,10},{4,13},{5,12},{6,15},{7,14},{8,1},{9,0},... | collective-permute-start | bytes 6152 | tf_op jit(solution)/shard_map/ppermute | solution.py:740
  59.6 1.3 %collective-permute-done.8 = f32[4,128]{1,0:T(4,128)S(1)} collective-permute-done((f32[4,128]{1,0:T(4,128)S(1)}, f32[4,128]{1,0:T(4,128)S(1)}, u32[]{:S(2)}, u32[]{:S(2)}) %collective-permute-start.8) | collective-permute-done | bytes 2080 | tf_op jit(solution)/shard_map/ppermute | solution.py:740
  60.9 2.4 %collective-permute-start.9 = (f32[4,128]{1,0:T(4,128)S(1)}, f32[4,128]{1,0:T(4,128)S(1)}, u32[]{:S(2)}, u32[]{:S(2)}) collective-permute-start(f32[4,128]{1,0:T(4,128)S(1)} %add.15), channel_id=1, source_target_pairs={{0,5},{1,4},{2,7},{3,6},{4,1},{5,0},{6,3},{7,2},{8,13},{9,12},{10,... | collective-permute-start | bytes 6152 | tf_op jit(solution)/shard_map/ppermute | solution.py:740
  63.3 1.3 %collective-permute-done.9 = f32[4,128]{1,0:T(4,128)S(1)} collective-permute-done((f32[4,128]{1,0:T(4,128)S(1)}, f32[4,128]{1,0:T(4,128)S(1)}, u32[]{:S(2)}, u32[]{:S(2)}) %collective-permute-start.9) | collective-permute-done | bytes 2080 | tf_op jit(solution)/shard_map/ppermute | solution.py:740
  64.6 0.0 collective-permute-done.10.recv_next
  64.6 2.5 %final_update.1 = (f32[4,256,512]{2,1,0:T(8,128)}, f32[4,256,512]{2,1,0:T(8,128)}) custom-call(f32[4,128]{1,0:T(4,128)S(1)} %add.16.tables, f32[4,256,512]{2,1,0:T(8,128)S(1)} %get-tuple-element.48.b, f32[256,512]{1,0:T(8,128)S(1)} %get-tuple-element.62.s_first, f32[2,256,512]{2,1,0:T(8,128)S(1)} %get-tuple-element.70.s_mid, ...), custom_call_target="tpu_custom_call" | custom-call | flops 4194304 | bytes 11534336 | tf_op jit(solution)/shard_map/final_update/pallas_call | solution.py:951
  (8 shorter events, 0.0 us)
Async XLA Ops:
  0.6 3.1 %copy-start = (f32[4,128,128]{2,1,0:T(8,128)S(1)}, f32[4,128,128]{2,1,0:T(8,128)}, u32[]{:S(2)}) copy-start(f32[4,128,128]{2,1,0:T(8,128)} %proj.1) | copy-start | bytes 786436
  0.6 3.1 %copy-start.2 = (s32[1,1,1024]{2,1,0:T(1,128)S(1)}, s32[1,1,1024]{2,1,0:T(1,128)}, u32[]{:S(2)}) copy-start(s32[1,1,1024]{2,1,0:T(1,128)} %kind.1) | copy-start | bytes 12292
  0.7 3.1 %copy-start.1 = (s32[1,1,1024]{2,1,0:T(1,128)S(1)}, s32[1,1,1024]{2,1,0:T(1,128)}, u32[]{:S(2)}) copy-start(s32[1,1,1024]{2,1,0:T(1,128)} %perm.1) | copy-start | bytes 12292
  1.8 17.9 %collective-permute-start = (f32[264,512]{1,0:T(8,128)S(1)}, f32[264,512]{1,0:T(8,128)S(1)}, u32[]{:S(2)}, u32[]{:S(2)}) collective-permute-start(f32[264,512]{1,0:T(8,128)S(1)} %pack.1), channel_id=1, source_target_pairs={{4,0},{8,4},{12,8},{16,12},{20,16},{24,20},{28,24},{5,1},{9,5},{13... | collective-permute-start | bytes 1622024 | tf_op jit(solution)/shard_map/ppermute | solution.py:724
  9.5 29.1 %collective-permute-start.4 = (f32[256,512]{1,0:T(8,128)S(1)}, f32[256,512]{1,0:T(8,128)S(1)}, u32[]{:S(2)}, u32[]{:S(2)}) collective-permute-start(f32[256,512]{1,0:T(8,128)S(1)} %get-tuple-element.66), channel_id=1, source_target_pairs={{4,0},{8,4},{12,8},{16,12},{20,16},{24,20},{28,24},{5,1},{9,5},{13... | collective-permute-start | bytes 1572872 | tf_op jit(solution)/shard_map/ppermute | solution.py:724
  25.9 15.9 %collective-permute-start.3 = (f32[264,512]{1,0:T(8,128)S(1)}, f32[264,512]{1,0:T(8,128)S(1)}, u32[]{:S(2)}, u32[]{:S(2)}) collective-permute-start(f32[264,512]{1,0:T(8,128)S(1)} %wait.1.back_before), channel_id=1, source_target_pairs={{0,4},{4,8},{8,12},{12,16},{16,20},{20,24},{24,28},{1,5},{5,9},{9,... | collective-permute-start | bytes 1622024 | tf_op jit(solution)/shard_map/ppermute | solution.py:724
  30.8 6.2 %collective-permute-start.1 = (f32[15,512]{1,0:T(8,128)S(1)}, f32[15,512]{1,0:T(8,128)S(1)}, u32[]{:S(2)}, u32[]{:S(2)}) collective-permute-start(f32[15,512]{1,0:T(8,128)S(1)} %get-tuple-element.60.earlier), channel_id=1, source_target_pairs={{0,1},{1,2},{2,3},{4,5},{5,6},{6,7},{8,9},{9,10},{10,11},{12,13},{... | collective-permute-start | bytes 92168 | tf_op jit(solution)/shard_map/ppermute | solution.py:724
  32.1 4.9 %collective-permute-start.2 = (f32[10,512]{1,0:T(8,128)S(1)}, f32[10,512]{1,0:T(8,128)S(1)}, u32[]{:S(2)}, u32[]{:S(2)}) collective-permute-start(f32[10,512]{1,0:T(8,128)S(1)} %get-tuple-element.61), channel_id=1, source_target_pairs={{1,0},{2,1},{3,2},{5,4},{6,5},{7,6},{9,8},{10,9},{11,10},{13,12},{... | collective-permute-start | bytes 61448 | tf_op jit(solution)/shard_map/ppermute | solution.py:724
  41.9 22.7 %collective-permute-start.10 = (f32[264,512]{1,0:T(8,128)S(1)}, f32[264,512]{1,0:T(8,128)S(1)}, u32[]{:S(2)}, u32[]{:S(2)}) collective-permute-start(f32[264,512]{1,0:T(8,128)S(1)} %hold.1), channel_id=1, source_target_pairs={{0,4},{4,8},{8,12},{12,16},{16,20},{20,24},{24,28},{1,5},{5,9},{9,... | collective-permute-start | bytes 1622024 | tf_op jit(solution)/shard_map/ppermute | solution.py:724
  48.6 1.7 %collective-permute-start.5 = (f32[4,128]{1,0:T(4,128)S(1)}, f32[4,128]{1,0:T(4,128)S(1)}, u32[]{:S(2)}, u32[]{:S(2)}) collective-permute-start(f32[4,128]{1,0:T(4,128)S(1)} %get-tuple-element.74.one), channel_id=1, source_target_pairs={{0,1},{1,0},{2,3},{3,2},{4,5},{5,4},{6,7},{7,6},{8,9},{9,8},{10,11... | collective-permute-start | bytes 6152 | tf_op jit(solution)/shard_map/ppermute | solution.py:740
  50.3 3.1 %collective-permute-start.6 = (f32[4,128]{1,0:T(4,128)S(1)}, f32[4,128]{1,0:T(4,128)S(1)}, u32[]{:S(2)}, u32[]{:S(2)}) collective-permute-start(f32[4,128]{1,0:T(4,128)S(1)} %add.17), channel_id=1, source_target_pairs={{0,3},{1,2},{2,1},{3,0},{4,7},{5,6},{6,5},{7,4},{8,11},{9,10},{10,... | collective-permute-start | bytes 6152 | tf_op jit(solution)/shard_map/ppermute | solution.py:740
  53.4 4.3 %collective-permute-start.7 = (f32[4,128]{1,0:T(4,128)S(1)}, f32[4,128]{1,0:T(4,128)S(1)}, u32[]{:S(2)}, u32[]{:S(2)}) collective-permute-start(f32[4,128]{1,0:T(4,128)S(1)} %add.13), channel_id=1, source_target_pairs={{0,17},{1,16},{2,19},{3,18},{4,21},{5,20},{6,23},{7,22},{8,25},{9,... | collective-permute-start | bytes 6152 | tf_op jit(solution)/shard_map/ppermute | solution.py:740
  57.7 3.2 %collective-permute-start.8 = (f32[4,128]{1,0:T(4,128)S(1)}, f32[4,128]{1,0:T(4,128)S(1)}, u32[]{:S(2)}, u32[]{:S(2)}) collective-permute-start(f32[4,128]{1,0:T(4,128)S(1)} %add.14), channel_id=1, source_target_pairs={{0,9},{1,8},{2,11},{3,10},{4,13},{5,12},{6,15},{7,14},{8,1},{9,0},... | collective-permute-start | bytes 6152 | tf_op jit(solution)/shard_map/ppermute | solution.py:740
  60.9 3.7 %collective-permute-start.9 = (f32[4,128]{1,0:T(4,128)S(1)}, f32[4,128]{1,0:T(4,128)S(1)}, u32[]{:S(2)}, u32[]{:S(2)}) collective-permute-start(f32[4,128]{1,0:T(4,128)S(1)} %add.15), channel_id=1, source_target_pairs={{0,5},{1,4},{2,7},{3,6},{4,1},{5,0},{6,3},{7,2},{8,13},{9,12},{10,... | collective-permute-start | bytes 6152 | tf_op jit(solution)/shard_map/ppermute | solution.py:740

commit v6 on v4

--- a/solution.py
+++ b/solution.py
@@ -348,7 +348,14 @@
     sums[...] = as_tile([jnp.sum(square)])
 
 
-def kinds_kernel(code_row, picks, kinds_by_block):
+def kinds_kernel(code_row, picks, proj_t, proj_n, kinds_by_block, squares):
+    width = proj_t.shape[1] // 2
+    for kind in range(proj_t.shape[0] // width):
+        here = pl.ds(kind * width, width)
+        left, right = proj_t[here, :], proj_n[here, :]
+        both = mm(left[:, :width], right)
+        square = both[:, :width] + both[:, width:] + mm(left[:, width:], right[:, :width])
+        squares[here, :] = jnp.concatenate(two_parts(square), axis=1)
     depth = kinds_by_block.shape[1]
     row = mm(jnp.broadcast_to(code_row[...], (2 * SUB, code_row.shape[1])).astype(BF16), picks[...])
     kinds_by_block[...] = jnp.zeros_like(kinds_by_block)
@@ -415,10 +422,10 @@
     back[rows : rows + 2, :] = missing[...]
 
 
-def own_second_kernel(s_first, recv, proj_t, proj_n, own):
+def own_second_kernel(s_first, recv, squares, own):
     rows, depth = own.shape
-    width = proj_t.shape[1] // 2
-    kinds = proj_t.shape[0] // width
+    width = squares.shape[1] // 2
+    kinds = squares.shape[0] // width
     for group in range(depth // width):
         part = pl.ds(group * width, width)
         codes = []
@@ -428,8 +435,7 @@
             codes.append(jnp.transpose(jnp.broadcast_to(row, (LANES, LANES))))
         codes = kinds - jnp.concatenate(codes, axis=0).astype(jnp.int32)
         field = s_first[:, part] + recv[:rows, part]
-        projected = apply_proj(codes, *two_parts(field), proj_t, kinds, width)
-        own[:, part] = penalty * apply_proj(codes, *two_parts(projected), proj_n, kinds, width)
+        own[:, part] = penalty * apply_proj(codes, *two_parts(field), squares, kinds, width)
 
 
 def hold_kernel(later, back_in, back):
@@ -808,15 +814,15 @@
         cost_estimate=mortar_cost,
         name="jump_first",
     )(*near_core(image_low, b, face_right, s_last, picks, codes, proj_t))
-    (kinds_by_block,) = pl.pallas_call(
+    kinds_by_block, squares = pl.pallas_call(
         kinds_kernel,
-        in_specs=[VMEM] * 2,
-        out_specs=[VMEM],
-        out_shape=[held(SUB, depth)],
+        in_specs=[VMEM] * 4,
+        out_specs=[VMEM] * 2,
+        out_shape=[held(SUB, depth), held(kinds * width, 2 * width, dtype=BF16)],
         compiler_params=params(8),
         cost_estimate=cost(16 * blocks * blocks, 2 * blocks * blocks),
         name="kinds",
-    )(*near_core(code_row, picks))
+    )(*near_core(code_row, picks, proj_t, proj_n))
     (back,) = pl.pallas_call(
         back_first_kernel,
         in_specs=[VMEM] * 5,
@@ -924,13 +930,13 @@
     )
     (own_next,) = pl.pallas_call(
         own_second_kernel,
-        in_specs=[VMEM] * 4,
+        in_specs=[VMEM] * 3,
         out_specs=[VMEM],
         out_shape=[held(rows, depth)],
         compiler_params=params(16),
         cost_estimate=mortar_cost,
         name="own_second",
-    )(*near_core(s_first, recv, proj_t, proj_n))
+    )(*near_core(s_first, recv, squares))
     tables = gather_rows(table, own_next)
 
     return pl.pallas_call(

time: 66.3 us -> 65.6 us (0.989)
  Pallas kernels: 25 us -> 24.3 us
    pallas_call x2, Pallas kernels: 2.02 us -> 1.3 us  [the longest x1 0.79 us: body(): pl.pallas_call(own_second_kernel, in_specs=[VMEM] * 3, out_specs=[VMEM],...]
where the time goes in v6:
time: 65.6 us; the launch traced here: 65.3 us
  starting transfers between devices  26.3 us (40%)
  Pallas kernels  24.3 us (37%)
  waiting for transfers between devices  13.2 us (20%)
  between operations  1.5 us (2%)
    ppermute x5, starting transfers between devices, gather_rows(): other = lax.ppermute(table, ('sub', 'blk'), pairs)  13.7 us
    ppermute x6, starting transfers between devices, shifted(): lax.ppermute(array, axis, [(i, i + by) for i in range(size) if 0 <= i + b...  12.6 us
    ppermute x6, waiting for transfers between devices, shifted(): lax.ppermute(array, axis, [(i, i + by) for i in range(size) if 0 <= i + b...  7.94 us
    pallas_call x1, Pallas kernels, body(): pl.pallas_call(first_kernel, in_specs=[SMEM] + [VMEM] * 3 + [HBM] * 5, ou...  5.76 us
    ppermute x5, waiting for transfers between devices, gather_rows(): other = lax.ppermute(table, ('sub', 'blk'), pairs)  5.26 us
    pallas_call x1, Pallas kernels, body(): pl.pallas_call(second_high_kernel, in_specs=[VMEM] * 11, out_specs=[VMEM]...  3.13 us
    pallas_call x1, Pallas kernels, body(): pl.pallas_call(final_kernel, in_specs=[VMEM] * 13, out_specs=[HBM] * 2, o...  2.46 us
    pallas_call x1, Pallas kernels, body(): pl.pallas_call(second_added_kernel, in_specs=[VMEM] * 18, out_specs=[VMEM...  2.14 us
  transfers between devices with their start and end apart: 11, of which 6 were waited for; matrix products, arithmetic and copies ran while one was open for 0% of the time, Pallas kernels for 32%

profile of v6, /device:TPU:0, one launch (start us, length us, event | category | flops | bytes accessed | tf_op | source)
XLA Modules:
  0.0 65.3 jit_solution(7088452906389984467)
XLA Ops:
  0.6 0.0 copy-start.1
  0.6 0.0 copy-start.2
  0.7 0.0 copy-start
  0.7 1.1 %pack.1 = f32[264,512]{1,0:T(8,128)S(1)} custom-call(f32[4,256,512]{2,1,0:T(8,128)} %b_hbm.3, f32[4,256,512]{2,1,0:T(8,128)} %ty_hbm.3), custom_call_target="tpu_custom_call" | custom-call | bytes 524288 | tf_op jit(solution)/shard_map/pack/pallas_call | solution.py:764
  1.8 1.3 %collective-permute-start = (f32[264,512]{1,0:T(8,128)S(1)}, f32[264,512]{1,0:T(8,128)S(1)}, u32[]{:S(2)}, u32[]{:S(2)}) collective-permute-start(f32[264,512]{1,0:T(8,128)S(1)} %pack.1), channel_id=1, source_target_pairs={{4,0},{8,4},{12,8},{16,12},{20,16},{24,20},{28,24},{5,1},{9,5},{13... | collective-permute-start | bytes 1622024 | tf_op jit(solution)/shard_map/ppermute | solution.py:725
  3.7 0.0 copy-done.1
  3.7 0.0 copy-done.2
  3.7 0.0 copy-done
  3.8 5.8 %stencil_first.1 = (f32[4,256,512]{2,1,0:T(8,128)S(1)}, f32[4,256,512]{2,1,0:T(8,128)S(1)}, f32[4,256,512]{2,1,0:T(8,128)S(1)}, f32[4,256,512]{2,1,0:T(8,128)S(1...) custom-call(s32[1,1]{1,0:T(1,128)S(6)} %copy.25.count, ...), custom_call_target="tpu_custom_call" | custom-call | flops 10485760 | bytes 12582912 | tf_op jit(solution)/shard_map/stencil_first/pallas_call | solution.py:776
  9.5 1.3 %collective-permute-start.4 = (f32[256,512]{1,0:T(8,128)S(1)}, f32[256,512]{1,0:T(8,128)S(1)}, u32[]{:S(2)}, u32[]{:S(2)}) collective-permute-start(f32[256,512]{1,0:T(8,128)S(1)} %get-tuple-element.70), channel_id=1, source_target_pairs={{4,0},{8,4},{12,8},{16,12},{20,16},{24,20},{28,24},{5,1},{9,5},{13... | collective-permute-start | bytes 1572872 | tf_op jit(solution)/shard_map/ppermute | solution.py:725
  10.8 1.9 %stencil_second_low.1.earlier.image_low_in = f32[2,256,512]{2,1,0:T(8,128)S(1)} custom-call(f32[256,512]{1,0:T(8,128)S(1)} %get-tuple-element.44.s_first.s_first_in, f32[2,256,512]{2,1,0:T(8,128)S(1)} %get-tuple-element.45.s_mid.s_mid_in, f32[4,256,512]{2,1,0:T(8,128)S(1)} %get-tuple-element.46.tx, f32[4,256,512]{2,1,0:T(8,128)S(1)} %get-tuple-element.47.ty, ...), custom_call_target="tpu_custom_call" | custom-call | flops 10485760 | bytes 7864320 | tf_op jit(solution)/shard_map/stencil_second_low/pallas_call | solution.py:797
  12.7 0.5 kinds.1
  13.2 6.5 %collective-permute-done.right.right_before = f32[264,512]{1,0:T(8,128)S(1)} collective-permute-done((f32[264,512]{1,0:T(8,128)S(1)}, f32[264,512]{1,0:T(8,128)S(1)}, u32[]{:S(2)}, u32[]{:S(2)}) %collective-permute-start) | collective-permute-done | bytes 540704 | tf_op jit(solution)/shard_map/ppermute | solution.py:725
  19.7 1.8 %jump_first.1 = (f32[256,512]{1,0:T(8,128)S(1)}, f32[256,512]{1,0:T(8,128)S(1)}, f32[8,128]{1,0:T(8,128)S(1)}) custom-call(f32[2,256,512]{2,1,0:T(8,128)S(1)} %stencil_second_low.1.earlier.image_low_in, f32[4,256,512]{2,1,0:T(8,128)S(1)} %get-tuple-element.50.b, f32[264,512]{1,0:T(8,128)S(1)} %collective-permute-done.right.right_before, ...), custom_call_target="tpu_custom_call" | custom-call | flops 939524096 | bytes 1835008 | tf_op jit(solution)/shard_map/jump_first/pallas_call | solution.py:808
  21.5 1.3 %back_first.1.later.back.back_before = f32[264,512]{1,0:T(8,128)S(1)} custom-call(f32[256,512]{1,0:T(8,128)S(1)} %get-tuple-element.55.jump, f32[8,512]{1,0:T(8,128)S(1)} %get-tuple-element.58.kinds_by_block, bf16[1024,1024]{1,0:T(8,128)(2,1)S(1)} %get-tuple-element.59.puts, s32[1024,128]{1,0:T(8,128)S(1)} %get-tuple-element.53.codes, ...), custom_call_target="tpu_custom_call" | custom-call | flops 939524096 | bytes 1835008 | tf_op jit(solution)/shard_map/back_first/pallas_call | solution.py:826
  22.8 1.3 %collective-permute-start.1 = (f32[15,512]{1,0:T(8,128)S(1)}, f32[15,512]{1,0:T(8,128)S(1)}, u32[]{:S(2)}, u32[]{:S(2)}) collective-permute-start(f32[15,512]{1,0:T(8,128)S(1)} %get-tuple-element.63), channel_id=1, source_target_pairs={{0,1},{1,2},{2,3},{4,5},{5,6},{6,7},{8,9},{9,10},{10,11},{12,13},{... | collective-permute-start | bytes 92168 | tf_op jit(solution)/shard_map/ppermute | solution.py:725
  24.1 1.3 %collective-permute-start.2 = (f32[10,512]{1,0:T(8,128)S(1)}, f32[10,512]{1,0:T(8,128)S(1)}, u32[]{:S(2)}, u32[]{:S(2)}) collective-permute-start(f32[10,512]{1,0:T(8,128)S(1)} %get-tuple-element.64), channel_id=1, source_target_pairs={{1,0},{2,1},{3,2},{5,4},{6,5},{7,6},{9,8},{10,9},{11,10},{13,12},{... | collective-permute-start | bytes 61448 | tf_op jit(solution)/shard_map/ppermute | solution.py:725
  25.4 4.9 %collective-permute-start.3 = (f32[264,512]{1,0:T(8,128)S(1)}, f32[264,512]{1,0:T(8,128)S(1)}, u32[]{:S(2)}, u32[]{:S(2)}) collective-permute-start(f32[264,512]{1,0:T(8,128)S(1)} %back_first.1.later.back.back_before), channel_id=1, source_target_pairs={{0,4},{4,8},{8,12},{12,16},{16,20},{20,24},{24,28},{1,5},{5,9},{9,... | collective-permute-start | bytes 1622024 | tf_op jit(solution)/shard_map/ppermute | solution.py:725
  30.3 3.1 %stencil_second_high.1 = (f32[2,256,512]{2,1,0:T(8,128)S(1)}, f32[8,128]{1,0:T(8,128)S(1)}) custom-call(f32[264,512]{1,0:T(8,128)S(1)} %back_first.1.later.back.back_before, f32[8,128]{1,0:T(8,128)S(1)} %get-tuple-element.43.first_sums.sums_in, f32[8,128]{1,0:T(8,128)S(1)} %get-tuple-element.60.jump_sums, f32[4,256,512]{2,1,0:T(8,128)S(1)} %get-tuple-element.50.b, ...), custom_call_target="tpu_custom_call" | custom-call | flops 10485760 | bytes 7864320 | tf_op jit(solution)/shard_map/stencil_second_high/pallas_call | solution.py:838
  33.4 0.0 collective-permute-done.2.down
  33.4 0.0 collective-permute-done.1.up
  33.4 0.3 edges_first.1
  33.8 1.3 %back_second.1.back_in = f32[264,512]{1,0:T(8,128)S(1)} custom-call(f32[256,512]{1,0:T(8,128)S(1)} %get-tuple-element.69.w_last, f32[2,512]{1,0:T(2,128)S(1)} %get-tuple-element.72.missing, bf16[1024,1024]{1,0:T(8,128)(2,1)S(1)} %get-tuple-element.59.puts, s32[1024,128]{1,0:T(8,128)S(1)} %get-tuple-element.53.codes, ...), custom_call_target="tpu_custom_call" | custom-call | flops 939524096 | bytes 1835008 | tf_op jit(solution)/shard_map/back_second/pallas_call | solution.py:890
  35.0 0.0 collective-permute-done.4.right
  35.1 1.8 %jump_second.1 = (f32[256,512]{1,0:T(8,128)S(1)}, f32[8,128]{1,0:T(8,128)S(1)}) custom-call(f32[8,128]{1,0:T(8,128)S(1)} %get-tuple-element.62.near_sums.high_sums, f32[256,512]{1,0:T(8,128)S(1)} %get-tuple-element.69.w_last, f32[256,512]{1,0:T(8,128)S(1)} %get-tuple-element.55.jump, f32[264,512]{1,0:T(8,128)S(1)} %collective-permute-done.right.right_before, ...), custom_call_target="tpu_custom_call" | custom-call | flops 939524096 | bytes 1835008 | tf_op jit(solution)/shard_map/jump_second/pallas_call | solution.py:876
  36.9 2.6 %collective-permute-start.10 = (f32[264,512]{1,0:T(8,128)S(1)}, f32[264,512]{1,0:T(8,128)S(1)}, u32[]{:S(2)}, u32[]{:S(2)}) collective-permute-start(f32[264,512]{1,0:T(8,128)S(1)} %hold.1), channel_id=1, source_target_pairs={{0,4},{4,8},{8,12},{12,16},{16,20},{20,24},{24,28},{1,5},{5,9},{9,... | collective-permute-start | bytes 1622024 | tf_op jit(solution)/shard_map/ppermute | solution.py:725
  39.5 1.4 %collective-permute-done.3.recv = f32[264,512]{1,0:T(8,128)S(1)} collective-permute-done((f32[264,512]{1,0:T(8,128)S(1)}, f32[264,512]{1,0:T(8,128)S(1)}, u32[]{:S(2)}, u32[]{:S(2)}) %collective-permute-start.3) | collective-permute-done | bytes 540704 | tf_op jit(solution)/shard_map/ppermute | solution.py:725
  40.9 2.1 %stencil_second_added.1 = (f32[2,256,512]{2,1,0:T(8,128)S(1)}, f32[4,512]{1,0:T(4,128)S(1)}, f32[4,128]{1,0:T(4,128)S(1)}) custom-call(f32[8,128]{1,0:T(8,128)S(1)} %get-tuple-element.67.first_sums, f32[8,128]{1,0:T(8,128)S(1)} %get-tuple-element.60.jump_sums, f32[8,128]{1,0:T(8,128)S(1)} %get-tuple-element.62.near_sums.high_sums, ...), custom_call_target="tpu_custom_call", output_to_operand_aliasing={{0}: (17, {})} | custom-call | flops 10485760 | bytes 7864320 | tf_op jit(solution)/shard_map/stencil_second_added/pallas_call | solution.py:913
  43.1 4.1 %collective-permute-start.5 = (f32[4,128]{1,0:T(4,128)S(1)}, f32[4,128]{1,0:T(4,128)S(1)}, u32[]{:S(2)}, u32[]{:S(2)}) collective-permute-start(f32[4,128]{1,0:T(4,128)S(1)} %get-tuple-element.78.one), channel_id=1, source_target_pairs={{0,1},{1,0},{2,3},{3,2},{4,5},{5,4},{6,7},{7,6},{8,9},{9,8},{10,11... | collective-permute-start | bytes 6152 | tf_op jit(solution)/shard_map/ppermute | solution.py:741
  47.2 0.8 %own_second.1.earlier.own_next = f32[256,512]{1,0:T(8,128)S(1)} custom-call(f32[256,512]{1,0:T(8,128)S(1)} %get-tuple-element.65.s_first, f32[264,512]{1,0:T(8,128)S(1)} %collective-permute-done.3.recv, bf16[512,256]{1,0:T(8,128)(2,1)S(1)} %get-tuple-element.66.squares), custom_call_target="tpu_custom_call" | custom-call | flops 939524096 | bytes 1835008 | tf_op jit(solution)/shard_map/own_second/pallas_call | solution.py:931
  48.0 0.0 collective-permute-done.5.other
  48.0 2.6 %collective-permute-start.6 = (f32[4,128]{1,0:T(4,128)S(1)}, f32[4,128]{1,0:T(4,128)S(1)}, u32[]{:S(2)}, u32[]{:S(2)}) collective-permute-start(f32[4,128]{1,0:T(4,128)S(1)} %add.17), channel_id=1, source_target_pairs={{0,3},{1,2},{2,1},{3,0},{4,7},{5,6},{6,5},{7,4},{8,11},{9,10},{10,... | collective-permute-start | bytes 6152 | tf_op jit(solution)/shard_map/ppermute | solution.py:741
  50.7 1.3 %collective-permute-done.6 = f32[4,128]{1,0:T(4,128)S(1)} collective-permute-done((f32[4,128]{1,0:T(4,128)S(1)}, f32[4,128]{1,0:T(4,128)S(1)}, u32[]{:S(2)}, u32[]{:S(2)}) %collective-permute-start.6) | collective-permute-done | bytes 2080 | tf_op jit(solution)/shard_map/ppermute | solution.py:741
  52.0 2.7 %collective-permute-start.7 = (f32[4,128]{1,0:T(4,128)S(1)}, f32[4,128]{1,0:T(4,128)S(1)}, u32[]{:S(2)}, u32[]{:S(2)}) collective-permute-start(f32[4,128]{1,0:T(4,128)S(1)} %add.13), channel_id=1, source_target_pairs={{0,17},{1,16},{2,19},{3,18},{4,21},{5,20},{6,23},{7,22},{8,25},{9,... | collective-permute-start | bytes 6152 | tf_op jit(solution)/shard_map/ppermute | solution.py:741
  54.7 1.3 %collective-permute-done.7 = f32[4,128]{1,0:T(4,128)S(1)} collective-permute-done((f32[4,128]{1,0:T(4,128)S(1)}, f32[4,128]{1,0:T(4,128)S(1)}, u32[]{:S(2)}, u32[]{:S(2)}) %collective-permute-start.7) | collective-permute-done | bytes 2080 | tf_op jit(solution)/shard_map/ppermute | solution.py:741
  56.0 2.2 %collective-permute-start.8 = (f32[4,128]{1,0:T(4,128)S(1)}, f32[4,128]{1,0:T(4,128)S(1)}, u32[]{:S(2)}, u32[]{:S(2)}) collective-permute-start(f32[4,128]{1,0:T(4,128)S(1)} %add.14), channel_id=1, source_target_pairs={{0,9},{1,8},{2,11},{3,10},{4,13},{5,12},{6,15},{7,14},{8,1},{9,0},... | collective-permute-start | bytes 6152 | tf_op jit(solution)/shard_map/ppermute | solution.py:741
  58.3 1.3 %collective-permute-done.8 = f32[4,128]{1,0:T(4,128)S(1)} collective-permute-done((f32[4,128]{1,0:T(4,128)S(1)}, f32[4,128]{1,0:T(4,128)S(1)}, u32[]{:S(2)}, u32[]{:S(2)}) %collective-permute-start.8) | collective-permute-done | bytes 2080 | tf_op jit(solution)/shard_map/ppermute | solution.py:741
  59.6 2.0 %collective-permute-start.9 = (f32[4,128]{1,0:T(4,128)S(1)}, f32[4,128]{1,0:T(4,128)S(1)}, u32[]{:S(2)}, u32[]{:S(2)}) collective-permute-start(f32[4,128]{1,0:T(4,128)S(1)} %add.15), channel_id=1, source_target_pairs={{0,5},{1,4},{2,7},{3,6},{4,1},{5,0},{6,3},{7,2},{8,13},{9,12},{10,... | collective-permute-start | bytes 6152 | tf_op jit(solution)/shard_map/ppermute | solution.py:741
  61.6 1.3 %collective-permute-done.9 = f32[4,128]{1,0:T(4,128)S(1)} collective-permute-done((f32[4,128]{1,0:T(4,128)S(1)}, f32[4,128]{1,0:T(4,128)S(1)}, u32[]{:S(2)}, u32[]{:S(2)}) %collective-permute-start.9) | collective-permute-done | bytes 2080 | tf_op jit(solution)/shard_map/ppermute | solution.py:741
  62.9 0.0 collective-permute-done.10.recv_next
  62.9 2.5 %final_update.1 = (f32[4,256,512]{2,1,0:T(8,128)}, f32[4,256,512]{2,1,0:T(8,128)}) custom-call(f32[4,128]{1,0:T(4,128)S(1)} %add.16.tables, f32[4,256,512]{2,1,0:T(8,128)S(1)} %get-tuple-element.50.b, f32[256,512]{1,0:T(8,128)S(1)} %get-tuple-element.65.s_first, f32[2,256,512]{2,1,0:T(8,128)S(1)} %get-tuple-element.74.s_mid, ...), custom_call_target="tpu_custom_call" | custom-call | flops 4194304 | bytes 11534336 | tf_op jit(solution)/shard_map/final_update/pallas_call | solution.py:942
  (7 shorter events, 0.0 us)
Async XLA Ops:
  0.6 3.1 %copy-start.1 = (s32[1,1,1024]{2,1,0:T(1,128)S(1)}, s32[1,1,1024]{2,1,0:T(1,128)}, u32[]{:S(2)}) copy-start(s32[1,1,1024]{2,1,0:T(1,128)} %perm.1) | copy-start | bytes 12292
  0.6 3.1 %copy-start.2 = (s32[1,1,1024]{2,1,0:T(1,128)S(1)}, s32[1,1,1024]{2,1,0:T(1,128)}, u32[]{:S(2)}) copy-start(s32[1,1,1024]{2,1,0:T(1,128)} %kind.1) | copy-start | bytes 12292
  0.7 3.1 %copy-start = (f32[4,128,128]{2,1,0:T(8,128)S(1)}, f32[4,128,128]{2,1,0:T(8,128)}, u32[]{:S(2)}) copy-start(f32[4,128,128]{2,1,0:T(8,128)} %proj.1) | copy-start | bytes 786436
  1.8 17.9 %collective-permute-start = (f32[264,512]{1,0:T(8,128)S(1)}, f32[264,512]{1,0:T(8,128)S(1)}, u32[]{:S(2)}, u32[]{:S(2)}) collective-permute-start(f32[264,512]{1,0:T(8,128)S(1)} %pack.1), channel_id=1, source_target_pairs={{4,0},{8,4},{12,8},{16,12},{20,16},{24,20},{28,24},{5,1},{9,5},{13... | collective-permute-start | bytes 1622024 | tf_op jit(solution)/shard_map/ppermute | solution.py:725
  9.5 25.5 %collective-permute-start.4 = (f32[256,512]{1,0:T(8,128)S(1)}, f32[256,512]{1,0:T(8,128)S(1)}, u32[]{:S(2)}, u32[]{:S(2)}) collective-permute-start(f32[256,512]{1,0:T(8,128)S(1)} %get-tuple-element.70), channel_id=1, source_target_pairs={{4,0},{8,4},{12,8},{16,12},{20,16},{24,20},{28,24},{5,1},{9,5},{13... | collective-permute-start | bytes 1572872 | tf_op jit(solution)/shard_map/ppermute | solution.py:725
  22.8 10.6 %collective-permute-start.1 = (f32[15,512]{1,0:T(8,128)S(1)}, f32[15,512]{1,0:T(8,128)S(1)}, u32[]{:S(2)}, u32[]{:S(2)}) collective-permute-start(f32[15,512]{1,0:T(8,128)S(1)} %get-tuple-element.63), channel_id=1, source_target_pairs={{0,1},{1,2},{2,3},{4,5},{5,6},{6,7},{8,9},{9,10},{10,11},{12,13},{... | collective-permute-start | bytes 92168 | tf_op jit(solution)/shard_map/ppermute | solution.py:725
  24.1 9.3 %collective-permute-start.2 = (f32[10,512]{1,0:T(8,128)S(1)}, f32[10,512]{1,0:T(8,128)S(1)}, u32[]{:S(2)}, u32[]{:S(2)}) collective-permute-start(f32[10,512]{1,0:T(8,128)S(1)} %get-tuple-element.64), channel_id=1, source_target_pairs={{1,0},{2,1},{3,2},{5,4},{6,5},{7,6},{9,8},{10,9},{11,10},{13,12},{... | collective-permute-start | bytes 61448 | tf_op jit(solution)/shard_map/ppermute | solution.py:725
  25.4 15.5 %collective-permute-start.3 = (f32[264,512]{1,0:T(8,128)S(1)}, f32[264,512]{1,0:T(8,128)S(1)}, u32[]{:S(2)}, u32[]{:S(2)}) collective-permute-start(f32[264,512]{1,0:T(8,128)S(1)} %back_first.1.later.back.back_before), channel_id=1, source_target_pairs={{0,4},{4,8},{8,12},{12,16},{16,20},{20,24},{24,28},{1,5},{5,9},{9,... | collective-permute-start | bytes 1622024 | tf_op jit(solution)/shard_map/ppermute | solution.py:725
  36.9 26.0 %collective-permute-start.10 = (f32[264,512]{1,0:T(8,128)S(1)}, f32[264,512]{1,0:T(8,128)S(1)}, u32[]{:S(2)}, u32[]{:S(2)}) collective-permute-start(f32[264,512]{1,0:T(8,128)S(1)} %hold.1), channel_id=1, source_target_pairs={{0,4},{4,8},{8,12},{12,16},{16,20},{20,24},{24,28},{1,5},{5,9},{9,... | collective-permute-start | bytes 1622024 | tf_op jit(solution)/shard_map/ppermute | solution.py:725
  43.1 4.9 %collective-permute-start.5 = (f32[4,128]{1,0:T(4,128)S(1)}, f32[4,128]{1,0:T(4,128)S(1)}, u32[]{:S(2)}, u32[]{:S(2)}) collective-permute-start(f32[4,128]{1,0:T(4,128)S(1)} %get-tuple-element.78.one), channel_id=1, source_target_pairs={{0,1},{1,0},{2,3},{3,2},{4,5},{5,4},{6,7},{7,6},{8,9},{9,8},{10,11... | collective-permute-start | bytes 6152 | tf_op jit(solution)/shard_map/ppermute | solution.py:741
  48.0 4.0 %collective-permute-start.6 = (f32[4,128]{1,0:T(4,128)S(1)}, f32[4,128]{1,0:T(4,128)S(1)}, u32[]{:S(2)}, u32[]{:S(2)}) collective-permute-start(f32[4,128]{1,0:T(4,128)S(1)} %add.17), channel_id=1, source_target_pairs={{0,3},{1,2},{2,1},{3,0},{4,7},{5,6},{6,5},{7,4},{8,11},{9,10},{10,... | collective-permute-start | bytes 6152 | tf_op jit(solution)/shard_map/ppermute | solution.py:741
  52.0 4.0 %collective-permute-start.7 = (f32[4,128]{1,0:T(4,128)S(1)}, f32[4,128]{1,0:T(4,128)S(1)}, u32[]{:S(2)}, u32[]{:S(2)}) collective-permute-start(f32[4,128]{1,0:T(4,128)S(1)} %add.13), channel_id=1, source_target_pairs={{0,17},{1,16},{2,19},{3,18},{4,21},{5,20},{6,23},{7,22},{8,25},{9,... | collective-permute-start | bytes 6152 | tf_op jit(solution)/shard_map/ppermute | solution.py:741
  56.0 3.6 %collective-permute-start.8 = (f32[4,128]{1,0:T(4,128)S(1)}, f32[4,128]{1,0:T(4,128)S(1)}, u32[]{:S(2)}, u32[]{:S(2)}) collective-permute-start(f32[4,128]{1,0:T(4,128)S(1)} %add.14), channel_id=1, source_target_pairs={{0,9},{1,8},{2,11},{3,10},{4,13},{5,12},{6,15},{7,14},{8,1},{9,0},... | collective-permute-start | bytes 6152 | tf_op jit(solution)/shard_map/ppermute | solution.py:741
  59.6 3.3 %collective-permute-start.9 = (f32[4,128]{1,0:T(4,128)S(1)}, f32[4,128]{1,0:T(4,128)S(1)}, u32[]{:S(2)}, u32[]{:S(2)}) collective-permute-start(f32[4,128]{1,0:T(4,128)S(1)} %add.15), channel_id=1, source_target_pairs={{0,5},{1,4},{2,7},{3,6},{4,1},{5,0},{6,3},{7,2},{8,13},{9,12},{10,... | collective-permute-start | bytes 6152 | tf_op jit(solution)/shard_map/ppermute | solution.py:741

commit v7 on v6

--- a/solution.py
+++ b/solution.py
@@ -438,7 +438,7 @@
         own[:, part] = penalty * apply_proj(codes, *two_parts(field), squares, kinds, width)
 
 
-def hold_kernel(later, back_in, back):
+def hold_kernel(later, much_later, back_in, back):
     back[back.shape[0] - SUB + 2 :, :] = jnp.zeros((SUB - 2, back.shape[1]), F32)
 
 
@@ -716,6 +716,12 @@
     return pl.CostEstimate(flops=int(flops), bytes_accessed=int(size), transcendentals=0)
 
 
+def scaled(estimate, by):
+    return pl.CostEstimate(
+        flops=int(estimate.flops * by) + 1, bytes_accessed=int(estimate.bytes_accessed * by) + 1, transcendentals=0
+    )
+
+
 def params(mib):
     return pltpu.CompilerParams(vmem_limit_bytes=mib * 1024 * 1024)
 
@@ -746,7 +752,7 @@
                 out_specs=[VMEM],
                 out_shape=[held(*table.shape)],
                 compiler_params=params(2),
-                cost_estimate=cost(table.size, 12 * table.size),
+                cost_estimate=scaled(cost(table.size, 12 * table.size), 0.03),
                 name="add",
             )(*near_core(own, table, other))
         else:
@@ -768,7 +774,7 @@
         out_shape=[held(rows + SUB, depth)],
         scratch_shapes=[pltpu.SemaphoreType.DMA((2,))],
         compiler_params=params(2),
-        cost_estimate=cost(0, 4 * rows * depth),
+        cost_estimate=scaled(cost(0, 4 * rows * depth), 100),
         name="pack",
     )(*in_hbm(right_side, trans_y))
     face_right = shifted(face, "sub", -1)
@@ -785,7 +791,7 @@
         ],
         scratch_shapes=[pltpu.VMEM((2, SUB, LANES), F32), pltpu.SemaphoreType.DMA((5, steps))],
         compiler_params=params(16),
-        cost_estimate=cost(20 * cells, 24 * cells),
+        cost_estimate=scaled(cost(20 * cells, 24 * cells), 4),
         name="stencil_first",
     )(
         pair_count, pair_perm, pair_type, proj,
@@ -800,7 +806,7 @@
         out_specs=[VMEM],
         out_shape=[held(split, rows, depth)],
         compiler_params=params(8),
-        cost_estimate=cost(20 * cells, 15 * cells),
+        cost_estimate=scaled(cost(20 * cells, 15 * cells), 20),
         name="stencil_second_low",
     )(*near_core(s_first, s_mid, tx, ty, tz, st))
 
@@ -811,7 +817,7 @@
         out_specs=[VMEM] * 3,
         out_shape=[held(rows, depth), held(rows, depth), held(SUB, LANES)],
         compiler_params=params(16),
-        cost_estimate=mortar_cost,
+        cost_estimate=scaled(mortar_cost, 0.3),
         name="jump_first",
     )(*near_core(image_low, b, face_right, s_last, picks, codes, proj_t))
     kinds_by_block, squares = pl.pallas_call(
@@ -820,7 +826,7 @@
         out_specs=[VMEM] * 2,
         out_shape=[held(SUB, depth), held(kinds * width, 2 * width, dtype=BF16)],
         compiler_params=params(8),
-        cost_estimate=cost(16 * blocks * blocks, 2 * blocks * blocks),
+        cost_estimate=scaled(cost(16 * blocks * blocks, 2 * blocks * blocks), 20),
         name="kinds",
     )(*near_core(code_row, picks, proj_t, proj_n))
     (back,) = pl.pallas_call(
@@ -829,7 +835,7 @@
         out_specs=[VMEM],
         out_shape=[held(rows + SUB, depth)],
         compiler_params=params(16),
-        cost_estimate=mortar_cost,
+        cost_estimate=scaled(mortar_cost, 20),
         name="back_first",
     )(*near_core(jump, kinds_by_block, puts, codes, proj_n))
     recv = shifted(back, "sub", 1)
@@ -842,7 +848,7 @@
         out_shape=[held(layers - split, rows, depth), held(SUB, LANES)],
         scratch_shapes=[pltpu.VMEM((6, SUB, LANES), F32)],
         compiler_params=params(8),
-        cost_estimate=cost(20 * cells, 15 * cells),
+        cost_estimate=scaled(cost(20 * cells, 15 * cells), 1),
         name="stencil_second_high",
     )(*near_core(back, first_sums, jump_sums, b, s_mid, s_last, w_last, tx, ty, tz, st))
     up_out, down_out = pl.pallas_call(
@@ -851,7 +857,7 @@
         out_specs=[VMEM] * 2,
         out_shape=[held(3 * layers + 3, depth), held(2 * layers + 2, depth)],
         compiler_params=params(2),
-        cost_estimate=cost(0, 64 * depth),
+        cost_estimate=scaled(cost(0, 64 * depth), 4),
         name="rows",
     )(*near_core(face_right, b, ty, s_first, s_mid, w_last, back))
     up = shifted(up_out, "blk", 1)
@@ -865,7 +871,7 @@
         + [held(2, depth), held(2, depth), held(layers, depth), held(layers, depth)],
         input_output_aliases={10: 0, 11: 1, 12: 2, 13: 3, 14: 4},
         compiler_params=params(4),
-        cost_estimate=cost(320 * depth, 640 * depth),
+        cost_estimate=scaled(cost(320 * depth, 640 * depth), 1),
         name="edges_first",
     )(
         *near_core(
@@ -880,7 +886,7 @@
         out_shape=[held(rows, depth), held(SUB, LANES)],
         scratch_shapes=[pltpu.VMEM((rows, depth), F32)],
         compiler_params=params(16),
-        cost_estimate=mortar_cost,
+        cost_estimate=scaled(mortar_cost, 100),
         name="jump_second",
     )(
         *near_core(
@@ -893,20 +899,20 @@
         out_specs=[VMEM],
         out_shape=[held(rows + SUB, depth)],
         compiler_params=params(16),
-        cost_estimate=mortar_cost,
+        cost_estimate=scaled(mortar_cost, 20),
         name="back_second",
     )(*near_core(w_last, missing, puts, codes, proj_n))
 
     (back_next,) = pl.pallas_call(
         hold_kernel,
-        in_specs=[VMEM] * 2,
+        in_specs=[VMEM] * 3,
         out_specs=[VMEM],
         out_shape=[held(rows + SUB, depth)],
-        input_output_aliases={1: 0},
+        input_output_aliases={2: 0},
         compiler_params=params(2),
-        cost_estimate=cost(0, 8 * depth),
+        cost_estimate=scaled(cost(0, 8 * depth), 20),
         name="hold",
-    )(*near_core(second_sums, back_next))
+    )(*near_core(second_sums, recv, back_next))
     recv_next = shifted(back_next, "sub", 1)
 
     count = subs * blks
@@ -920,7 +926,7 @@
         input_output_aliases={17: 0},
         scratch_shapes=[pltpu.VMEM((6, SUB, LANES), F32)],
         compiler_params=params(8),
-        cost_estimate=cost(20 * cells, 15 * cells),
+        cost_estimate=scaled(cost(20 * cells, 15 * cells), 0.3),
         name="stencil_second_added",
     )(
         *near_core(
@@ -934,7 +940,7 @@
         out_specs=[VMEM],
         out_shape=[held(rows, depth)],
         compiler_params=params(16),
-        cost_estimate=mortar_cost,
+        cost_estimate=scaled(mortar_cost, 0.3),
         name="own_second",
     )(*near_core(s_first, recv, squares))
     tables = gather_rows(table, own_next)
@@ -946,7 +952,7 @@
         out_shape=[jax.ShapeDtypeStruct((layers, rows, depth), F32)] * 2,
         scratch_shapes=[pltpu.VMEM((layers, rows, depth), F32)] * 2 + [pltpu.SemaphoreType.DMA((2, steps))],
         compiler_params=params(8),
-        cost_estimate=cost(8 * cells, 22 * cells),
+        cost_estimate=scaled(cost(8 * cells, 22 * cells), 0),
         name="final_update",
     )(*near_core(tables, b, s_first, s_mid, w_last, recv, image_low, image_high, image_ends, edge_high, jump_next, recv_next, own_next))
 

time: 65.6 us -> 67.1 us (1.023)
  waiting for transfers between devices: 13.2 us -> 16.1 us
  starting transfers between devices: 26.3 us -> 25 us
    ppermute x5, starting transfers between devices: 13.7 us -> 10.5 us  [gather_rows(): other = lax.ppermute(table, ('sub', 'blk'), pairs)]
    ppermute x6, waiting for transfers between devices: 7.94 us -> 10.5 us  [shifted(): lax.ppermute(array, axis, [(i, i + by) for i in range(size) if 0 <= i + b...]
    ppermute x6, starting transfers between devices: 12.6 us -> 14.5 us  [shifted(): lax.ppermute(array, axis, [(i, i + by) for i in range(size) if 0 <= i + b...]
  transfers between devices with their start and end apart: 11 -> 11, of which waited for: 6 -> 6; matrix products, arithmetic and copies ran while one was open for 0% -> 0% of each run, Pallas kernels for 32% -> 31%
where the time goes in v7:
time: 67.1 us; the launch traced here: 66.8 us
  starting transfers between devices  25 us (37%)
  Pallas kernels  24.2 us (36%)
  waiting for transfers between devices  16.1 us (24%)
  between operations  1.49 us (2%)
    ppermute x6, starting transfers between devices, shifted(): lax.ppermute(array, axis, [(i, i + by) for i in range(size) if 0 <= i + b...  14.5 us
    ppermute x6, waiting for transfers between devices, shifted(): lax.ppermute(array, axis, [(i, i + by) for i in range(size) if 0 <= i + b...  10.5 us
    ppermute x5, starting transfers between devices, gather_rows(): other = lax.ppermute(table, ('sub', 'blk'), pairs)  10.5 us
    pallas_call x1, Pallas kernels, body(): pl.pallas_call(first_kernel, in_specs=[SMEM] + [VMEM] * 3 + [HBM] * 5, ou...  5.76 us
    ppermute x5, waiting for transfers between devices, gather_rows(): other = lax.ppermute(table, ('sub', 'blk'), pairs)  5.57 us
    pallas_call x1, Pallas kernels, body(): pl.pallas_call(second_high_kernel, in_specs=[VMEM] * 11, out_specs=[VMEM]...  3.14 us
    pallas_call x1, Pallas kernels, body(): pl.pallas_call(final_kernel, in_specs=[VMEM] * 13, out_specs=[HBM] * 2, o...  2.46 us
    pallas_call x1, Pallas kernels, body(): pl.pallas_call(second_added_kernel, in_specs=[VMEM] * 18, out_specs=[VMEM...  2.13 us
  transfers between devices with their start and end apart: 11, of which 6 were waited for; matrix products, arithmetic and copies ran while one was open for 0% of the time, Pallas kernels for 31%

profile of v7, /device:TPU:0, one launch (start us, length us, event | category | flops | bytes accessed | tf_op | source)
XLA Modules:
  0.0 66.8 jit_solution(13733898061686842433)
XLA Ops:
  0.6 0.0 copy-start.1
  0.6 0.0 copy-start.2
  0.7 0.0 copy-start
  0.7 1.1 %pack.1 = f32[264,512]{1,0:T(8,128)S(1)} custom-call(f32[4,256,512]{2,1,0:T(8,128)} %b_hbm.3, f32[4,256,512]{2,1,0:T(8,128)} %ty_hbm.3), custom_call_target="tpu_custom_call" | custom-call | flops 1 | bytes 52428800 | tf_op jit(solution)/shard_map/pack/pallas_call | solution.py:770
  1.8 1.3 %collective-permute-start = (f32[264,512]{1,0:T(8,128)S(1)}, f32[264,512]{1,0:T(8,128)S(1)}, u32[]{:S(2)}, u32[]{:S(2)}) collective-permute-start(f32[264,512]{1,0:T(8,128)S(1)} %pack.1), channel_id=1, source_target_pairs={{4,0},{8,4},{12,8},{16,12},{20,16},{24,20},{28,24},{5,1},{9,5},{13... | collective-permute-start | bytes 1622024 | tf_op jit(solution)/shard_map/ppermute | solution.py:731
  3.7 0.0 copy-done.1
  3.7 0.0 copy-done.2
  3.7 0.0 copy-done
  3.8 5.8 %stencil_first.1 = (f32[4,256,512]{2,1,0:T(8,128)S(1)}, f32[4,256,512]{2,1,0:T(8,128)S(1)}, f32[4,256,512]{2,1,0:T(8,128)S(1)}, f32[4,256,512]{2,1,0:T(8,128)S(1...) custom-call(s32[1,1]{1,0:T(1,128)S(6)} %copy.25.count, ...), custom_call_target="tpu_custom_call" | custom-call | flops 41943040 | bytes 50331648 | tf_op jit(solution)/shard_map/stencil_first/pallas_call | solution.py:782
  9.5 1.3 %collective-permute-start.4 = (f32[256,512]{1,0:T(8,128)S(1)}, f32[256,512]{1,0:T(8,128)S(1)}, u32[]{:S(2)}, u32[]{:S(2)}) collective-permute-start(f32[256,512]{1,0:T(8,128)S(1)} %get-tuple-element.70), channel_id=1, source_target_pairs={{4,0},{8,4},{12,8},{16,12},{20,16},{24,20},{28,24},{5,1},{9,5},{13... | collective-permute-start | bytes 1572872 | tf_op jit(solution)/shard_map/ppermute | solution.py:731
  10.8 1.9 %stencil_second_low.1.earlier.image_low_in = f32[2,256,512]{2,1,0:T(8,128)S(1)} custom-call(f32[256,512]{1,0:T(8,128)S(1)} %get-tuple-element.44.s_first.s_first_in, f32[2,256,512]{2,1,0:T(8,128)S(1)} %get-tuple-element.45.s_mid.s_mid_in, f32[4,256,512]{2,1,0:T(8,128)S(1)} %get-tuple-element.46.tx, f32[4,256,512]{2,1,0:T(8,128)S(1)} %get-tuple-element.47.ty, ...), custom_call_target="tpu_custom_call" | custom-call | flops 209715200 | bytes 157286400 | tf_op jit(solution)/shard_map/stencil_second_low/pallas_call | solution.py:803
  12.7 0.5 kinds.1
  13.2 6.5 %collective-permute-done.right.right_before = f32[264,512]{1,0:T(8,128)S(1)} collective-permute-done((f32[264,512]{1,0:T(8,128)S(1)}, f32[264,512]{1,0:T(8,128)S(1)}, u32[]{:S(2)}, u32[]{:S(2)}) %collective-permute-start) | collective-permute-done | bytes 540704 | tf_op jit(solution)/shard_map/ppermute | solution.py:731
  19.7 1.7 %jump_first.1 = (f32[256,512]{1,0:T(8,128)S(1)}, f32[256,512]{1,0:T(8,128)S(1)}, f32[8,128]{1,0:T(8,128)S(1)}) custom-call(f32[2,256,512]{2,1,0:T(8,128)S(1)} %stencil_second_low.1.earlier.image_low_in, f32[4,256,512]{2,1,0:T(8,128)S(1)} %get-tuple-element.50.b, f32[264,512]{1,0:T(8,128)S(1)} %collective-permute-done.right.right_before, ...), custom_call_target="tpu_custom_call" | custom-call | flops 281857216 | bytes 550503 | tf_op jit(solution)/shard_map/jump_first/pallas_call | solution.py:814
  21.5 1.3 %back_first.1.later.back.back_before = f32[264,512]{1,0:T(8,128)S(1)} custom-call(f32[256,512]{1,0:T(8,128)S(1)} %get-tuple-element.55.jump, f32[8,512]{1,0:T(8,128)S(1)} %get-tuple-element.58.kinds_by_block, bf16[1024,1024]{1,0:T(8,128)(2,1)S(1)} %get-tuple-element.59.puts, s32[1024,128]{1,0:T(8,128)S(1)} %get-tuple-element.53.codes, ...), custom_call_target="tpu_custom_call" | custom-call | flops 18790481920 | bytes 36700160 | tf_op jit(solution)/shard_map/back_first/pallas_call | solution.py:832
  22.7 1.3 %collective-permute-start.1 = (f32[15,512]{1,0:T(8,128)S(1)}, f32[15,512]{1,0:T(8,128)S(1)}, u32[]{:S(2)}, u32[]{:S(2)}) collective-permute-start(f32[15,512]{1,0:T(8,128)S(1)} %get-tuple-element.63), channel_id=1, source_target_pairs={{0,1},{1,2},{2,3},{4,5},{5,6},{6,7},{8,9},{9,10},{10,11},{12,13},{... | collective-permute-start | bytes 92168 | tf_op jit(solution)/shard_map/ppermute | solution.py:731
  24.0 1.3 %collective-permute-start.2 = (f32[10,512]{1,0:T(8,128)S(1)}, f32[10,512]{1,0:T(8,128)S(1)}, u32[]{:S(2)}, u32[]{:S(2)}) collective-permute-start(f32[10,512]{1,0:T(8,128)S(1)} %get-tuple-element.64), channel_id=1, source_target_pairs={{1,0},{2,1},{3,2},{5,4},{6,5},{7,6},{9,8},{10,9},{11,10},{13,12},{... | collective-permute-start | bytes 61448 | tf_op jit(solution)/shard_map/ppermute | solution.py:731
  25.3 4.9 %collective-permute-start.3 = (f32[264,512]{1,0:T(8,128)S(1)}, f32[264,512]{1,0:T(8,128)S(1)}, u32[]{:S(2)}, u32[]{:S(2)}) collective-permute-start(f32[264,512]{1,0:T(8,128)S(1)} %back_first.1.later.back.back_before), channel_id=1, source_target_pairs={{0,4},{4,8},{8,12},{12,16},{16,20},{20,24},{24,28},{1,5},{5,9},{9,... | collective-permute-start | bytes 1622024 | tf_op jit(solution)/shard_map/ppermute | solution.py:731
  30.2 3.1 %stencil_second_high.1 = (f32[2,256,512]{2,1,0:T(8,128)S(1)}, f32[8,128]{1,0:T(8,128)S(1)}) custom-call(f32[264,512]{1,0:T(8,128)S(1)} %back_first.1.later.back.back_before, f32[8,128]{1,0:T(8,128)S(1)} %get-tuple-element.43.first_sums.sums_in, f32[8,128]{1,0:T(8,128)S(1)} %get-tuple-element.60.jump_sums, f32[4,256,512]{2,1,0:T(8,128)S(1)} %get-tuple-element.50.b, ...), custom_call_target="tpu_custom_call" | custom-call | flops 10485761 | bytes 7864321 | tf_op jit(solution)/shard_map/stencil_second_high/pallas_call | solution.py:844
  33.4 0.0 collective-permute-done.2.down
  33.4 0.0 collective-permute-done.1.up
  33.4 0.3 edges_first.1
  33.8 0.0 collective-permute-done.4.right
  33.8 1.8 %jump_second.1 = (f32[256,512]{1,0:T(8,128)S(1)}, f32[8,128]{1,0:T(8,128)S(1)}) custom-call(f32[8,128]{1,0:T(8,128)S(1)} %get-tuple-element.62.near_sums.high_sums, f32[256,512]{1,0:T(8,128)S(1)} %get-tuple-element.69.w_last, f32[256,512]{1,0:T(8,128)S(1)} %get-tuple-element.55.jump, f32[264,512]{1,0:T(8,128)S(1)} %collective-permute-done.right.right_before, ...), custom_call_target="tpu_custom_call" | custom-call | flops 93952409600 | bytes 183500800 | tf_op jit(solution)/shard_map/jump_second/pallas_call | solution.py:882
  35.6 1.3 %back_second.1.back_in = f32[264,512]{1,0:T(8,128)S(1)} custom-call(f32[256,512]{1,0:T(8,128)S(1)} %get-tuple-element.69.w_last, f32[2,512]{1,0:T(2,128)S(1)} %get-tuple-element.72.missing, bf16[1024,1024]{1,0:T(8,128)(2,1)S(1)} %get-tuple-element.59.puts, s32[1024,128]{1,0:T(8,128)S(1)} %get-tuple-element.53.codes, ...), custom_call_target="tpu_custom_call" | custom-call | flops 18790481920 | bytes 36700160 | tf_op jit(solution)/shard_map/back_second/pallas_call | solution.py:896
  36.9 4.0 %collective-permute-done.3.recv.much_later = f32[264,512]{1,0:T(8,128)S(1)} collective-permute-done((f32[264,512]{1,0:T(8,128)S(1)}, f32[264,512]{1,0:T(8,128)S(1)}, u32[]{:S(2)}, u32[]{:S(2)}) %collective-permute-start.3) | collective-permute-done | bytes 540704 | tf_op jit(solution)/shard_map/ppermute | solution.py:731
  40.9 4.4 %collective-permute-start.10 = (f32[264,512]{1,0:T(8,128)S(1)}, f32[264,512]{1,0:T(8,128)S(1)}, u32[]{:S(2)}, u32[]{:S(2)}) collective-permute-start(f32[264,512]{1,0:T(8,128)S(1)} %hold.1), channel_id=1, source_target_pairs={{0,4},{4,8},{8,12},{12,16},{16,20},{20,24},{24,28},{1,5},{5,9},{9,... | collective-permute-start | bytes 1622024 | tf_op jit(solution)/shard_map/ppermute | solution.py:731
  45.3 2.1 %stencil_second_added.1 = (f32[2,256,512]{2,1,0:T(8,128)S(1)}, f32[4,512]{1,0:T(4,128)S(1)}, f32[4,128]{1,0:T(4,128)S(1)}) custom-call(f32[8,128]{1,0:T(8,128)S(1)} %get-tuple-element.67.first_sums, f32[8,128]{1,0:T(8,128)S(1)} %get-tuple-element.60.jump_sums, f32[8,128]{1,0:T(8,128)S(1)} %get-tuple-element.62.near_sums.high_sums, ...), custom_call_target="tpu_custom_call", output_to_operand_aliasing={{0}: (17, {})} | custom-call | flops 3145729 | bytes 2359297 | tf_op jit(solution)/shard_map/stencil_second_added/pallas_call | solution.py:919
  47.4 1.6 %collective-permute-start.5 = (f32[4,128]{1,0:T(4,128)S(1)}, f32[4,128]{1,0:T(4,128)S(1)}, u32[]{:S(2)}, u32[]{:S(2)}) collective-permute-start(f32[4,128]{1,0:T(4,128)S(1)} %get-tuple-element.78.one), channel_id=1, source_target_pairs={{0,1},{1,0},{2,3},{3,2},{4,5},{5,4},{6,7},{7,6},{8,9},{9,8},{10,11... | collective-permute-start | bytes 6152 | tf_op jit(solution)/shard_map/ppermute | solution.py:747
  49.0 0.8 %own_second.1.earlier.own_next = f32[256,512]{1,0:T(8,128)S(1)} custom-call(f32[256,512]{1,0:T(8,128)S(1)} %get-tuple-element.65.s_first, f32[264,512]{1,0:T(8,128)S(1)} %collective-permute-done.3.recv.much_later, bf16[512,256]{1,0:T(8,128)(2,1)S(1)} %get-tuple-element.66.squares), custom_call_target="tpu_custom_call" | custom-call | flops 281857216 | bytes 550503 | tf_op jit(solution)/shard_map/own_second/pallas_call | solution.py:937
  49.8 0.0 collective-permute-done.5.other
  49.8 2.9 %collective-permute-start.6 = (f32[4,128]{1,0:T(4,128)S(1)}, f32[4,128]{1,0:T(4,128)S(1)}, u32[]{:S(2)}, u32[]{:S(2)}) collective-permute-start(f32[4,128]{1,0:T(4,128)S(1)} %add.17), channel_id=1, source_target_pairs={{0,3},{1,2},{2,1},{3,0},{4,7},{5,6},{6,5},{7,4},{8,11},{9,10},{10,... | collective-permute-start | bytes 6152 | tf_op jit(solution)/shard_map/ppermute | solution.py:747
  52.8 1.3 %collective-permute-done.6 = f32[4,128]{1,0:T(4,128)S(1)} collective-permute-done((f32[4,128]{1,0:T(4,128)S(1)}, f32[4,128]{1,0:T(4,128)S(1)}, u32[]{:S(2)}, u32[]{:S(2)}) %collective-permute-start.6) | collective-permute-done | bytes 2080 | tf_op jit(solution)/shard_map/ppermute | solution.py:747
  54.1 2.7 %collective-permute-start.7 = (f32[4,128]{1,0:T(4,128)S(1)}, f32[4,128]{1,0:T(4,128)S(1)}, u32[]{:S(2)}, u32[]{:S(2)}) collective-permute-start(f32[4,128]{1,0:T(4,128)S(1)} %add.13), channel_id=1, source_target_pairs={{0,17},{1,16},{2,19},{3,18},{4,21},{5,20},{6,23},{7,22},{8,25},{9,... | collective-permute-start | bytes 6152 | tf_op jit(solution)/shard_map/ppermute | solution.py:747
  56.8 1.3 %collective-permute-done.7 = f32[4,128]{1,0:T(4,128)S(1)} collective-permute-done((f32[4,128]{1,0:T(4,128)S(1)}, f32[4,128]{1,0:T(4,128)S(1)}, u32[]{:S(2)}, u32[]{:S(2)}) %collective-permute-start.7) | collective-permute-done | bytes 2080 | tf_op jit(solution)/shard_map/ppermute | solution.py:747
  58.1 1.9 %collective-permute-start.8 = (f32[4,128]{1,0:T(4,128)S(1)}, f32[4,128]{1,0:T(4,128)S(1)}, u32[]{:S(2)}, u32[]{:S(2)}) collective-permute-start(f32[4,128]{1,0:T(4,128)S(1)} %add.14), channel_id=1, source_target_pairs={{0,9},{1,8},{2,11},{3,10},{4,13},{5,12},{6,15},{7,14},{8,1},{9,0},... | collective-permute-start | bytes 6152 | tf_op jit(solution)/shard_map/ppermute | solution.py:747
  60.0 1.3 %collective-permute-done.8 = f32[4,128]{1,0:T(4,128)S(1)} collective-permute-done((f32[4,128]{1,0:T(4,128)S(1)}, f32[4,128]{1,0:T(4,128)S(1)}, u32[]{:S(2)}, u32[]{:S(2)}) %collective-permute-start.8) | collective-permute-done | bytes 2080 | tf_op jit(solution)/shard_map/ppermute | solution.py:747
  61.3 1.4 %collective-permute-start.9 = (f32[4,128]{1,0:T(4,128)S(1)}, f32[4,128]{1,0:T(4,128)S(1)}, u32[]{:S(2)}, u32[]{:S(2)}) collective-permute-start(f32[4,128]{1,0:T(4,128)S(1)} %add.15), channel_id=1, source_target_pairs={{0,5},{1,4},{2,7},{3,6},{4,1},{5,0},{6,3},{7,2},{8,13},{9,12},{10,... | collective-permute-start | bytes 6152 | tf_op jit(solution)/shard_map/ppermute | solution.py:747
  62.7 1.6 %collective-permute-done.9 = f32[4,128]{1,0:T(4,128)S(1)} collective-permute-done((f32[4,128]{1,0:T(4,128)S(1)}, f32[4,128]{1,0:T(4,128)S(1)}, u32[]{:S(2)}, u32[]{:S(2)}) %collective-permute-start.9) | collective-permute-done | bytes 2080 | tf_op jit(solution)/shard_map/ppermute | solution.py:747
  64.3 0.0 collective-permute-done.10.recv_next
  64.3 2.5 %final_update.1 = (f32[4,256,512]{2,1,0:T(8,128)}, f32[4,256,512]{2,1,0:T(8,128)}) custom-call(f32[4,128]{1,0:T(4,128)S(1)} %add.16.tables, f32[4,256,512]{2,1,0:T(8,128)S(1)} %get-tuple-element.50.b, f32[256,512]{1,0:T(8,128)S(1)} %get-tuple-element.65.s_first, f32[2,256,512]{2,1,0:T(8,128)S(1)} %get-tuple-element.74.s_mid, ...), custom_call_target="tpu_custom_call" | custom-call | flops 1 | bytes 1 | tf_op jit(solution)/shard_map/final_update/pallas_call | solution.py:948
  (7 shorter events, 0.0 us)
Async XLA Ops:
  0.6 3.1 %copy-start.1 = (s32[1,1,1024]{2,1,0:T(1,128)S(1)}, s32[1,1,1024]{2,1,0:T(1,128)}, u32[]{:S(2)}) copy-start(s32[1,1,1024]{2,1,0:T(1,128)} %perm.1) | copy-start | bytes 12292
  0.6 3.1 %copy-start.2 = (s32[1,1,1024]{2,1,0:T(1,128)S(1)}, s32[1,1,1024]{2,1,0:T(1,128)}, u32[]{:S(2)}) copy-start(s32[1,1,1024]{2,1,0:T(1,128)} %kind.1) | copy-start | bytes 12292
  0.7 3.1 %copy-start = (f32[4,128,128]{2,1,0:T(8,128)S(1)}, f32[4,128,128]{2,1,0:T(8,128)}, u32[]{:S(2)}) copy-start(f32[4,128,128]{2,1,0:T(8,128)} %proj.1) | copy-start | bytes 786436
  1.8 17.9 %collective-permute-start = (f32[264,512]{1,0:T(8,128)S(1)}, f32[264,512]{1,0:T(8,128)S(1)}, u32[]{:S(2)}, u32[]{:S(2)}) collective-permute-start(f32[264,512]{1,0:T(8,128)S(1)} %pack.1), channel_id=1, source_target_pairs={{4,0},{8,4},{12,8},{16,12},{20,16},{24,20},{28,24},{5,1},{9,5},{13... | collective-permute-start | bytes 1622024 | tf_op jit(solution)/shard_map/ppermute | solution.py:731
  9.5 24.2 %collective-permute-start.4 = (f32[256,512]{1,0:T(8,128)S(1)}, f32[256,512]{1,0:T(8,128)S(1)}, u32[]{:S(2)}, u32[]{:S(2)}) collective-permute-start(f32[256,512]{1,0:T(8,128)S(1)} %get-tuple-element.70), channel_id=1, source_target_pairs={{4,0},{8,4},{12,8},{16,12},{20,16},{24,20},{28,24},{5,1},{9,5},{13... | collective-permute-start | bytes 1572872 | tf_op jit(solution)/shard_map/ppermute | solution.py:731
  22.7 10.7 %collective-permute-start.1 = (f32[15,512]{1,0:T(8,128)S(1)}, f32[15,512]{1,0:T(8,128)S(1)}, u32[]{:S(2)}, u32[]{:S(2)}) collective-permute-start(f32[15,512]{1,0:T(8,128)S(1)} %get-tuple-element.63), channel_id=1, source_target_pairs={{0,1},{1,2},{2,3},{4,5},{5,6},{6,7},{8,9},{9,10},{10,11},{12,13},{... | collective-permute-start | bytes 92168 | tf_op jit(solution)/shard_map/ppermute | solution.py:731
  24.0 9.3 %collective-permute-start.2 = (f32[10,512]{1,0:T(8,128)S(1)}, f32[10,512]{1,0:T(8,128)S(1)}, u32[]{:S(2)}, u32[]{:S(2)}) collective-permute-start(f32[10,512]{1,0:T(8,128)S(1)} %get-tuple-element.64), channel_id=1, source_target_pairs={{1,0},{2,1},{3,2},{5,4},{6,5},{7,6},{9,8},{10,9},{11,10},{13,12},{... | collective-permute-start | bytes 61448 | tf_op jit(solution)/shard_map/ppermute | solution.py:731
  25.3 15.5 %collective-permute-start.3 = (f32[264,512]{1,0:T(8,128)S(1)}, f32[264,512]{1,0:T(8,128)S(1)}, u32[]{:S(2)}, u32[]{:S(2)}) collective-permute-start(f32[264,512]{1,0:T(8,128)S(1)} %back_first.1.later.back.back_before), channel_id=1, source_target_pairs={{0,4},{4,8},{8,12},{12,16},{16,20},{20,24},{24,28},{1,5},{5,9},{9,... | collective-permute-start | bytes 1622024 | tf_op jit(solution)/shard_map/ppermute | solution.py:731
  40.9 23.4 %collective-permute-start.10 = (f32[264,512]{1,0:T(8,128)S(1)}, f32[264,512]{1,0:T(8,128)S(1)}, u32[]{:S(2)}, u32[]{:S(2)}) collective-permute-start(f32[264,512]{1,0:T(8,128)S(1)} %hold.1), channel_id=1, source_target_pairs={{0,4},{4,8},{8,12},{12,16},{16,20},{20,24},{24,28},{1,5},{5,9},{9,... | collective-permute-start | bytes 1622024 | tf_op jit(solution)/shard_map/ppermute | solution.py:731
  47.4 2.4 %collective-permute-start.5 = (f32[4,128]{1,0:T(4,128)S(1)}, f32[4,128]{1,0:T(4,128)S(1)}, u32[]{:S(2)}, u32[]{:S(2)}) collective-permute-start(f32[4,128]{1,0:T(4,128)S(1)} %get-tuple-element.78.one), channel_id=1, source_target_pairs={{0,1},{1,0},{2,3},{3,2},{4,5},{5,4},{6,7},{7,6},{8,9},{9,8},{10,11... | collective-permute-start | bytes 6152 | tf_op jit(solution)/shard_map/ppermute | solution.py:747
  49.8 4.2 %collective-permute-start.6 = (f32[4,128]{1,0:T(4,128)S(1)}, f32[4,128]{1,0:T(4,128)S(1)}, u32[]{:S(2)}, u32[]{:S(2)}) collective-permute-start(f32[4,128]{1,0:T(4,128)S(1)} %add.17), channel_id=1, source_target_pairs={{0,3},{1,2},{2,1},{3,0},{4,7},{5,6},{6,5},{7,4},{8,11},{9,10},{10,... | collective-permute-start | bytes 6152 | tf_op jit(solution)/shard_map/ppermute | solution.py:747
  54.1 4.0 %collective-permute-start.7 = (f32[4,128]{1,0:T(4,128)S(1)}, f32[4,128]{1,0:T(4,128)S(1)}, u32[]{:S(2)}, u32[]{:S(2)}) collective-permute-start(f32[4,128]{1,0:T(4,128)S(1)} %add.13), channel_id=1, source_target_pairs={{0,17},{1,16},{2,19},{3,18},{4,21},{5,20},{6,23},{7,22},{8,25},{9,... | collective-permute-start | bytes 6152 | tf_op jit(solution)/shard_map/ppermute | solution.py:747
  58.1 3.2 %collective-permute-start.8 = (f32[4,128]{1,0:T(4,128)S(1)}, f32[4,128]{1,0:T(4,128)S(1)}, u32[]{:S(2)}, u32[]{:S(2)}) collective-permute-start(f32[4,128]{1,0:T(4,128)S(1)} %add.14), channel_id=1, source_target_pairs={{0,9},{1,8},{2,11},{3,10},{4,13},{5,12},{6,15},{7,14},{8,1},{9,0},... | collective-permute-start | bytes 6152 | tf_op jit(solution)/shard_map/ppermute | solution.py:747
  61.3 3.0 %collective-permute-start.9 = (f32[4,128]{1,0:T(4,128)S(1)}, f32[4,128]{1,0:T(4,128)S(1)}, u32[]{:S(2)}, u32[]{:S(2)}) collective-permute-start(f32[4,128]{1,0:T(4,128)S(1)} %add.15), channel_id=1, source_target_pairs={{0,5},{1,4},{2,7},{3,6},{4,1},{5,0},{6,3},{7,2},{8,13},{9,12},{10,... | collective-permute-start | bytes 6152 | tf_op jit(solution)/shard_map/ppermute | solution.py:747
